TPU v7x, 512 devices: a whole 4x8x8 slice. The times are simulated.
512 devices in a mesh: row: 32 (over y, x), col: 16 (over z, core).
Axes of the slice: x: 4, y: 8, z: 8, core: 2. Of those that a mesh axis runs over, the one named last changes fastest.
Arguments:
- activations: bfloat16 [576, 8192], P('row', 'col'), may hold values from -6 to 6
- gate_matrix: bfloat16 [8192, 28672], P('col', 'row'), may hold values from -0.0625 to 0.0625
- up_matrix: bfloat16 [8192, 28672], P('col', 'row'), may hold values from -0.0625 to 0.0625
- down_matrix: bfloat16 [28672, 8192], P('row', 'col'), may hold values from -0.03125 to 0.03125
Outputs:
- layer_out: bfloat16 [576, 8192], P('row', 'col')
All inputs are finite; a program needn't handle non-finite values.
Results may differ from a plain program's by a relative error of at most 0.0049.
Values may be sent and summed in bfloat16 or wider, within the bound.
No kernel may reach another device: no remote copies, remote signals or barrier semaphores. Data moves between devices by JAX's collectives and lax.ppermute only.
A program may use at most 64 MiB of HBM per device.

v0:
```python
import jax
import jax.numpy as jnp
from jax import lax
from jax.sharding import PartitionSpec as P


def activate(summed, hidden_width):
    gate_part = summed[:, :hidden_width]
    up_part = summed[:, hidden_width:]
    return (jax.nn.silu(gate_part) * up_part).astype(jnp.bfloat16)


def shards(activations, gate_matrix, up_matrix, down_matrix):
    gathered = lax.all_gather(activations, "row", axis=0, tiled=True)
    hidden_width = gate_matrix.shape[1]
    gate_term = jnp.dot(gathered, gate_matrix, preferred_element_type=jnp.float32)
    up_term = jnp.dot(gathered, up_matrix, preferred_element_type=jnp.float32)
    summed = lax.psum(jnp.concatenate([gate_term, up_term], axis=1), "col")
    hidden = activate(summed, hidden_width)
    partial_out = jnp.dot(hidden, down_matrix, preferred_element_type=jnp.float32)
    result = lax.psum_scatter(partial_out, "row", scatter_dimension=0, tiled=True)
    return result.astype(jnp.bfloat16)


def solution(mesh):
    placed = (P("row", "col"), P("col", "row"), P("col", "row"), P("row", "col"))
    return jax.shard_map(
        shards, mesh=mesh, in_specs=placed, out_specs=P("row", "col"), check_vma=False
    )
```

profile of v0, /device:TPU:14, one launch (start us, length us, event | category | flops | bytes accessed | tf_op | source)
XLA Modules:
  0.0 315.8 jit_solution(8600206868353178816)
XLA Ops:
  6.5 50.4 %all-gather = bf16[32,18,512]{2,1,0:T(8,128)(2,1)S(1)} all-gather(bf16[1,18,512]{2,1,0:T(8,128)(2,1)} %bitcast.9), channel_id=1, replica_groups=mesh['row'=32,'col'=16] {'row'}, dimensions={0}, use_global_device_ids=true | all-gather | bytes 608256 | tf_op jit(solution)/shard_map/all_gather | solution.py:14
  57.0 0.2 reshape.1
  57.2 0.0 copy-start.1
  57.2 0.8 fusion.6
  58.0 0.4 copy-done.1
  58.4 0.8 fusion.7
  59.1 2.3 pad_maximum_fusion
  61.4 0.0 all-reduce.4.cloned.1.call-update
  61.4 129.4 %all-reduce.4.cloned.1.call-done = f32[576,1792]{1,0:T(8,128)} async-done(((f32[576,1792]{1,0:T(8,128)}), f32[576,1792]{1,0:T(8,128)}) %all-reduce.4.cloned.1.call-update) | async-done | bytes 4128784 | tf_op jit(solution)/shard_map/psum | solution.py:18
  190.8 3.0 fusion.2
  193.8 72.6 %fusion = f32[24,512]{1,0:T(8,128)S(1)} fusion(f32[576,512]{1,0:T(8,128)S(1)} %fusion.2), kind=kCustom, calls=%all-reduce-scatter | all-reduce-scatter fusion | flops 393217 | bytes 1230848
  266.4 4.2 %collective-permute-start = (bf16[24,512]{1,0:T(8,128)(2,1)S(1)}, bf16[24,512]{1,0:T(8,128)(2,1)S(1)}, u32[]{:S(2)}, u32[]{:S(2)}) collective-permute-start(bf16[24,512]{1,0:T(8,128)(2,1)S(1)} %convert.14), channel_id=1, source_target_pairs={{0,16},{16,32},{32,48},{48,64},{64,80},{80,96},{96,112},{112,128},... | collective-permute-start | bytes 73736
  270.6 5.0 %collective-permute-start.1 = (bf16[24,512]{1,0:T(8,128)(2,1)S(1)}, bf16[24,512]{1,0:T(8,128)(2,1)S(1)}, u32[]{:S(2)}, u32[]{:S(2)}) collective-permute-start(bf16[24,512]{1,0:T(8,128)(2,1)S(1)} %convert.14), channel_id=1, source_target_pairs={{0,32},{16,48},{32,64},{48,80},{64,96},{80,112},{96,128},{112,144}... | collective-permute-start | bytes 73736
  275.6 12.3 %collective-permute-start.7 = (bf16[18,512]{1,0:T(8,128)(2,1)S(1)}, bf16[18,512]{1,0:T(8,128)(2,1)S(1)}, u32[]{:S(2)}, u32[]{:S(2)}) collective-permute-start(bf16[18,512]{1,0:T(8,128)(2,1)S(1)} %slice.10), channel_id=1, source_target_pairs={{0,128},{16,144},{32,160},{48,176},{64,192},{80,208},{96,224},{112... | collective-permute-start | bytes 55304
  287.9 1.9 collective-permute-start.2
  289.8 3.1 collective-permute-start.3
  292.9 3.4 %collective-permute-start.4 = (bf16[24,512]{1,0:T(8,128)(2,1)S(1)}, bf16[24,512]{1,0:T(8,128)(2,1)S(1)}, u32[]{:S(2)}, u32[]{:S(2)}) collective-permute-start(bf16[24,512]{1,0:T(8,128)(2,1)S(1)} %convert.14), channel_id=1, source_target_pairs={{0,80},{16,96},{32,112},{48,128},{64,144},{80,160},{96,176},{112,1... | collective-permute-start | bytes 73736
  296.3 3.0 collective-permute-start.5
  299.4 1.9 collective-permute-start.6
  301.3 1.3 dynamic-slice.4
  303.3 1.2 collective-permute-done.5
  304.5 2.8 collective-permute-done.6
  307.2 1.1 concatenate.4
  308.3 0.6 dynamic-slice_convert_fusion
  (13 shorter events, 0.0 us)
Async XLA Ops:
  6.5 50.6 %copy-start = (bf16[512,896]{1,0:T(8,128)(2,1)S(1)}, bf16[512,896]{1,0:T(8,128)(2,1)}, u32[]{:S(2)}) copy-start(bf16[512,896]{1,0:T(8,128)(2,1)} %param.5) | copy-start | bytes 2752516
  6.5 184.2 %all-reduce.4.cloned.1.call-start = ((), (), s32[]{:S(2)}) async-start(), calls=%async_computation | async-start | bytes 8257536 | tf_op jit(solution)/shard_map/psum | solution.py:18
  57.2 1.2 copy-start.1
  61.4 129.4 %copy-start.2 = (bf16[896,512]{1,0:T(8,128)(2,1)S(1)}, bf16[896,512]{1,0:T(8,128)(2,1)}, u32[]{:S(2)}) copy-start(bf16[896,512]{1,0:T(8,128)(2,1)} %param.7) | copy-start | bytes 2752516
  266.4 29.9 %collective-permute-start = (bf16[24,512]{1,0:T(8,128)(2,1)S(1)}, bf16[24,512]{1,0:T(8,128)(2,1)S(1)}, u32[]{:S(2)}, u32[]{:S(2)}) collective-permute-start(bf16[24,512]{1,0:T(8,128)(2,1)S(1)} %convert.14), channel_id=1, source_target_pairs={{0,16},{16,32},{32,48},{48,64},{64,80},{80,96},{96,112},{112,128},... | collective-permute-start | bytes 73736
  270.6 28.8 %collective-permute-start.1 = (bf16[24,512]{1,0:T(8,128)(2,1)S(1)}, bf16[24,512]{1,0:T(8,128)(2,1)S(1)}, u32[]{:S(2)}, u32[]{:S(2)}) collective-permute-start(bf16[24,512]{1,0:T(8,128)(2,1)S(1)} %convert.14), channel_id=1, source_target_pairs={{0,32},{16,48},{32,64},{48,80},{64,96},{80,112},{96,128},{112,144}... | collective-permute-start | bytes 73736
  275.6 17.3 %collective-permute-start.7 = (bf16[18,512]{1,0:T(8,128)(2,1)S(1)}, bf16[18,512]{1,0:T(8,128)(2,1)S(1)}, u32[]{:S(2)}, u32[]{:S(2)}) collective-permute-start(bf16[18,512]{1,0:T(8,128)(2,1)S(1)} %slice.10), channel_id=1, source_target_pairs={{0,128},{16,144},{32,160},{48,176},{64,192},{80,208},{96,224},{112... | collective-permute-start | bytes 55304
  287.9 15.4 %collective-permute-start.2 = (bf16[24,512]{1,0:T(8,128)(2,1)S(1)}, bf16[24,512]{1,0:T(8,128)(2,1)S(1)}, u32[]{:S(2)}, u32[]{:S(2)}) collective-permute-start(bf16[24,512]{1,0:T(8,128)(2,1)S(1)} %convert.14), channel_id=1, source_target_pairs={{0,48},{16,64},{32,80},{48,96},{64,112},{80,128},{96,144},{112,160... | collective-permute-start | bytes 73736
  289.8 13.5 %collective-permute-start.3 = (bf16[24,512]{1,0:T(8,128)(2,1)S(1)}, bf16[24,512]{1,0:T(8,128)(2,1)S(1)}, u32[]{:S(2)}, u32[]{:S(2)}) collective-permute-start(bf16[24,512]{1,0:T(8,128)(2,1)S(1)} %convert.14), channel_id=1, source_target_pairs={{0,64},{16,80},{32,96},{48,112},{64,128},{80,144},{96,160},{112,17... | collective-permute-start | bytes 73736
  292.9 10.4 %collective-permute-start.4 = (bf16[24,512]{1,0:T(8,128)(2,1)S(1)}, bf16[24,512]{1,0:T(8,128)(2,1)S(1)}, u32[]{:S(2)}, u32[]{:S(2)}) collective-permute-start(bf16[24,512]{1,0:T(8,128)(2,1)S(1)} %convert.14), channel_id=1, source_target_pairs={{0,80},{16,96},{32,112},{48,128},{64,144},{80,160},{96,176},{112,1... | collective-permute-start | bytes 73736
  296.3 8.1 %collective-permute-start.5 = (bf16[24,512]{1,0:T(8,128)(2,1)S(1)}, bf16[24,512]{1,0:T(8,128)(2,1)S(1)}, u32[]{:S(2)}, u32[]{:S(2)}) collective-permute-start(bf16[24,512]{1,0:T(8,128)(2,1)S(1)} %convert.14), channel_id=1, source_target_pairs={{0,96},{16,112},{32,128},{48,144},{64,160},{80,176},{96,192},{112,... | collective-permute-start | bytes 73736
  299.4 7.8 %collective-permute-start.6 = (bf16[24,512]{1,0:T(8,128)(2,1)S(1)}, bf16[24,512]{1,0:T(8,128)(2,1)S(1)}, u32[]{:S(2)}, u32[]{:S(2)}) collective-permute-start(bf16[24,512]{1,0:T(8,128)(2,1)S(1)} %convert.14), channel_id=1, source_target_pairs={{0,112},{16,128},{32,144},{48,160},{64,176},{80,192},{96,208},{112... | collective-permute-start | bytes 73736
Sparse Core Ops, SparseCore 0:
  61.5 129.1 all-reduce.3
where the time goes:
time: 316 us
  waiting for transfers between devices  133 us (42%)
  blocking collectives  123 us (39%)
  starting transfers between devices  34.8 us (11%)
  between operations  14.2 us (4%)
  matrix products  4.54 us (1%)
  local copies, waits for them, and re-layouts  3.62 us (1%)
    psum x1, waiting for transfers between devices, shards(): summed = lax.psum(jnp.concatenate([gate_term, up_term], axis=1), 'col')  129 us
    unnamed x1, blocking collectives  72.6 us
    all_gather x1, blocking collectives, shards(): gathered = lax.all_gather(activations, 'row', axis=0, tiled=True)  50.4 us
    unnamed x8, starting transfers between devices  34.8 us
  transfers between devices with their start and end apart: 9, of which 3 were waited for; matrix products, arithmetic and copies ran while one was open for 0% of the time, Pallas kernels for 0%

commit v1 on v0

v1 whole, which is shorter than its diff:
```python
import functools

import jax
import jax.numpy as jnp
from jax import lax
from jax.experimental import pallas as pl
from jax.experimental.pallas import tpu as pltpu
from jax.sharding import PartitionSpec as P

LANES = 128
VMEM = pltpu.CompilerParams(vmem_limit_bytes=48 * 1024 * 1024)
SCALE = 16.0
DOWN, UP, KEPT = (-1, 4, 2), (1, -2), (0, -3, 3)
NEAR, BELOW, ABOVE = (0, 3, -3), (-1, 2, 4), (1, -2)


def along(axis_size, step):
    return [(i, (i + step) % axis_size) for i in range(axis_size)]


def swap(axis_size):
    return [(i, i ^ 1) for i in range(axis_size)]


def one_hot(rows, columns, tokens, column_tiles, flip):
    r = lax.broadcasted_iota(jnp.int32, (rows, columns), 0)
    c = lax.broadcasted_iota(jnp.int32, (rows, columns), 1)
    if flip:
        r, c = c, r
    return (c == (r % tokens) * column_tiles + r // tokens).astype(jnp.bfloat16)


def unpack_kernel(order, z_ref, own_ref, other_ref, out_ref):
    blocks = len(order)
    sources, rows = own_ref.shape[0] // blocks, own_ref.shape[1]
    tokens = out_ref.shape[1]
    tiles = sources * rows // tokens
    place = one_hot(tiles * tokens, sources * rows, tokens, tiles, False)
    width = tiles * LANES
    for j, offset in enumerate(order):
        block = lax.rem(z_ref[0] + offset + blocks, blocks)
        start = block * sources
        own = own_ref[pl.ds(start, sources)].reshape(sources * rows, LANES)
        other = other_ref[pl.ds(start, sources)].reshape(sources * rows, LANES)
        both = jnp.concatenate([own, other], axis=1)
        moved = jnp.dot(place, both, preferred_element_type=jnp.float32).astype(
            jnp.bfloat16
        )
        for q in range(tiles):
            part = moved[q * tokens : (q + 1) * tokens]
            out_ref[j, :, q * LANES : (q + 1) * LANES] = part[:, :LANES]
            out_ref[j, :, width + q * LANES : width + (q + 1) * LANES] = part[:, LANES:]


def unpack(order, z, own, other, tokens):
    width = own.shape[0] * own.shape[1] * LANES // (len(order) * tokens)
    return pl.pallas_call(
        functools.partial(unpack_kernel, order),
        out_shape=jax.ShapeDtypeStruct((len(order), tokens, 2 * width), jnp.bfloat16),
        in_specs=[
            pl.BlockSpec(memory_space=pltpu.SMEM),
            pl.BlockSpec(memory_space=pltpu.VMEM),
            pl.BlockSpec(memory_space=pltpu.VMEM),
        ],
        out_specs=pl.BlockSpec(memory_space=pltpu.VMEM),
        compiler_params=VMEM,
    )(z, own, other)


def activate_kernel(core_ref, total_ref, out_ref):
    tokens, width = total_ref.shape
    tiles = width // LANES // 2
    gate = total_ref[:, : tiles * LANES]
    mixed = total_ref[:, tiles * LANES : (tiles + 1) * LANES]
    up = total_ref[:, (tiles + 1) * LANES :]
    whole = (gate / (1 + jnp.exp(-gate)) * up).astype(jnp.bfloat16)
    for q in range(tiles):
        out_ref[:, q * LANES : (q + 1) * LANES] = whole[:, q * LANES : (q + 1) * LANES]
    half = mixed / (1 + jnp.exp(-mixed)) * pltpu.roll(mixed, LANES // 2, 1)
    lane = lax.broadcasted_iota(jnp.int32, (tokens, LANES), 1)
    mine = (lane // (LANES // 2)) == core_ref[0]
    out_ref[:, tiles * LANES :] = jnp.where(mine, half, 0.0).astype(jnp.bfloat16)


def activate(core, total):
    tokens, width = total.shape
    return pl.pallas_call(
        activate_kernel,
        out_shape=jax.ShapeDtypeStruct(
            (tokens, (width // LANES // 2 + 1) * LANES), jnp.bfloat16
        ),
        in_specs=[
            pl.BlockSpec(memory_space=pltpu.SMEM),
            pl.BlockSpec(memory_space=pltpu.VMEM),
        ],
        out_specs=pl.BlockSpec(memory_space=pltpu.VMEM),
        compiler_params=VMEM,
    )(core, total)


def down_kernel(groups, where_ref, *refs):
    n = len(groups)
    mine, theirs = refs[:n], refs[n : 2 * n]
    weight_ref, out_ref, hidden_ref = refs[2 * n :]
    blocks = sum(len(g) for g in groups)
    tokens = mine[0].shape[1]
    tiles = mine[0].shape[2] // LANES - 1
    sources, rows = out_ref.shape[0] // blocks, out_ref.shape[1]
    first = where_ref[1] == 0
    at = 0
    for a_ref, b_ref, group in zip(mine, theirs, groups):
        for j in range(len(group)):
            a, b = a_ref[j], b_ref[j]
            low, high = jnp.where(first, a, b), jnp.where(first, b, a)
            split = tiles * LANES
            hidden_ref[at, :, :split] = low[:, :split]
            hidden_ref[at, :, split : split + LANES] = low[:, split:] + high[:, split:]
            hidden_ref[at, :, split + LANES :] = high[:, :split]
            at += 1
    column_tiles = weight_ref.shape[1] // LANES
    place = one_hot(sources * rows, column_tiles * tokens, tokens, column_tiles, True)
    weight = weight_ref[...]
    at = 0
    for group in groups:
        for offset in group:
            result = jnp.dot(
                hidden_ref[at], weight, preferred_element_type=jnp.float32
            ).astype(jnp.bfloat16)
            stacked = jnp.concatenate(
                [result[:, q * LANES : (q + 1) * LANES] for q in range(column_tiles)],
                axis=0,
            )
            packed = jnp.dot(
                place, stacked, preferred_element_type=jnp.float32
            ).astype(jnp.bfloat16)
            block = lax.rem(where_ref[0] + offset + blocks, blocks)
            out_ref[pl.ds(block * sources, sources)] = packed.reshape(
                sources, rows, LANES
            )
            at += 1


def down(groups, where, mine, theirs, weight, sources, rows):
    blocks = sum(len(g) for g in groups)
    tokens = mine[0].shape[1]
    whole = pl.BlockSpec(memory_space=pltpu.VMEM)
    return pl.pallas_call(
        functools.partial(down_kernel, groups),
        out_shape=jax.ShapeDtypeStruct((sources * blocks, rows, LANES), jnp.bfloat16),
        in_specs=[pl.BlockSpec(memory_space=pltpu.SMEM)]
        + [whole] * (2 * len(groups) + 1),
        out_specs=whole,
        scratch_shapes=[pltpu.VMEM((blocks, tokens, weight.shape[0]), jnp.bfloat16)],
        compiler_params=VMEM,
    )(where, *mine, *theirs, weight)


def sum_kernel(shares_ref, out_ref):
    total = shares_ref[0].astype(jnp.float32)
    for r in range(1, shares_ref.shape[0]):
        total += shares_ref[r].astype(jnp.float32)
    out_ref[...] = total.astype(jnp.bfloat16)


def add_up(shares):
    return pl.pallas_call(
        sum_kernel,
        out_shape=jax.ShapeDtypeStruct(shares.shape[1:], jnp.bfloat16),
        in_specs=[pl.BlockSpec(memory_space=pltpu.VMEM)],
        out_specs=pl.BlockSpec(memory_space=pltpu.VMEM),
        compiler_params=VMEM,
    )(shares)


def split_columns(gate, up):
    width = gate.shape[1]
    half, tile = width // 2, width // 2 // LANES * LANES
    low = [gate[:, :half], up[:, tile:half], up[:, :tile]]
    high = [
        gate[:, width - tile :],
        up[:, half : width - tile],
        gate[:, half : width - tile],
        up[:, width - tile :],
    ]
    return jnp.concatenate(low, axis=1), jnp.concatenate(high, axis=1)


def shards(activations, gate_matrix, up_matrix, down_matrix):
    n_row, n_col = lax.axis_size("row"), lax.axis_size("col")
    depth = n_col // 2
    me = lax.axis_index("col")
    z, core = me // 2, me % 2
    own_tokens, width = activations.shape
    tokens = n_row * own_tokens // depth
    rows = own_tokens * width // LANES
    shift = lambda x, step: lax.ppermute(x, "col", along(n_col, 2 * step))
    other_core = lambda x: lax.ppermute(x, "col", swap(n_col))

    packed = activations.reshape(rows, LANES)
    spread = jnp.broadcast_to(packed[None], (n_row, rows, LANES))
    got = lax.all_to_all(spread, "row", 0, 0, tiled=True)

    low, high = split_columns(gate_matrix, up_matrix)
    kept = jnp.where(core == 0, low, high)
    weights = jnp.concatenate(
        [kept, other_core(jnp.where(core == 0, high, low))], axis=0
    )

    order = DOWN + UP + KEPT
    inputs = unpack(order, z.reshape(1), got, other_core(got), tokens)

    def partial(first, count):
        term = jnp.dot(
            inputs[first : first + count].reshape(count * tokens, 2 * width),
            weights,
            preferred_element_type=jnp.float32,
        )
        return (term * SCALE).reshape(count, tokens, weights.shape[1])

    narrow = lambda x: x.astype(jnp.float16)
    wide = lambda x: x.astype(jnp.float32)
    from_above = wide(shift(narrow(partial(0, 3)), -1))
    from_below = wide(shift(narrow(partial(3, 2)), 1))
    stay = partial(5, 3)
    to_below = shift(narrow(stay[1] + from_above[1] + from_below[1]), -3)
    to_above = shift(narrow(stay[2] + from_above[2]), 3)
    total = stay[0] + from_above[0] + from_below[0] + (wide(to_below) + wide(to_above))

    hidden = activate(core.reshape(1), total * (1 / SCALE))
    near = jnp.stack([hidden, shift(hidden, -3), shift(hidden, 3)])
    below = shift(near, 1)
    above = shift(jnp.stack([near[0], near[2]]), -1)
    mine = (near, below, above)
    theirs = tuple(other_core(x) for x in mine)
    share = down(
        (NEAR, BELOW, ABOVE),
        jnp.stack([z, core]),
        mine,
        theirs,
        down_matrix,
        n_row // depth,
        rows,
    )
    shares = lax.all_to_all(share, "row", 0, 0, tiled=True)
    return add_up(shares).reshape(own_tokens, width)


def solution(mesh):
    placed = (P("row", "col"), P("col", "row"), P("col", "row"), P("row", "col"))
    return jax.shard_map(
        shards, mesh=mesh, in_specs=placed, out_specs=P("row", "col"), check_vma=False
    )
```

time: 316 us -> 134 us (0.42)
  the two profiles are of different devices: /device:TPU:14 before, /device:TPU:1 now
where the time goes in v1:
time: 134 us
  starting transfers between devices  67.8 us (51%)
  waiting for transfers between devices  29.7 us (22%)
  blocking collectives  22.2 us (17%)
  local copies, waits for them, and re-layouts  5.67 us (4%)
  Pallas kernels  4.38 us (3%)
  other arithmetic  1.8 us (1%)
  matrix products  1.78 us (1%)
    ppermute x8, starting transfers between devices, shards(): shift = lambda x, step: lax.ppermute(x, 'col', along(n_col, 2 * step))  41.8 us
    all_to_all x1, blocking collectives, shards(): shares = lax.all_to_all(share, 'row', 0, 0, tiled=True)  22.2 us
    ppermute x8, waiting for transfers between devices, shards(): shift = lambda x, step: lax.ppermute(x, 'col', along(n_col, 2 * step))  16.1 us
    ppermute x5, starting transfers between devices, shards(): other_core = lambda x: lax.ppermute(x, 'col', swap(n_col))  15.4 us
    all_to_all x1, waiting for transfers between devices, shards(): got = lax.all_to_all(spread, 'row', 0, 0, tiled=True)  10.8 us
    all_to_all x1, starting transfers between devices, shards(): got = lax.all_to_all(spread, 'row', 0, 0, tiled=True)  10.5 us
    pallas_call x1, Pallas kernels, down(): pl.pallas_call(functools.partial(down_kernel, groups), out_shape=jax.Shap...  3.41 us
    ppermute x5, waiting for transfers between devices, shards(): other_core = lambda x: lax.ppermute(x, 'col', swap(n_col))  2.86 us
  transfers between devices with their start and end apart: 14, of which 7 were waited for; matrix products, arithmetic and copies ran while one was open for 2% of the time, Pallas kernels for 1%

profile of v1, /device:TPU:1, one launch (start us, length us, event | category | flops | bytes accessed | tf_op | source)
XLA Modules:
  0.0 133.6 jit_solution(8524003511741573028)
XLA Ops:
  1.7 10.5 %all-to-all-start = ((bf16[32,72,128]{2,1,0:T(8,128)(2,1)}), bf16[32,72,128]{2,1,0:T(8,128)(2,1)S(1)}, u32[]{:S(2)}, u32[]{:S(2)}) async-start(bf16[32,72,128]{2,1,0:T(8,128)(2,1)} %broadcast_in_dim.8), calls=%async_computation | async-start | bytes 1179648 | tf_op jit(solution)/shard_map/all_to_all | solution.py:201
  14.6 1.4 %broadcast_select_fusion.1 = (bf16[512,896]{1,0:T(8,128)(2,1)S(1)}, bf16[512,896]{1,0:T(8,128)(2,1)}) fusion(pred[]{:T(512)S(6)} %eq.6, bf16[512,384]{1,0:T(8,128)(2,1)S(1)} %get-tuple-element.14, bf16[512,64]{1,0:T(8,128)(2,1)S(1)} %get-tuple-element.12, bf16[512,448]{1,0:T(8,128)(2,1)S(1)} %slice-done.1, bf16[512,384]{1,0:T(8,128)(2,1)S(1)} %get-tuple-element.13, ...), kind=kLoop, calls=%fused_computation.9 | loop fusion | flops 7340032 | bytes 3670017 | tf_op jit(solution)/shard_map/jit(_where)/select_n | solution.py:204
  16.0 2.9 %collective-permute-start.1 = (bf16[512,896]{1,0:T(8,128)(2,1)}, bf16[512,896]{1,0:T(8,128)(2,1)S(1)}, u32[]{:S(2)}, u32[]{:S(2)}) collective-permute-start(bf16[512,896]{1,0:T(8,128)(2,1)} %get-tuple-element.6), channel_id=1, source_target_pairs={{0,1},{1,0},{2,3},{3,2},{4,5},{5,4},{6,7},{7,6},{8,9},{9,8},{10,11... | collective-permute-start | bytes 2752520 | tf_op jit(solution)/shard_map/ppermute | solution.py:197
  18.8 10.8 %all-to-all-done.own_ref = bf16[32,72,128]{2,1,0:T(8,128)(2,1)S(1)} async-done(((bf16[32,72,128]{2,1,0:T(8,128)(2,1)}), bf16[32,72,128]{2,1,0:T(8,128)(2,1)S(1)}, u32[]{:S(2)}, u32[]{:S(2)}) %all-to-all-start) | async-done | bytes 589856 | tf_op jit(solution)/shard_map/all_to_all | solution.py:201
  29.7 4.4 %collective-permute-start = (bf16[32,72,128]{2,1,0:T(8,128)(2,1)S(1)}, bf16[32,72,128]{2,1,0:T(8,128)(2,1)S(1)}, u32[]{:S(2)}, u32[]{:S(2)}) collective-permute-start(bf16[32,72,128]{2,1,0:T(8,128)(2,1)S(1)} %all-to-all-done.own_ref), channel_id=1, source_target_pairs={{0,1},{1,0},{2,3},{3,2},{4,5},{5,4},{6,7},{7,6},{8,9},{9,8},{10,11... | collective-permute-start | bytes 1769480 | tf_op jit(solution)/shard_map/ppermute | solution.py:197
  34.1 1.6 %collective-permute-done.other_ref = bf16[32,72,128]{2,1,0:T(8,128)(2,1)S(1)} collective-permute-done((bf16[32,72,128]{2,1,0:T(8,128)(2,1)S(1)}, bf16[32,72,128]{2,1,0:T(8,128)(2,1)S(1)}, u32[]{:S(2)}, u32[]{:S(2)}) %collective-permute-start) | collective-permute-done | bytes 589856 | tf_op jit(solution)/shard_map/ppermute | solution.py:197
  38.1 10.7 %collective-permute-start.2 = (f16[3,72,896]{2,1,0:T(8,128)(2,1)S(1)}, f16[3,72,896]{2,1,0:T(8,128)(2,1)S(1)}, u32[]{:S(2)}, u32[]{:S(2)}) collective-permute-start(f16[3,72,896]{2,1,0:T(8,128)(2,1)S(1)} %bitcast.53), channel_id=1, source_target_pairs={{0,14},{1,15},{2,0},{3,1},{4,2},{5,3},{6,4},{7,5},{8,6},{9,7},{10,... | collective-permute-start | bytes 1161224 | tf_op jit(solution)/shard_map/ppermute | solution.py:196
  49.3 1.9 %collective-permute-start.3 = (f16[2,72,896]{2,1,0:T(8,128)(2,1)S(1)}, f16[2,72,896]{2,1,0:T(8,128)(2,1)S(1)}, u32[]{:S(2)}, u32[]{:S(2)}) collective-permute-start(f16[2,72,896]{2,1,0:T(8,128)(2,1)S(1)} %bitcast.54), channel_id=1, source_target_pairs={{0,2},{1,3},{2,4},{3,5},{4,6},{5,7},{6,8},{7,9},{8,10},{9,11},{10,... | collective-permute-start | bytes 774152 | tf_op jit(solution)/shard_map/ppermute | solution.py:196
  51.9 7.6 %collective-permute-done.3 = f16[2,72,896]{2,1,0:T(8,128)(2,1)S(1)} collective-permute-done((f16[2,72,896]{2,1,0:T(8,128)(2,1)S(1)}, f16[2,72,896]{2,1,0:T(8,128)(2,1)S(1)}, u32[]{:S(2)}, u32[]{:S(2)}) %collective-permute-start.3) | collective-permute-done | bytes 258080 | tf_op jit(solution)/shard_map/ppermute | solution.py:196
  59.7 1.9 %collective-permute-start.4 = (f16[72,896]{1,0:T(8,128)(2,1)S(1)}, f16[72,896]{1,0:T(8,128)(2,1)S(1)}, u32[]{:S(2)}, u32[]{:S(2)}) collective-permute-start(f16[72,896]{1,0:T(8,128)(2,1)S(1)} %get-tuple-element.7), channel_id=1, source_target_pairs={{0,10},{1,11},{2,12},{3,13},{4,14},{5,15},{6,0},{7,1},{8,2},{9,3},... | collective-permute-start | bytes 387080 | tf_op jit(solution)/shard_map/ppermute | solution.py:196
  61.7 5.3 %collective-permute-start.5 = (f16[72,896]{1,0:T(8,128)(2,1)S(1)}, f16[72,896]{1,0:T(8,128)(2,1)S(1)}, u32[]{:S(2)}, u32[]{:S(2)}) collective-permute-start(f16[72,896]{1,0:T(8,128)(2,1)S(1)} %get-tuple-element.8), channel_id=1, source_target_pairs={{0,6},{1,7},{2,8},{3,9},{4,10},{5,11},{6,12},{7,13},{8,14},{9,15},... | collective-permute-start | bytes 387080 | tf_op jit(solution)/shard_map/ppermute | solution.py:196
  67.0 3.7 %collective-permute-done.4 = f16[72,896]{1,0:T(8,128)(2,1)S(1)} collective-permute-done((f16[72,896]{1,0:T(8,128)(2,1)S(1)}, f16[72,896]{1,0:T(8,128)(2,1)S(1)}, u32[]{:S(2)}, u32[]{:S(2)}) %collective-permute-start.4) | collective-permute-done | bytes 129056 | tf_op jit(solution)/shard_map/ppermute | solution.py:196
  70.7 1.5 %collective-permute-done.5 = f16[72,896]{1,0:T(8,128)(2,1)S(1)} collective-permute-done((f16[72,896]{1,0:T(8,128)(2,1)S(1)}, f16[72,896]{1,0:T(8,128)(2,1)S(1)}, u32[]{:S(2)}, u32[]{:S(2)}) %collective-permute-start.5) | collective-permute-done | bytes 129056 | tf_op jit(solution)/shard_map/ppermute | solution.py:196
  72.4 2.5 %collective-permute-start.7 = (bf16[72,512]{1,0:T(8,128)(2,1)S(1)}, bf16[72,512]{1,0:T(8,128)(2,1)S(1)}, u32[]{:S(2)}, u32[]{:S(2)}) collective-permute-start(bf16[72,512]{1,0:T(8,128)(2,1)S(1)} %shard_map.47), channel_id=1, source_target_pairs={{0,6},{1,7},{2,8},{3,9},{4,10},{5,11},{6,12},{7,13},{8,14},{9,15},... | collective-permute-start | bytes 221192 | tf_op jit(solution)/shard_map/ppermute | solution.py:196
  74.9 5.8 %collective-permute-start.6 = (bf16[72,512]{1,0:T(8,128)(2,1)S(1)}, bf16[72,512]{1,0:T(8,128)(2,1)S(1)}, u32[]{:S(2)}, u32[]{:S(2)}) collective-permute-start(bf16[72,512]{1,0:T(8,128)(2,1)S(1)} %shard_map.47), channel_id=1, source_target_pairs={{0,10},{1,11},{2,12},{3,13},{4,14},{5,15},{6,0},{7,1},{8,2},{9,3},... | collective-permute-start | bytes 221192 | tf_op jit(solution)/shard_map/ppermute | solution.py:196
  80.7 3.2 %collective-permute-done.6 = bf16[72,512]{1,0:T(8,128)(2,1)S(1)} collective-permute-done((bf16[72,512]{1,0:T(8,128)(2,1)S(1)}, bf16[72,512]{1,0:T(8,128)(2,1)S(1)}, u32[]{:S(2)}, u32[]{:S(2)}) %collective-permute-start.6) | collective-permute-done | bytes 73760 | tf_op jit(solution)/shard_map/ppermute | solution.py:196
  83.9 6.7 %collective-permute-start.8 = (bf16[3,72,512]{2,1,0:T(8,128)(2,1)S(1)}, bf16[3,72,512]{2,1,0:T(8,128)(2,1)S(1)}, u32[]{:S(2)}, u32[]{:S(2)}) collective-permute-start(bf16[3,72,512]{2,1,0:T(8,128)(2,1)S(1)} %pad_maximum_fusion.6.refs_0_), channel_id=1, source_target_pairs={{0,2},{1,3},{2,4},{3,5},{4,6},{5,7},{6,8},{7,9},{8,10},{9,11},{10,... | collective-permute-start | bytes 663560 | tf_op jit(solution)/shard_map/ppermute | solution.py:196
  90.7 7.0 %collective-permute-start.9 = (bf16[2,72,512]{2,1,0:T(8,128)(2,1)S(1)}, bf16[2,72,512]{2,1,0:T(8,128)(2,1)S(1)}, u32[]{:S(2)}, u32[]{:S(2)}) collective-permute-start(bf16[2,72,512]{2,1,0:T(8,128)(2,1)S(1)} %pad_maximum_fusion.7), channel_id=1, source_target_pairs={{0,14},{1,15},{2,0},{3,1},{4,2},{5,3},{6,4},{7,5},{8,6},{9,7},{10,... | collective-permute-start | bytes 442376 | tf_op jit(solution)/shard_map/ppermute | solution.py:196
  97.7 3.4 %collective-permute-start.10 = (bf16[3,72,512]{2,1,0:T(8,128)(2,1)S(1)}, bf16[3,72,512]{2,1,0:T(8,128)(2,1)S(1)}, u32[]{:S(2)}, u32[]{:S(2)}) collective-permute-start(bf16[3,72,512]{2,1,0:T(8,128)(2,1)S(1)} %pad_maximum_fusion.6.refs_0_), channel_id=1, source_target_pairs={{0,1},{1,0},{2,3},{3,2},{4,5},{5,4},{6,7},{7,6},{8,9},{9,8},{10,11... | collective-permute-start | bytes 663560 | tf_op jit(solution)/shard_map/ppermute | solution.py:197
  101.1 2.9 %collective-permute-start.11 = (bf16[3,72,512]{2,1,0:T(8,128)(2,1)S(1)}, bf16[3,72,512]{2,1,0:T(8,128)(2,1)S(1)}, u32[]{:S(2)}, u32[]{:S(2)}) collective-permute-start(bf16[3,72,512]{2,1,0:T(8,128)(2,1)S(1)} %collective-permute-done.8.refs_1_), channel_id=1, source_target_pairs={{0,1},{1,0},{2,3},{3,2},{4,5},{5,4},{6,7},{7,6},{8,9},{9,8},{10,11... | collective-permute-start | bytes 663560 | tf_op jit(solution)/shard_map/ppermute | solution.py:197
  104.0 1.9 %collective-permute-start.12 = (bf16[2,72,512]{2,1,0:T(8,128)(2,1)S(1)}, bf16[2,72,512]{2,1,0:T(8,128)(2,1)S(1)}, u32[]{:S(2)}, u32[]{:S(2)}) collective-permute-start(bf16[2,72,512]{2,1,0:T(8,128)(2,1)S(1)} %collective-permute-done.9.refs_2_), channel_id=1, source_target_pairs={{0,1},{1,0},{2,3},{3,2},{4,5},{5,4},{6,7},{7,6},{8,9},{9,8},{10,11... | collective-permute-start | bytes 442376 | tf_op jit(solution)/shard_map/ppermute | solution.py:197
  106.0 1.3 collective-permute-done.12.refs_5_
  107.3 3.4 %shard_map.48 = bf16[32,72,128]{2,1,0:T(8,128)(2,1)S(1)} custom-call(s32[2]{0:T(128)S(1)} %pad_add_fusion.where_ref, bf16[3,72,512]{2,1,0:T(8,128)(2,1)S(1)} %pad_maximum_fusion.6.refs_0_, bf16[3,72,512]{2,1,0:T(8,128)(2,1)S(1)} %collective-permute-done.8.refs_1_, bf16[2,72,512]{2,1,0:T(8,128)(2,1)S(1)} %collective-permute-done.9.refs_2_, ...), custom_call_target="tpu_custom_call" | custom-call | tf_op jit(solution)/shard_map/pallas_call | solution.py:147
  110.7 22.2 %all_to_all.10.shares_ref = bf16[32,72,128]{2,1,0:T(8,128)(2,1)S(1)} all-to-all(bf16[32,72,128]{2,1,0:T(8,128)(2,1)S(1)} %shard_map.48), channel_id=1, replica_groups=mesh['row'=32,'col'=16] {'row'}, dimensions={0} | all-to-all | bytes 1179648 | tf_op jit(solution)/shard_map/all_to_all | solution.py:244
  (41 shorter events, 8.8 us)
Async XLA Ops:
  1.7 28.0 %all-to-all-start = ((bf16[32,72,128]{2,1,0:T(8,128)(2,1)}), bf16[32,72,128]{2,1,0:T(8,128)(2,1)S(1)}, u32[]{:S(2)}, u32[]{:S(2)}) async-start(bf16[32,72,128]{2,1,0:T(8,128)(2,1)} %broadcast_in_dim.8), calls=%async_computation | async-start | bytes 1179648 | tf_op jit(solution)/shard_map/all_to_all | solution.py:201
  12.2 1.2 copy-start.2
  12.2 1.4 %copy-start.3 = (bf16[512,896]{1,0:T(8,128)(2,1)S(1)}, bf16[512,896]{1,0:T(8,128)(2,1)}, u32[]{:S(2)}) copy-start(bf16[512,896]{1,0:T(8,128)(2,1)} %param.6) | copy-start | bytes 2752516
  13.4 1.1 slice-start.1
  13.4 1.2 slice-start.2
  16.0 21.5 %collective-permute-start.1 = (bf16[512,896]{1,0:T(8,128)(2,1)}, bf16[512,896]{1,0:T(8,128)(2,1)S(1)}, u32[]{:S(2)}, u32[]{:S(2)}) collective-permute-start(bf16[512,896]{1,0:T(8,128)(2,1)} %get-tuple-element.6), channel_id=1, source_target_pairs={{0,1},{1,0},{2,3},{3,2},{4,5},{5,4},{6,7},{7,6},{8,9},{9,8},{10,11... | collective-permute-start | bytes 2752520 | tf_op jit(solution)/shard_map/ppermute | solution.py:197
  29.7 6.0 %collective-permute-start = (bf16[32,72,128]{2,1,0:T(8,128)(2,1)S(1)}, bf16[32,72,128]{2,1,0:T(8,128)(2,1)S(1)}, u32[]{:S(2)}, u32[]{:S(2)}) collective-permute-start(bf16[32,72,128]{2,1,0:T(8,128)(2,1)S(1)} %all-to-all-done.own_ref), channel_id=1, source_target_pairs={{0,1},{1,0},{2,3},{3,2},{4,5},{5,4},{6,7},{7,6},{8,9},{9,8},{10,11... | collective-permute-start | bytes 1769480 | tf_op jit(solution)/shard_map/ppermute | solution.py:197
  36.4 1.0 copy-start
  37.5 11.3 %slice-start = ((bf16[8,72,1024]{2,1,0:T(8,128)(2,1)}), bf16[2,72,1024]{2,1,0:T(8,128)(2,1)S(1)}, s32[]{:S(2)}) async-start(bf16[8,72,1024]{2,1,0:T(8,128)(2,1)} %copy-done), calls=%async_computation.2 | async-start | bytes 589824 | tf_op jit(solution)/shard_map/slice | solution.py:214
  38.1 21.4 %collective-permute-start.2 = (f16[3,72,896]{2,1,0:T(8,128)(2,1)S(1)}, f16[3,72,896]{2,1,0:T(8,128)(2,1)S(1)}, u32[]{:S(2)}, u32[]{:S(2)}) collective-permute-start(f16[3,72,896]{2,1,0:T(8,128)(2,1)S(1)} %bitcast.53), channel_id=1, source_target_pairs={{0,14},{1,15},{2,0},{3,1},{4,2},{5,3},{6,4},{7,5},{8,6},{9,7},{10,... | collective-permute-start | bytes 1161224 | tf_op jit(solution)/shard_map/ppermute | solution.py:196
  49.3 10.2 %collective-permute-start.3 = (f16[2,72,896]{2,1,0:T(8,128)(2,1)S(1)}, f16[2,72,896]{2,1,0:T(8,128)(2,1)S(1)}, u32[]{:S(2)}, u32[]{:S(2)}) collective-permute-start(f16[2,72,896]{2,1,0:T(8,128)(2,1)S(1)} %bitcast.54), channel_id=1, source_target_pairs={{0,2},{1,3},{2,4},{3,5},{4,6},{5,7},{6,8},{7,9},{8,10},{9,11},{10,... | collective-permute-start | bytes 774152 | tf_op jit(solution)/shard_map/ppermute | solution.py:196
  59.7 11.0 %collective-permute-start.4 = (f16[72,896]{1,0:T(8,128)(2,1)S(1)}, f16[72,896]{1,0:T(8,128)(2,1)S(1)}, u32[]{:S(2)}, u32[]{:S(2)}) collective-permute-start(f16[72,896]{1,0:T(8,128)(2,1)S(1)} %get-tuple-element.7), channel_id=1, source_target_pairs={{0,10},{1,11},{2,12},{3,13},{4,14},{5,15},{6,0},{7,1},{8,2},{9,3},... | collective-permute-start | bytes 387080 | tf_op jit(solution)/shard_map/ppermute | solution.py:196
  61.7 45.6 %copy-start.1 = (bf16[896,512]{1,0:T(8,128)(2,1)S(1)}, bf16[896,512]{1,0:T(8,128)(2,1)}, u32[]{:S(2)}) copy-start(bf16[896,512]{1,0:T(8,128)(2,1)} %refs_6_.1) | copy-start | bytes 2752516
  61.7 10.5 %collective-permute-start.5 = (f16[72,896]{1,0:T(8,128)(2,1)S(1)}, f16[72,896]{1,0:T(8,128)(2,1)S(1)}, u32[]{:S(2)}, u32[]{:S(2)}) collective-permute-start(f16[72,896]{1,0:T(8,128)(2,1)S(1)} %get-tuple-element.8), channel_id=1, source_target_pairs={{0,6},{1,7},{2,8},{3,9},{4,10},{5,11},{6,12},{7,13},{8,14},{9,15},... | collective-permute-start | bytes 387080 | tf_op jit(solution)/shard_map/ppermute | solution.py:196
  72.4 8.3 %collective-permute-start.7 = (bf16[72,512]{1,0:T(8,128)(2,1)S(1)}, bf16[72,512]{1,0:T(8,128)(2,1)S(1)}, u32[]{:S(2)}, u32[]{:S(2)}) collective-permute-start(bf16[72,512]{1,0:T(8,128)(2,1)S(1)} %shard_map.47), channel_id=1, source_target_pairs={{0,6},{1,7},{2,8},{3,9},{4,10},{5,11},{6,12},{7,13},{8,14},{9,15},... | collective-permute-start | bytes 221192 | tf_op jit(solution)/shard_map/ppermute | solution.py:196
  74.9 9.0 %collective-permute-start.6 = (bf16[72,512]{1,0:T(8,128)(2,1)S(1)}, bf16[72,512]{1,0:T(8,128)(2,1)S(1)}, u32[]{:S(2)}, u32[]{:S(2)}) collective-permute-start(bf16[72,512]{1,0:T(8,128)(2,1)S(1)} %shard_map.47), channel_id=1, source_target_pairs={{0,10},{1,11},{2,12},{3,13},{4,14},{5,15},{6,0},{7,1},{8,2},{9,3},... | collective-permute-start | bytes 221192 | tf_op jit(solution)/shard_map/ppermute | solution.py:196
  83.9 17.2 %collective-permute-start.8 = (bf16[3,72,512]{2,1,0:T(8,128)(2,1)S(1)}, bf16[3,72,512]{2,1,0:T(8,128)(2,1)S(1)}, u32[]{:S(2)}, u32[]{:S(2)}) collective-permute-start(bf16[3,72,512]{2,1,0:T(8,128)(2,1)S(1)} %pad_maximum_fusion.6.refs_0_), channel_id=1, source_target_pairs={{0,2},{1,3},{2,4},{3,5},{4,6},{5,7},{6,8},{7,9},{8,10},{9,11},{10,... | collective-permute-start | bytes 663560 | tf_op jit(solution)/shard_map/ppermute | solution.py:196
  90.7 13.3 %collective-permute-start.9 = (bf16[2,72,512]{2,1,0:T(8,128)(2,1)S(1)}, bf16[2,72,512]{2,1,0:T(8,128)(2,1)S(1)}, u32[]{:S(2)}, u32[]{:S(2)}) collective-permute-start(bf16[2,72,512]{2,1,0:T(8,128)(2,1)S(1)} %pad_maximum_fusion.7), channel_id=1, source_target_pairs={{0,14},{1,15},{2,0},{3,1},{4,2},{5,3},{6,4},{7,5},{8,6},{9,7},{10,... | collective-permute-start | bytes 442376 | tf_op jit(solution)/shard_map/ppermute | solution.py:196
  97.7 8.3 %collective-permute-start.10 = (bf16[3,72,512]{2,1,0:T(8,128)(2,1)S(1)}, bf16[3,72,512]{2,1,0:T(8,128)(2,1)S(1)}, u32[]{:S(2)}, u32[]{:S(2)}) collective-permute-start(bf16[3,72,512]{2,1,0:T(8,128)(2,1)S(1)} %pad_maximum_fusion.6.refs_0_), channel_id=1, source_target_pairs={{0,1},{1,0},{2,3},{3,2},{4,5},{5,4},{6,7},{7,6},{8,9},{9,8},{10,11... | collective-permute-start | bytes 663560 | tf_op jit(solution)/shard_map/ppermute | solution.py:197
  101.1 6.2 %collective-permute-start.11 = (bf16[3,72,512]{2,1,0:T(8,128)(2,1)S(1)}, bf16[3,72,512]{2,1,0:T(8,128)(2,1)S(1)}, u32[]{:S(2)}, u32[]{:S(2)}) collective-permute-start(bf16[3,72,512]{2,1,0:T(8,128)(2,1)S(1)} %collective-permute-done.8.refs_1_), channel_id=1, source_target_pairs={{0,1},{1,0},{2,3},{3,2},{4,5},{5,4},{6,7},{7,6},{8,9},{9,8},{10,11... | collective-permute-start | bytes 663560 | tf_op jit(solution)/shard_map/ppermute | solution.py:197
  104.0 3.3 %collective-permute-start.12 = (bf16[2,72,512]{2,1,0:T(8,128)(2,1)S(1)}, bf16[2,72,512]{2,1,0:T(8,128)(2,1)S(1)}, u32[]{:S(2)}, u32[]{:S(2)}) collective-permute-start(bf16[2,72,512]{2,1,0:T(8,128)(2,1)S(1)} %collective-permute-done.9.refs_2_), channel_id=1, source_target_pairs={{0,1},{1,0},{2,3},{3,2},{4,5},{5,4},{6,7},{7,6},{8,9},{9,8},{10,11... | collective-permute-start | bytes 442376 | tf_op jit(solution)/shard_map/ppermute | solution.py:197

commit v2 on v0

v2 whole, which is shorter than its diff:
```python
import functools

import jax
import jax.numpy as jnp
from jax import lax
from jax.experimental import pallas as pl
from jax.experimental.pallas import tpu as pltpu
from jax.sharding import PartitionSpec as P

LANES = 128
MAIN = 16
EXTRA = 2
PAIR = 2
STRIDE = 48
LIMIT = pltpu.CompilerParams(vmem_limit_bytes=48 * 1024 * 1024)
SCALAR = pl.BlockSpec(memory_space=pltpu.SMEM)
WHOLE = pl.BlockSpec(memory_space=pltpu.VMEM)
SCALE = 16.0


def lanes(q):
    return slice(q * LANES, (q + 1) * LANES)


def rows_of(q, count):
    return slice(q * count, (q + 1) * count)


def gather_extra(tiles, shift_of):
    row = lax.broadcasted_iota(jnp.int32, tiles[0].shape, 0) // EXTRA
    out = tiles[0] if shift_of(0) % 8 == 0 else pltpu.roll(tiles[0], shift_of(0) % 8, 0)
    for q in range(1, len(tiles)):
        moved = tiles[q]
        if shift_of(q) % 8:
            moved = pltpu.roll(moved, shift_of(q) % 8, 0)
        out = jnp.where(row == q, moved, out)
    return out


def spread_kernel(x_ref, out_ref):
    x = x_ref[...].astype(jnp.float32)
    tiles = x.shape[1] // LANES
    for q in range(tiles):
        for r in range(out_ref.shape[0]):
            out_ref[r, rows_of(q, MAIN), :] = x_ref[:MAIN, lanes(q)]
    tail = jnp.concatenate(
        [x[MAIN:, lanes(q)] for q in range(tiles)], axis=0
    ).astype(jnp.bfloat16)
    for r in range(out_ref.shape[0]):
        out_ref[r, tiles * MAIN :, :] = tail


def spread(x, copies):
    rows = x.shape[0] * x.shape[1] // LANES
    return pl.pallas_call(
        spread_kernel,
        out_shape=jax.ShapeDtypeStruct((copies, rows, LANES), x.dtype),
        in_specs=[WHOLE],
        out_specs=WHOLE,
        compiler_params=LIMIT,
    )(x)


def up_kernel(core_ref, own_ref, other_ref, *refs):
    gate_own, gate_other, up_own, up_other, out_ref, held = refs
    blocks = out_ref.shape[0]
    tiles = own_ref.shape[1] // (MAIN + EXTRA)
    width = tiles * LANES
    wide_tiles = gate_own.shape[1] // LANES
    span = PAIR * MAIN
    r = lax.broadcasted_iota(jnp.int32, (tiles * 8, PAIR * 8), 0)
    c = lax.broadcasted_iota(jnp.int32, (tiles * 8, PAIR * 8), 1)
    n = (r % 8) % (PAIR * EXTRA)
    place = c == (n // EXTRA) * 8 + (r // 8) * EXTRA + n % EXTRA
    place = place.astype(jnp.bfloat16)
    for b in range(blocks):
        tails = []
        for s in range(PAIR):
            own = own_ref[b * 2 * PAIR + core_ref[0] * PAIR + s]
            other = other_ref[b, s]
            for q in range(tiles):
                held[b, rows_of(s, MAIN), lanes(q)] = own[rows_of(q, MAIN)]
                held[b, rows_of(s, MAIN), lanes(tiles + q)] = other[rows_of(q, MAIN)]
            tails.append(
                jnp.concatenate([own[tiles * MAIN :], other[tiles * MAIN :]], axis=1)
            )
        moved = jnp.dot(
            place,
            jnp.concatenate(tails, axis=0),
            preferred_element_type=jnp.float32,
        ).astype(jnp.bfloat16)
        for q in range(tiles):
            held[b, span : span + 8, lanes(q)] = moved[rows_of(q, 8), :LANES]
            held[b, span : span + 8, lanes(tiles + q)] = moved[rows_of(q, 8), LANES:]
    left = held[:, :, :width].reshape(blocks * STRIDE, width)
    right = held[:, :, width:].reshape(blocks * STRIDE, width)
    top = lax.broadcasted_iota(jnp.int32, (8, LANES), 0) < PAIR * EXTRA

    def dot(x, w):
        return jnp.dot(x, w, preferred_element_type=jnp.float32)

    gate = (dot(left, gate_own[...]) + dot(right, gate_other[...])) * SCALE
    up = (dot(left, up_own[...]) + dot(right, up_other[...])) * SCALE
    for b in range(blocks):
        at = b * STRIDE
        for j in range(wide_tiles):
            out_ref[b, rows_of(j, span), :] = gate[at : at + span, lanes(j)]
            out_ref[b, rows_of(wide_tiles + j, span), :] = up[at : at + span, lanes(j)]
            mixed = jnp.where(
                top,
                gate[at + span : at + span + 8, lanes(j)],
                up[at + span : at + span + 8, lanes(j)],
            )
            start = 2 * wide_tiles * span + 8 * j
            out_ref[b, start : start + 8, :] = mixed


def up_product(core, own, other, gate_own, gate_other, up_own, up_other):
    blocks = other.shape[0]
    tiles = own.shape[1] // (MAIN + EXTRA)
    rows = PAIR * (MAIN + EXTRA) * 2 * gate_own.shape[1] // LANES
    return pl.pallas_call(
        up_kernel,
        out_shape=jax.ShapeDtypeStruct((blocks, rows, LANES), jnp.float32),
        in_specs=[SCALAR] + [WHOLE] * 6,
        out_specs=WHOLE,
        scratch_shapes=[pltpu.VMEM((blocks, STRIDE, 2 * tiles * LANES), jnp.bfloat16)],
        compiler_params=LIMIT,
    )(core, own, other, gate_own, gate_other, up_own, up_other)


def activate_kernel(sum_ref, out_ref):
    span = PAIR * MAIN
    wide_tiles = out_ref.shape[1] // LANES
    for j in range(wide_tiles):
        gate = sum_ref[rows_of(j, span), :]
        up = sum_ref[rows_of(wide_tiles + j, span), :]
        out_ref[:span, lanes(j)] = (gate / (1 + jnp.exp(-gate)) * up).astype(
            jnp.bfloat16
        )
        start = 2 * wide_tiles * span + 8 * j
        mixed = sum_ref[start : start + 8, :]
        tail = mixed / (1 + jnp.exp(-mixed)) * pltpu.roll(mixed, PAIR * EXTRA, 0)
        out_ref[span:, lanes(j)] = tail[: PAIR * EXTRA].astype(jnp.bfloat16)


def activate(total, hidden_width):
    return pl.pallas_call(
        activate_kernel,
        out_shape=jax.ShapeDtypeStruct(
            (PAIR * (MAIN + EXTRA), hidden_width), jnp.bfloat16
        ),
        in_specs=[WHOLE],
        out_specs=WHOLE,
        compiler_params=LIMIT,
    )(total)


def down_kernel(hidden_ref, weight_ref, out_ref, held):
    blocks, count = hidden_ref.shape[:2]
    span = PAIR * MAIN
    for b in range(blocks):
        held[b, :count, :] = hidden_ref[b]
    tiles = weight_ref.shape[1] // LANES
    result = jnp.dot(
        held[...].reshape(blocks * STRIDE, held.shape[2]),
        weight_ref[...],
        preferred_element_type=jnp.float32,
    )
    for b in range(blocks):
        at = b * STRIDE
        ends = [result[at + span : at + span + 8, lanes(q)] for q in range(tiles)]
        for s in range(PAIR):
            for q in range(tiles):
                out_ref[b * PAIR + s, rows_of(q, MAIN), :] = result[
                    at + s * MAIN : at + (s + 1) * MAIN, lanes(q)
                ].astype(jnp.bfloat16)
            tail = gather_extra(ends, lambda q: (q - s) * EXTRA)
            out_ref[b * PAIR + s, tiles * MAIN :, :] = tail.astype(jnp.bfloat16)


def down_product(hidden, weight):
    blocks, count, width = hidden.shape
    rows = (MAIN + EXTRA) * weight.shape[1] // LANES
    return pl.pallas_call(
        down_kernel,
        out_shape=jax.ShapeDtypeStruct((PAIR * blocks, rows, LANES), jnp.bfloat16),
        in_specs=[WHOLE] * 2,
        out_specs=WHOLE,
        scratch_shapes=[pltpu.VMEM((blocks, STRIDE, width), jnp.bfloat16)],
        compiler_params=LIMIT,
    )(hidden, weight)


def finish_kernel(shares_ref, out_ref):
    tiles = out_ref.shape[1] // LANES
    total = shares_ref[0].astype(jnp.float32)
    for r in range(1, shares_ref.shape[0]):
        total += shares_ref[r].astype(jnp.float32)
    for q in range(tiles):
        out_ref[:MAIN, lanes(q)] = total[rows_of(q, MAIN)].astype(jnp.bfloat16)
        tail = total[tiles * MAIN + q * EXTRA : tiles * MAIN + (q + 1) * EXTRA]
        out_ref[MAIN:, lanes(q)] = tail.astype(jnp.bfloat16)


def finish(shares):
    width = shares.shape[1] // (MAIN + EXTRA) * LANES
    return pl.pallas_call(
        finish_kernel,
        out_shape=jax.ShapeDtypeStruct((MAIN + EXTRA, width), jnp.bfloat16),
        in_specs=[WHOLE],
        out_specs=WHOLE,
        compiler_params=LIMIT,
    )(shares)


def shards(activations, gate_matrix, up_matrix, down_matrix):
    n_row, n_col = lax.axis_size("row"), lax.axis_size("col")
    depth = n_col // 2
    core = lax.axis_index("col") % 2
    same_core = [[2 * i + k for i in range(depth)] for k in range(2)]

    def other_core(x):
        return lax.ppermute(x, "col", [(i, i ^ 1) for i in range(n_col)])

    own = lax.all_to_all(spread(activations, n_row), "row", 0, 0, tiled=True)
    gate_other, up_other = other_core(gate_matrix), other_core(up_matrix)
    by_core = own.reshape(depth, 2, PAIR, *own.shape[1:])
    give = lax.dynamic_index_in_dim(by_core, 1 - core, 1, keepdims=False)
    terms = up_product(
        core.reshape(1),
        own,
        other_core(give),
        gate_matrix,
        gate_other,
        up_matrix,
        up_other,
    )
    terms = lax.all_to_all(
        terms.astype(jnp.float16),
        "col",
        0,
        0,
        axis_index_groups=same_core,
        tiled=True,
    )
    total = jnp.sum(terms.astype(jnp.float32), axis=0) * (1 / SCALE)
    hidden = activate(total, gate_matrix.shape[1])
    gathered = lax.all_gather(hidden, "col", axis=0, tiled=False)
    share = down_product(gathered, down_matrix)
    return finish(lax.all_to_all(share, "row", 0, 0, tiled=True))


def solution(mesh):
    placed = (P("row", "col"), P("col", "row"), P("col", "row"), P("row", "col"))
    return jax.shard_map(
        shards, mesh=mesh, in_specs=placed, out_specs=P("row", "col"), check_vma=False
    )
```

time: 316 us -> 123 us (0.39)
  the two profiles are of different devices: /device:TPU:14 before, /device:TPU:1 now
where the time goes in v2:
time: 123 us
  blocking collectives  79.2 us (64%)
  starting transfers between devices  19.7 us (16%)
  waiting for transfers between devices  13.8 us (11%)
  Pallas kernels  7.06 us (6%)
  other arithmetic  1.87 us (2%)
    all_to_all x1, blocking collectives, shards(): lax.all_to_all(terms.astype(jnp.float16), 'col', 0, 0, axis_index_groups=...  37.4 us
    all_to_all x1, blocking collectives, shards(): return finish(lax.all_to_all(share, 'row', 0, 0, tiled=True))  22.2 us
    all_gather x1, blocking collectives, shards(): gathered = lax.all_gather(hidden, 'col', axis=0, tiled=False)  19.6 us
    all_to_all x1, waiting for transfers between devices, shards(): own = lax.all_to_all(spread(activations, n_row), 'row', 0, 0, tiled=True)  12.7 us
    all_to_all x1, starting transfers between devices, shards(): own = lax.all_to_all(spread(activations, n_row), 'row', 0, 0, tiled=True)  10.5 us
    ppermute x3, starting transfers between devices, other_core(): return lax.ppermute(x, 'col', [(i, i ^ 1) for i in range(n_col)])  9.17 us
    pallas_call x1, Pallas kernels, up_product(): pl.pallas_call(up_kernel, out_shape=jax.ShapeDtypeStruct((blocks, rows, L...  4.4 us
  transfers between devices with their start and end apart: 4, of which 2 were waited for; matrix products, arithmetic and copies ran while one was open for 0% of the time, Pallas kernels for 0%

profile of v2, /device:TPU:1, one launch (start us, length us, event | category | flops | bytes accessed | tf_op | source)
XLA Modules:
  0.0 122.7 jit_solution(13027558078354306300)
XLA Ops:
  0.0 0.0 copy-start.1
  0.0 0.0 copy-start.2
  0.0 0.9 copy-done.3
  0.9 0.9 shard_map.46
  1.8 10.5 %all-to-all-start = ((bf16[32,72,128]{2,1,0:T(8,128)(2,1)}), bf16[32,72,128]{2,1,0:T(8,128)(2,1)S(1)}, u32[]{:S(2)}, u32[]{:S(2)}) async-start(bf16[32,72,128]{2,1,0:T(8,128)(2,1)} %shard_map.46), calls=%async_computation | async-start | bytes 1179648 | tf_op jit(solution)/shard_map/all_to_all | solution.py:226
  12.3 2.9 %collective-permute-start.1 = (bf16[512,896]{1,0:T(8,128)(2,1)}, bf16[512,896]{1,0:T(8,128)(2,1)S(1)}, u32[]{:S(2)}, u32[]{:S(2)}) collective-permute-start(bf16[512,896]{1,0:T(8,128)(2,1)} %refs_0_.1), channel_id=1, source_target_pairs={{0,1},{1,0},{2,3},{3,2},{4,5},{5,4},{6,7},{7,6},{8,9},{9,8},{10,11... | collective-permute-start | bytes 2752520 | tf_op jit(solution)/shard_map/ppermute | solution.py:224
  15.2 1.9 %collective-permute-start.2 = (bf16[512,896]{1,0:T(8,128)(2,1)}, bf16[512,896]{1,0:T(8,128)(2,1)}, u32[]{:S(2)}, u32[]{:S(2)}) collective-permute-start(bf16[512,896]{1,0:T(8,128)(2,1)} %refs_2_.1), channel_id=1, source_target_pairs={{0,1},{1,0},{2,3},{3,2},{4,5},{5,4},{6,7},{7,6},{8,9},{9,8},{10,11... | collective-permute-start | bytes 2752520 | tf_op jit(solution)/shard_map/ppermute | solution.py:224
  17.1 12.7 %all-to-all-done.own_ref = bf16[32,72,128]{2,1,0:T(8,128)(2,1)S(1)} async-done(((bf16[32,72,128]{2,1,0:T(8,128)(2,1)}), bf16[32,72,128]{2,1,0:T(8,128)(2,1)S(1)}, u32[]{:S(2)}, u32[]{:S(2)}) %all-to-all-start) | async-done | bytes 589856 | tf_op jit(solution)/shard_map/all_to_all | solution.py:226
  29.8 4.4 %collective-permute-start = (bf16[8,2,72,128]{3,2,1,0:T(8,128)(2,1)S(1)}, bf16[8,2,72,128]{3,2,1,0:T(8,128)(2,1)S(1)}, u32[]{:S(2)}, u32[]{:S(2)}) collective-permute-start(bf16[8,2,72,128]{3,2,1,0:T(8,128)(2,1)S(1)} %dynamic-slice_bitcast_fusion), channel_id=1, source_target_pairs={{0,1},{1,0},{2,3},{3,2},{4,5},{5,4},{6,7},{7,6},{8,9},{9,8},{10,11... | collective-permute-start | bytes 884744 | tf_op jit(solution)/shard_map/ppermute | solution.py:224
  34.2 0.0 collective-permute-done.1.refs_1_
  34.2 0.0 collective-permute-done.2.refs_3_
  34.2 1.2 collective-permute-done.other_ref
  35.4 0.0 copy-done.1
  35.4 0.0 copy-done.2
  35.4 4.4 %shard_map.47 = f32[8,504,128]{2,1,0:T(8,128)} custom-call(s32[1]{0:T(128)} %bitcast.core_ref, bf16[32,72,128]{2,1,0:T(8,128)(2,1)S(1)} %all-to-all-done.own_ref, bf16[8,2,72,128]{3,2,1,0:T(8,128)(2,1)S(1)} %collective-permute-done.other_ref, bf16[512,896]{1,0:T(8,128)(2,1)S(1)} %copy-done.1, bf16[512,896]{1,0:T(8,128)(2,1)S(1)} %collective-permute-done.1.refs_1_, ...), custom_call_target="tpu_custom_call" | custom-call | tf_op jit(solution)/shard_map/pallas_call | solution.py:122
  39.8 1.7 %convert_element_type.6 = f16[8,504,128]{2,1,0:T(8,128)(2,1)S(1)} convert(f32[8,504,128]{2,1,0:T(8,128)} %shard_map.47) | non-fusion elementwise | flops 516096 | bytes 3096576 | tf_op jit(solution)/shard_map/convert_element_type | solution.py:240
  41.5 37.4 %all_to_all.15 = f16[8,504,128]{2,1,0:T(8,128)(2,1)S(1)} all-to-all(f16[8,504,128]{2,1,0:T(8,128)(2,1)S(1)} %convert_element_type.6), channel_id=1, replica_groups={{0,2,4,6,8,10,12,14},{1,3,5,7,9,11,13,15},{16,18,20,22,24,26,28,30},{17..., dimensions={0} | all-to-all | bytes 2064384 | tf_op jit(solution)/shard_map/all_to_all | solution.py:239
  78.9 0.1 convert_reduce_fusion
  79.1 0.1 shard_map.48
  79.1 19.6 %all-gather.1.hidden_ref = bf16[16,36,896]{2,1,0:T(8,128)(2,1)S(1)} all-gather(bf16[1,36,896]{2,1,0:T(8,128)(2,1)S(1)} %bitcast.8), channel_id=2, replica_groups=mesh['row'=32,'col'=16] {'col'}, dimensions={0}, use_global_device_ids=true | all-gather | bytes 1096704 | tf_op jit(solution)/shard_map/all_gather | solution.py:249
  98.7 0.0 copy-done
  98.7 1.0 shard_map.49
  99.7 22.2 %all_to_all.16.shares_ref = bf16[32,72,128]{2,1,0:T(8,128)(2,1)S(1)} all-to-all(bf16[32,72,128]{2,1,0:T(8,128)(2,1)S(1)} %shard_map.49), channel_id=1, replica_groups=mesh['row'=32,'col'=16] {'row'}, dimensions={0} | all-to-all | bytes 1179648 | tf_op jit(solution)/shard_map/all_to_all | solution.py:251
  121.9 0.7 shard_map.50
  (4 shorter events, 0.0 us)
Async XLA Ops:
  0.0 35.4 %copy-start.1 = (bf16[512,896]{1,0:T(8,128)(2,1)S(1)}, bf16[512,896]{1,0:T(8,128)(2,1)}, u32[]{:S(2)}) copy-start(bf16[512,896]{1,0:T(8,128)(2,1)} %refs_0_.1) | copy-start | bytes 2752516
  0.0 35.4 %copy-start.2 = (bf16[512,896]{1,0:T(8,128)(2,1)S(1)}, bf16[512,896]{1,0:T(8,128)(2,1)}, u32[]{:S(2)}) copy-start(bf16[512,896]{1,0:T(8,128)(2,1)} %refs_2_.1) | copy-start | bytes 2752516
  0.0 0.9 copy-start.3
  1.8 28.0 %all-to-all-start = ((bf16[32,72,128]{2,1,0:T(8,128)(2,1)}), bf16[32,72,128]{2,1,0:T(8,128)(2,1)S(1)}, u32[]{:S(2)}, u32[]{:S(2)}) async-start(bf16[32,72,128]{2,1,0:T(8,128)(2,1)} %shard_map.46), calls=%async_computation | async-start | bytes 1179648 | tf_op jit(solution)/shard_map/all_to_all | solution.py:226
  12.3 21.9 %collective-permute-start.1 = (bf16[512,896]{1,0:T(8,128)(2,1)}, bf16[512,896]{1,0:T(8,128)(2,1)S(1)}, u32[]{:S(2)}, u32[]{:S(2)}) collective-permute-start(bf16[512,896]{1,0:T(8,128)(2,1)} %refs_0_.1), channel_id=1, source_target_pairs={{0,1},{1,0},{2,3},{3,2},{4,5},{5,4},{6,7},{7,6},{8,9},{9,8},{10,11... | collective-permute-start | bytes 2752520 | tf_op jit(solution)/shard_map/ppermute | solution.py:224
  15.2 19.0 %collective-permute-start.2 = (bf16[512,896]{1,0:T(8,128)(2,1)}, bf16[512,896]{1,0:T(8,128)(2,1)}, u32[]{:S(2)}, u32[]{:S(2)}) collective-permute-start(bf16[512,896]{1,0:T(8,128)(2,1)} %refs_2_.1), channel_id=1, source_target_pairs={{0,1},{1,0},{2,3},{3,2},{4,5},{5,4},{6,7},{7,6},{8,9},{9,8},{10,11... | collective-permute-start | bytes 2752520 | tf_op jit(solution)/shard_map/ppermute | solution.py:224
  29.8 5.6 %collective-permute-start = (bf16[8,2,72,128]{3,2,1,0:T(8,128)(2,1)S(1)}, bf16[8,2,72,128]{3,2,1,0:T(8,128)(2,1)S(1)}, u32[]{:S(2)}, u32[]{:S(2)}) collective-permute-start(bf16[8,2,72,128]{3,2,1,0:T(8,128)(2,1)S(1)} %dynamic-slice_bitcast_fusion), channel_id=1, source_target_pairs={{0,1},{1,0},{2,3},{3,2},{4,5},{5,4},{6,7},{7,6},{8,9},{9,8},{10,11... | collective-permute-start | bytes 884744 | tf_op jit(solution)/shard_map/ppermute | solution.py:224
  78.9 19.8 %copy-start = (bf16[896,512]{1,0:T(8,128)(2,1)S(1)}, bf16[896,512]{1,0:T(8,128)(2,1)}, u32[]{:S(2)}) copy-start(bf16[896,512]{1,0:T(8,128)(2,1)} %weight_ref.1) | copy-start | bytes 2752516

commit v3 on v2

v3 whole, which is shorter than its diff:
```python
import functools

import jax
import jax.numpy as jnp
from jax import lax
from jax.experimental import pallas as pl
from jax.experimental.pallas import tpu as pltpu
from jax.sharding import PartitionSpec as P

LANES = 128
MAIN = 16
EXTRA = 2
PAIR = 2
STRIDE = 48
LIMIT = pltpu.CompilerParams(vmem_limit_bytes=24 * 1024 * 1024)
SCALAR = pl.BlockSpec(memory_space=pltpu.SMEM)
WHOLE = pl.BlockSpec(memory_space=pltpu.VMEM)
SCALE = 16.0


def lanes(q):
    return slice(q * LANES, (q + 1) * LANES)


def rows_of(q, count):
    return slice(q * count, (q + 1) * count)


def gather_extra(tiles, shift_of):
    row = lax.broadcasted_iota(jnp.int32, tiles[0].shape, 0) // EXTRA
    out = tiles[0] if shift_of(0) % 8 == 0 else pltpu.roll(tiles[0], shift_of(0) % 8, 0)
    for q in range(1, len(tiles)):
        moved = tiles[q]
        if shift_of(q) % 8:
            moved = pltpu.roll(moved, shift_of(q) % 8, 0)
        out = jnp.where(row == q, moved, out)
    return out


def spread_kernel(x_ref, out_ref):
    x = x_ref[...].astype(jnp.float32)
    tiles = x.shape[1] // LANES
    for q in range(tiles):
        for r in range(out_ref.shape[0]):
            out_ref[r, rows_of(q, MAIN), :] = x_ref[:MAIN, lanes(q)]
    tail = jnp.concatenate(
        [x[MAIN:, lanes(q)] for q in range(tiles)], axis=0
    ).astype(jnp.bfloat16)
    for r in range(out_ref.shape[0]):
        out_ref[r, tiles * MAIN :, :] = tail


def spread(x, copies):
    rows = x.shape[0] * x.shape[1] // LANES
    return pl.pallas_call(
        spread_kernel,
        out_shape=jax.ShapeDtypeStruct((copies, rows, LANES), x.dtype),
        in_specs=[WHOLE],
        out_specs=WHOLE,
        compiler_params=LIMIT,
    )(x)


def add_product(own_at, gate_ref, up_ref, base_ref, out_ref, held):
    blocks = out_ref.shape[0]
    tiles = held.shape[1] // LANES
    wide_tiles = gate_ref.shape[1] // LANES
    span = PAIR * MAIN
    shape = (tiles * blocks * 8, blocks * PAIR * 8)
    r = lax.broadcasted_iota(jnp.int32, shape, 0)
    c = lax.broadcasted_iota(jnp.int32, shape, 1)
    q, b, n = r // (blocks * 8), r // 8 % blocks, r % (PAIR * EXTRA)
    place = c == b * PAIR * 8 + n // EXTRA * 8 + q * EXTRA + n % EXTRA
    tails = []
    for b in range(blocks):
        for s in range(PAIR):
            block = own_at(b, s)
            for q in range(tiles):
                at = b * span + s * MAIN
                held[at : at + MAIN, lanes(q)] = block[rows_of(q, MAIN)]
            tails.append(block[tiles * MAIN :])
    moved = jnp.dot(
        place.astype(jnp.bfloat16),
        jnp.concatenate(tails, axis=0),
        preferred_element_type=jnp.float32,
    ).astype(jnp.bfloat16)
    for q in range(tiles):
        held[blocks * span :, lanes(q)] = moved[rows_of(q, blocks * 8)]
    top = lax.broadcasted_iota(jnp.int32, (8, LANES), 0) < PAIR * EXTRA
    x = held[...]
    for first in range(0, wide_tiles, 2):
        count = min(2, wide_tiles - first)
        columns = slice(first * LANES, (first + count) * LANES)
        gate = jnp.dot(x, gate_ref[:, columns], preferred_element_type=jnp.float32)
        up = jnp.dot(x, up_ref[:, columns], preferred_element_type=jnp.float32)
        for i in range(count):
            j = first + i
            for b in range(blocks):
                at = slice(b * span, (b + 1) * span)
                end = slice(blocks * span + b * 8, blocks * span + b * 8 + 8)
                start = 2 * wide_tiles * span + 8 * j
                mixed = jnp.where(top, gate[end, lanes(i)], up[end, lanes(i)])
                for where, value in (
                    (rows_of(j, span), gate[at, lanes(i)]),
                    (rows_of(wide_tiles + j, span), up[at, lanes(i)]),
                    (slice(start, start + 8), mixed),
                ):
                    if base_ref is not None:
                        value += base_ref[b, where, :]
                    out_ref[b, where, :] = value


def own_kernel(core_ref, own_ref, gate_ref, up_ref, out_ref, held):
    def own_at(b, s):
        return own_ref[b * 2 * PAIR + core_ref[0] * PAIR + s]

    add_product(own_at, gate_ref, up_ref, None, out_ref, held)


def other_kernel(other_ref, gate_ref, up_ref, base_ref, out_ref, held):
    add_product(
        lambda b, s: other_ref[b, s], gate_ref, up_ref, base_ref, out_ref, held
    )


def up_product(kernel, specs, blocks, operands, gate, up, *base):
    rows = PAIR * (MAIN + EXTRA) * 2 * gate.shape[1] // LANES
    held = pltpu.VMEM((blocks * (PAIR * MAIN + 8), gate.shape[0]), jnp.bfloat16)
    return pl.pallas_call(
        kernel,
        out_shape=pltpu.VMEM((blocks, rows, LANES), jnp.float32),
        in_specs=specs + [WHOLE] * (2 + len(base)),
        out_specs=WHOLE,
        scratch_shapes=[held],
        compiler_params=LIMIT,
    )(*operands, gate, up, *base)


def activate_kernel(theirs_ref, mine_ref, out_ref):
    def total(rows):
        return theirs_ref[rows, :] * (1 / SCALE) + mine_ref[rows, :]

    span = PAIR * MAIN
    wide_tiles = out_ref.shape[1] // LANES
    for j in range(wide_tiles):
        gate = total(rows_of(j, span))
        up = total(rows_of(wide_tiles + j, span))
        out_ref[:span, lanes(j)] = (gate / (1 + jnp.exp(-gate)) * up).astype(
            jnp.bfloat16
        )
        start = 2 * wide_tiles * span + 8 * j
        mixed = total(slice(start, start + 8))
        tail = mixed / (1 + jnp.exp(-mixed)) * pltpu.roll(mixed, PAIR * EXTRA, 0)
        out_ref[span:, lanes(j)] = tail[: PAIR * EXTRA].astype(jnp.bfloat16)


def activate(theirs, mine, hidden_width):
    return pl.pallas_call(
        activate_kernel,
        out_shape=jax.ShapeDtypeStruct(
            (PAIR * (MAIN + EXTRA), hidden_width), jnp.bfloat16
        ),
        in_specs=[WHOLE] * 2,
        out_specs=WHOLE,
        compiler_params=LIMIT,
    )(theirs, mine)


def down_kernel(hidden_ref, weight_ref, out_ref, held):
    blocks, count = hidden_ref.shape[:2]
    span = PAIR * MAIN
    for b in range(blocks):
        held[b, :count, :] = hidden_ref[b]
    tiles = weight_ref.shape[1] // LANES
    result = jnp.dot(
        held[...].reshape(blocks * STRIDE, held.shape[2]),
        weight_ref[...],
        preferred_element_type=jnp.float32,
    )
    for b in range(blocks):
        at = b * STRIDE
        ends = [result[at + span : at + span + 8, lanes(q)] for q in range(tiles)]
        for s in range(PAIR):
            for q in range(tiles):
                out_ref[b * PAIR + s, rows_of(q, MAIN), :] = result[
                    at + s * MAIN : at + (s + 1) * MAIN, lanes(q)
                ].astype(jnp.bfloat16)
            tail = gather_extra(ends, lambda q: (q - s) * EXTRA)
            out_ref[b * PAIR + s, tiles * MAIN :, :] = tail.astype(jnp.bfloat16)


def down_product(hidden, weight):
    blocks, count, width = hidden.shape
    rows = (MAIN + EXTRA) * weight.shape[1] // LANES
    return pl.pallas_call(
        down_kernel,
        out_shape=jax.ShapeDtypeStruct((PAIR * blocks, rows, LANES), jnp.bfloat16),
        in_specs=[WHOLE] * 2,
        out_specs=WHOLE,
        scratch_shapes=[pltpu.VMEM((blocks, STRIDE, width), jnp.bfloat16)],
        compiler_params=LIMIT,
    )(hidden, weight)


def finish_kernel(me_ref, mine_ref, shares_ref, out_ref):
    tiles = out_ref.shape[1] // LANES
    total = mine_ref[...]
    for r in range(shares_ref.shape[0]):
        share = shares_ref[r].astype(jnp.float32)
        total += jnp.where(r == me_ref[0], 0.0, share)
    for q in range(tiles):
        out_ref[:MAIN, lanes(q)] = total[rows_of(q, MAIN)].astype(jnp.bfloat16)
        tail = total[tiles * MAIN + q * EXTRA : tiles * MAIN + (q + 1) * EXTRA]
        out_ref[MAIN:, lanes(q)] = tail.astype(jnp.bfloat16)


def finish(me, mine, shares):
    width = shares.shape[1] // (MAIN + EXTRA) * LANES
    return pl.pallas_call(
        finish_kernel,
        out_shape=jax.ShapeDtypeStruct((MAIN + EXTRA, width), jnp.bfloat16),
        in_specs=[SCALAR, WHOLE, WHOLE],
        out_specs=WHOLE,
        compiler_params=LIMIT,
    )(me, mine, shares)


def shards(activations, gate_matrix, up_matrix, down_matrix):
    n_row, n_col = lax.axis_size("row"), lax.axis_size("col")
    depth = n_col // 2
    core = lax.axis_index("col") % 2
    same_core = [[2 * i + k for i in range(depth)] for k in range(2)]

    def other_core(x):
        return lax.ppermute(x, "col", [(i, i ^ 1) for i in range(n_col)])

    own = lax.all_to_all(spread(activations, n_row), "row", 0, 0, tiled=True)
    gate_other, up_other = other_core(gate_matrix), other_core(up_matrix)
    by_core = own.reshape(depth, 2, PAIR, *own.shape[1:])
    give = lax.dynamic_index_in_dim(by_core, 1 - core, 1, keepdims=False)
    other = other_core(give)
    terms = up_product(
        own_kernel,
        [SCALAR, WHOLE],
        depth,
        (core.reshape(1), own),
        gate_matrix,
        up_matrix,
    )
    terms = up_product(
        other_kernel, [WHOLE], depth, (other,), gate_other, up_other, terms
    )
    place = lax.axis_index("col") // 2
    mine = lax.dynamic_index_in_dim(terms, place, 0, keepdims=False)
    arrived = lax.all_to_all(
        (terms * SCALE).astype(jnp.float16),
        "col",
        0,
        0,
        axis_index_groups=same_core,
        tiled=True,
    ).astype(jnp.float32)
    here = jnp.arange(depth)[:, None, None] == place
    theirs = jnp.sum(jnp.where(here, 0, arrived), axis=0)
    hidden = activate(theirs, mine, gate_matrix.shape[1])
    gathered = lax.all_gather(hidden, "col", axis=0, tiled=False)
    share = down_product(gathered, down_matrix)
    r = lax.axis_index("row")
    mine = lax.dynamic_index_in_dim(share, r, 0, keepdims=False).astype(jnp.float32)
    return finish(r.reshape(1), mine, lax.all_to_all(share, "row", 0, 0, tiled=True))


def solution(mesh):
    placed = (P("row", "col"), P("col", "row"), P("col", "row"), P("row", "col"))
    return jax.shard_map(
        shards, mesh=mesh, in_specs=placed, out_specs=P("row", "col"), check_vma=False
    )
```

time: 123 us -> 123 us (level)
  blocking collectives: 79.2 us -> 18.2 us
  waiting for transfers between devices: 13.8 us -> 58.9 us
  starting transfers between devices: 19.7 us -> 34.2 us
  other arithmetic: 1.87 us -> 3.47 us
    all_to_all x2 -> x0, blocking collectives: 59.6 us -> none  [the longest x1 37.4 us: shards(): lax.all_to_all(terms.astype(jnp.float16), 'col', 0, 0, axis_index_groups=...]
    all_to_all x0 -> x2, waiting for transfers between devices: none -> 46 us  [the longest x1 28.9 us: shards(): lax.all_to_all((terms * SCALE).astype(jnp.float16), 'col', 0, 0, axis_ind...]
    all_to_all x0 -> x2, starting transfers between devices: none -> 14.6 us  [the longest x1 10 us: shards(): lax.all_to_all((terms * SCALE).astype(jnp.float16), 'col', 0, 0, axis_ind...]
    all_gather x1, blocking collectives: 19.6 us -> 18.2 us  [shards(): gathered = lax.all_gather(hidden, 'col', axis=0, tiled=False)]
    pallas_call x1 -> x2, Pallas kernels: 4.4 us -> 3.02 us  [up_product(): pl.pallas_call(kernel, out_shape=pltpu.VMEM((blocks, rows, LANES), jnp.fl...]
    reduce_sum x1, other arithmetic: 0.14 us -> 1.51 us  [shards(): theirs = jnp.sum(jnp.where(here, 0, arrived), axis=0)]
  transfers between devices with their start and end apart: 4 -> 6, of which waited for: 2 -> 4; matrix products, arithmetic and copies ran while one was open for 0% -> 1% of each run, Pallas kernels for 0% -> 1%
where the time goes in v3:
time: 123 us; the launch traced here: 122 us
  waiting for transfers between devices  58.9 us (48%)
  starting transfers between devices  34.2 us (28%)
  blocking collectives  18.2 us (15%)
  Pallas kernels  6.58 us (5%)
  other arithmetic  3.47 us (3%)
    all_to_all x1, waiting for transfers between devices, shards(): lax.all_to_all((terms * SCALE).astype(jnp.float16), 'col', 0, 0, axis_ind...  28.9 us
    all_gather x1, blocking collectives, shards(): gathered = lax.all_gather(hidden, 'col', axis=0, tiled=False)  18.2 us
    all_to_all x1, waiting for transfers between devices, shards(): lax.all_to_all(share, 'row', 0, 0, tiled=True)  17.1 us
    all_to_all x1, waiting for transfers between devices, shards(): own = lax.all_to_all(spread(activations, n_row), 'row', 0, 0, tiled=True)  12.7 us
    all_to_all x1, starting transfers between devices, shards(): own = lax.all_to_all(spread(activations, n_row), 'row', 0, 0, tiled=True)  10.5 us
    all_to_all x1, starting transfers between devices, shards(): lax.all_to_all((terms * SCALE).astype(jnp.float16), 'col', 0, 0, axis_ind...  10 us
    ppermute x3, starting transfers between devices, other_core(): return lax.ppermute(x, 'col', [(i, i ^ 1) for i in range(n_col)])  9.17 us
    all_to_all x1, starting transfers between devices, shards(): lax.all_to_all(share, 'row', 0, 0, tiled=True)  4.52 us
  transfers between devices with their start and end apart: 6, of which 4 were waited for; matrix products, arithmetic and copies ran while one was open for 1% of the time, Pallas kernels for 1%

profile of v3, /device:TPU:1, one launch (start us, length us, event | category | flops | bytes accessed | tf_op | source)
XLA Modules:
  0.0 122.5 jit_solution(1347461847335928393)
XLA Ops:
  0.0 0.9 copy-done.3
  0.9 0.9 shard_map.46
  1.8 10.5 %all-to-all-start = ((bf16[32,72,128]{2,1,0:T(8,128)(2,1)}), bf16[32,72,128]{2,1,0:T(8,128)(2,1)S(1)}, u32[]{:S(2)}, u32[]{:S(2)}) async-start(bf16[32,72,128]{2,1,0:T(8,128)(2,1)} %shard_map.46), calls=%async_computation | async-start | bytes 1179648 | tf_op jit(solution)/shard_map/all_to_all | solution.py:237
  12.3 2.9 %collective-permute-start.1 = (bf16[512,896]{1,0:T(8,128)(2,1)}, bf16[512,896]{1,0:T(8,128)(2,1)S(1)}, u32[]{:S(2)}, u32[]{:S(2)}) collective-permute-start(bf16[512,896]{1,0:T(8,128)(2,1)} %gate_ref.1), channel_id=1, source_target_pairs={{0,1},{1,0},{2,3},{3,2},{4,5},{5,4},{6,7},{7,6},{8,9},{9,8},{10,11... | collective-permute-start | bytes 2752520 | tf_op jit(solution)/shard_map/ppermute | solution.py:235
  15.2 1.9 %collective-permute-start.2 = (bf16[512,896]{1,0:T(8,128)(2,1)}, bf16[512,896]{1,0:T(8,128)(2,1)}, u32[]{:S(2)}, u32[]{:S(2)}) collective-permute-start(bf16[512,896]{1,0:T(8,128)(2,1)} %up_ref.1), channel_id=1, source_target_pairs={{0,1},{1,0},{2,3},{3,2},{4,5},{5,4},{6,7},{7,6},{8,9},{9,8},{10,11... | collective-permute-start | bytes 2752520 | tf_op jit(solution)/shard_map/ppermute | solution.py:235
  17.1 12.7 %all-to-all-done.own_ref = bf16[32,72,128]{2,1,0:T(8,128)(2,1)S(1)} async-done(((bf16[32,72,128]{2,1,0:T(8,128)(2,1)}), bf16[32,72,128]{2,1,0:T(8,128)(2,1)S(1)}, u32[]{:S(2)}, u32[]{:S(2)}) %all-to-all-start) | async-done | bytes 589856 | tf_op jit(solution)/shard_map/all_to_all | solution.py:237
  29.8 4.4 %collective-permute-start = (bf16[8,2,72,128]{3,2,1,0:T(8,128)(2,1)S(1)}, bf16[8,2,72,128]{3,2,1,0:T(8,128)(2,1)S(1)}, u32[]{:S(2)}, u32[]{:S(2)}) collective-permute-start(bf16[8,2,72,128]{3,2,1,0:T(8,128)(2,1)S(1)} %dynamic-slice_bitcast_fusion), channel_id=1, source_target_pairs={{0,1},{1,0},{2,3},{3,2},{4,5},{5,4},{6,7},{7,6},{8,9},{9,8},{10,11... | collective-permute-start | bytes 884744 | tf_op jit(solution)/shard_map/ppermute | solution.py:235
  34.2 0.0 copy-done
  34.2 0.9 shard_map.47.base_ref
  35.1 0.0 collective-permute-done.1.gate_ref
  35.2 0.0 collective-permute-done.2.up_ref
  35.2 0.2 collective-permute-done.other_ref
  35.4 2.1 %shard_map.48 = f32[8,504,128]{2,1,0:T(8,128)S(1)} custom-call(bf16[8,2,72,128]{3,2,1,0:T(8,128)(2,1)S(1)} %collective-permute-done.other_ref, bf16[512,896]{1,0:T(8,128)(2,1)S(1)} %collective-permute-done.1.gate_ref, bf16[512,896]{1,0:T(8,128)(2,1)} %collective-permute-done.2.up_ref, f32[8,504,128]{2,1,0:T(8,128)S(1)} %shard_map.47.base_ref), custom_call_target="tpu_custom_call" | custom-call | tf_op jit(solution)/shard_map/pallas_call | solution.py:129
  37.5 1.2 %multiply_convert_fusion = f16[8,504,128]{2,1,0:T(8,128)(2,1)} fusion(f32[8,504,128]{2,1,0:T(8,128)S(1)} %shard_map.48), kind=kLoop, calls=%fused_computation.1 | loop fusion | flops 1032192 | bytes 3096576 | tf_op jit(solution)/shard_map/convert_element_type | solution.py:256
  38.7 10.0 %all-to-all-start.1 = ((f16[8,504,128]{2,1,0:T(8,128)(2,1)}), f16[8,504,128]{2,1,0:T(8,128)(2,1)}, u32[]{:S(2)}, u32[]{:S(2)}) async-start(f16[8,504,128]{2,1,0:T(8,128)(2,1)} %multiply_convert_fusion), calls=%async_computation.1 | async-start | bytes 2064384 | tf_op jit(solution)/shard_map/all_to_all | solution.py:255
  48.8 28.9 %all-to-all-done.1 = f16[8,504,128]{2,1,0:T(8,128)(2,1)} async-done(((f16[8,504,128]{2,1,0:T(8,128)(2,1)}), f16[8,504,128]{2,1,0:T(8,128)(2,1)}, u32[]{:S(2)}, u32[]{:S(2)}) %all-to-all-start.1) | async-done | bytes 1032224 | tf_op jit(solution)/shard_map/all_to_all | solution.py:255
  77.7 1.5 %select_reduce_fusion.theirs_ref = f32[504,128]{1,0:T(8,128)S(1)} fusion(f16[8,504,128]{2,1,0:T(8,128)(2,1)} %all-to-all-done.1, pred[8]{0:T(512)(128)(4,1)S(1)} %iota_compare_fusion), kind=kLoop, calls=%fused_computation | loop fusion | flops 1483776 | bytes 1290248 | tf_op jit(solution)/shard_map/reduce_sum | solution.py:264
  79.2 0.1 shard_map.49
  79.3 18.2 %all-gather.1.hidden_ref = bf16[16,36,896]{2,1,0:T(8,128)(2,1)S(1)} all-gather(bf16[1,36,896]{2,1,0:T(8,128)(2,1)S(1)} %bitcast.14), channel_id=2, replica_groups=mesh['row'=32,'col'=16] {'col'}, dimensions={0}, use_global_device_ids=true | all-gather | bytes 1096704 | tf_op jit(solution)/shard_map/all_gather | solution.py:266
  97.5 1.8 %shard_map.50 = bf16[32,72,128]{2,1,0:T(8,128)(2,1)} custom-call(bf16[16,36,896]{2,1,0:T(8,128)(2,1)S(1)} %all-gather.1.hidden_ref, bf16[896,512]{1,0:T(8,128)(2,1)S(1)} %copy-done.2), custom_call_target="tpu_custom_call" | custom-call | tf_op jit(solution)/shard_map/pallas_call | solution.py:195
  99.3 4.5 %all-to-all-start.2 = ((bf16[32,72,128]{2,1,0:T(8,128)(2,1)}), bf16[32,72,128]{2,1,0:T(8,128)(2,1)S(1)}, u32[]{:S(2)}, u32[]{:S(2)}) async-start(bf16[32,72,128]{2,1,0:T(8,128)(2,1)} %shard_map.50), calls=%async_computation.2 | async-start | bytes 1179648 | tf_op jit(solution)/shard_map/all_to_all | solution.py:270
  103.8 0.7 bitcast_convert_fusion.mine_ref
  104.6 17.1 %all-to-all-done.2.shares_ref = bf16[32,72,128]{2,1,0:T(8,128)(2,1)S(1)} async-done(((bf16[32,72,128]{2,1,0:T(8,128)(2,1)}), bf16[32,72,128]{2,1,0:T(8,128)(2,1)S(1)}, u32[]{:S(2)}, u32[]{:S(2)}) %all-to-all-start.2) | async-done | bytes 589856 | tf_op jit(solution)/shard_map/all_to_all | solution.py:270
  121.7 0.8 shard_map.51
  (9 shorter events, 0.1 us)
Async XLA Ops:
  0.0 34.2 %copy-start = (bf16[512,896]{1,0:T(8,128)(2,1)S(1)}, bf16[512,896]{1,0:T(8,128)(2,1)}, u32[]{:S(2)}) copy-start(bf16[512,896]{1,0:T(8,128)(2,1)} %gate_ref.1) | copy-start | bytes 2752516
  0.0 34.2 %copy-start.1 = (bf16[512,896]{1,0:T(8,128)(2,1)S(1)}, bf16[512,896]{1,0:T(8,128)(2,1)}, u32[]{:S(2)}) copy-start(bf16[512,896]{1,0:T(8,128)(2,1)} %up_ref.1) | copy-start | bytes 2752516
  0.0 0.9 copy-start.3
  1.8 28.0 %all-to-all-start = ((bf16[32,72,128]{2,1,0:T(8,128)(2,1)}), bf16[32,72,128]{2,1,0:T(8,128)(2,1)S(1)}, u32[]{:S(2)}, u32[]{:S(2)}) async-start(bf16[32,72,128]{2,1,0:T(8,128)(2,1)} %shard_map.46), calls=%async_computation | async-start | bytes 1179648 | tf_op jit(solution)/shard_map/all_to_all | solution.py:237
  12.3 22.9 %collective-permute-start.1 = (bf16[512,896]{1,0:T(8,128)(2,1)}, bf16[512,896]{1,0:T(8,128)(2,1)S(1)}, u32[]{:S(2)}, u32[]{:S(2)}) collective-permute-start(bf16[512,896]{1,0:T(8,128)(2,1)} %gate_ref.1), channel_id=1, source_target_pairs={{0,1},{1,0},{2,3},{3,2},{4,5},{5,4},{6,7},{7,6},{8,9},{9,8},{10,11... | collective-permute-start | bytes 2752520 | tf_op jit(solution)/shard_map/ppermute | solution.py:235
  15.2 20.0 %collective-permute-start.2 = (bf16[512,896]{1,0:T(8,128)(2,1)}, bf16[512,896]{1,0:T(8,128)(2,1)}, u32[]{:S(2)}, u32[]{:S(2)}) collective-permute-start(bf16[512,896]{1,0:T(8,128)(2,1)} %up_ref.1), channel_id=1, source_target_pairs={{0,1},{1,0},{2,3},{3,2},{4,5},{5,4},{6,7},{7,6},{8,9},{9,8},{10,11... | collective-permute-start | bytes 2752520 | tf_op jit(solution)/shard_map/ppermute | solution.py:235
  29.8 5.6 %collective-permute-start = (bf16[8,2,72,128]{3,2,1,0:T(8,128)(2,1)S(1)}, bf16[8,2,72,128]{3,2,1,0:T(8,128)(2,1)S(1)}, u32[]{:S(2)}, u32[]{:S(2)}) collective-permute-start(bf16[8,2,72,128]{3,2,1,0:T(8,128)(2,1)S(1)} %dynamic-slice_bitcast_fusion), channel_id=1, source_target_pairs={{0,1},{1,0},{2,3},{3,2},{4,5},{5,4},{6,7},{7,6},{8,9},{9,8},{10,11... | collective-permute-start | bytes 884744 | tf_op jit(solution)/shard_map/ppermute | solution.py:235
  38.7 39.0 %all-to-all-start.1 = ((f16[8,504,128]{2,1,0:T(8,128)(2,1)}), f16[8,504,128]{2,1,0:T(8,128)(2,1)}, u32[]{:S(2)}, u32[]{:S(2)}) async-start(f16[8,504,128]{2,1,0:T(8,128)(2,1)} %multiply_convert_fusion), calls=%async_computation.1 | async-start | bytes 2064384 | tf_op jit(solution)/shard_map/all_to_all | solution.py:255
  48.7 48.7 %copy-start.2 = (bf16[896,512]{1,0:T(8,128)(2,1)S(1)}, bf16[896,512]{1,0:T(8,128)(2,1)}, u32[]{:S(2)}) copy-start(bf16[896,512]{1,0:T(8,128)(2,1)} %weight_ref.1) | copy-start | bytes 2752516
  99.3 22.4 %all-to-all-start.2 = ((bf16[32,72,128]{2,1,0:T(8,128)(2,1)}), bf16[32,72,128]{2,1,0:T(8,128)(2,1)S(1)}, u32[]{:S(2)}, u32[]{:S(2)}) async-start(bf16[32,72,128]{2,1,0:T(8,128)(2,1)} %shard_map.50), calls=%async_computation.2 | async-start | bytes 1179648 | tf_op jit(solution)/shard_map/all_to_all | solution.py:270

commit v4 on v3

--- a/solution.py
+++ b/solution.py
@@ -12,10 +12,12 @@
 EXTRA = 2
 PAIR = 2
 STRIDE = 48
-LIMIT = pltpu.CompilerParams(vmem_limit_bytes=24 * 1024 * 1024)
+LIMIT = pltpu.CompilerParams(vmem_limit_bytes=8 * 1024 * 1024)
 SCALAR = pl.BlockSpec(memory_space=pltpu.SMEM)
 WHOLE = pl.BlockSpec(memory_space=pltpu.VMEM)
 SCALE = 16.0
+ROW, COL = ("y", "x"), ("z", "core")
+ALONG_X = 4
 
 
 def lanes(q):
@@ -136,9 +138,9 @@
     )(*operands, gate, up, *base)
 
 
-def activate_kernel(theirs_ref, mine_ref, out_ref):
+def activate_kernel(sum_ref, out_ref):
     def total(rows):
-        return theirs_ref[rows, :] * (1 / SCALE) + mine_ref[rows, :]
+        return sum_ref[rows, :] * (1 / SCALE)
 
     span = PAIR * MAIN
     wide_tiles = out_ref.shape[1] // LANES
@@ -154,16 +156,16 @@
         out_ref[span:, lanes(j)] = tail[: PAIR * EXTRA].astype(jnp.bfloat16)
 
 
-def activate(theirs, mine, hidden_width):
+def activate(total, hidden_width):
     return pl.pallas_call(
         activate_kernel,
         out_shape=jax.ShapeDtypeStruct(
             (PAIR * (MAIN + EXTRA), hidden_width), jnp.bfloat16
         ),
-        in_specs=[WHOLE] * 2,
-        out_specs=WHOLE,
-        compiler_params=LIMIT,
-    )(theirs, mine)
+        in_specs=[WHOLE],
+        out_specs=WHOLE,
+        compiler_params=LIMIT,
+    )(total)
 
 
 def down_kernel(hidden_ref, weight_ref, out_ref, held):
@@ -202,39 +204,36 @@
     )(hidden, weight)
 
 
-def finish_kernel(me_ref, mine_ref, shares_ref, out_ref):
+def finish_kernel(shares_ref, out_ref):
     tiles = out_ref.shape[1] // LANES
-    total = mine_ref[...]
-    for r in range(shares_ref.shape[0]):
-        share = shares_ref[r].astype(jnp.float32)
-        total += jnp.where(r == me_ref[0], 0.0, share)
+    total = shares_ref[0].astype(jnp.float32)
+    for r in range(1, shares_ref.shape[0]):
+        total += shares_ref[r].astype(jnp.float32)
     for q in range(tiles):
         out_ref[:MAIN, lanes(q)] = total[rows_of(q, MAIN)].astype(jnp.bfloat16)
         tail = total[tiles * MAIN + q * EXTRA : tiles * MAIN + (q + 1) * EXTRA]
         out_ref[MAIN:, lanes(q)] = tail.astype(jnp.bfloat16)
 
 
-def finish(me, mine, shares):
+def finish(shares):
     width = shares.shape[1] // (MAIN + EXTRA) * LANES
     return pl.pallas_call(
         finish_kernel,
         out_shape=jax.ShapeDtypeStruct((MAIN + EXTRA, width), jnp.bfloat16),
-        in_specs=[SCALAR, WHOLE, WHOLE],
-        out_specs=WHOLE,
-        compiler_params=LIMIT,
-    )(me, mine, shares)
+        in_specs=[WHOLE],
+        out_specs=WHOLE,
+        compiler_params=LIMIT,
+    )(shares)
 
 
 def shards(activations, gate_matrix, up_matrix, down_matrix):
-    n_row, n_col = lax.axis_size("row"), lax.axis_size("col")
-    depth = n_col // 2
-    core = lax.axis_index("col") % 2
-    same_core = [[2 * i + k for i in range(depth)] for k in range(2)]
+    n_row, depth = lax.axis_size(ROW), lax.axis_size("z")
+    core = lax.axis_index("core")
 
     def other_core(x):
-        return lax.ppermute(x, "col", [(i, i ^ 1) for i in range(n_col)])
-
-    own = lax.all_to_all(spread(activations, n_row), "row", 0, 0, tiled=True)
+        return lax.ppermute(x, "core", [(0, 1), (1, 0)])
+
+    own = lax.all_to_all(spread(activations, n_row), ROW, 0, 0, tiled=True)
     gate_other, up_other = other_core(gate_matrix), other_core(up_matrix)
     by_core = own.reshape(depth, 2, PAIR, *own.shape[1:])
     give = lax.dynamic_index_in_dim(by_core, 1 - core, 1, keepdims=False)
@@ -250,28 +249,21 @@
     terms = up_product(
         other_kernel, [WHOLE], depth, (other,), gate_other, up_other, terms
     )
-    place = lax.axis_index("col") // 2
-    mine = lax.dynamic_index_in_dim(terms, place, 0, keepdims=False)
     arrived = lax.all_to_all(
-        (terms * SCALE).astype(jnp.float16),
-        "col",
-        0,
-        0,
-        axis_index_groups=same_core,
-        tiled=True,
-    ).astype(jnp.float32)
-    here = jnp.arange(depth)[:, None, None] == place
-    theirs = jnp.sum(jnp.where(here, 0, arrived), axis=0)
-    hidden = activate(theirs, mine, gate_matrix.shape[1])
-    gathered = lax.all_gather(hidden, "col", axis=0, tiled=False)
+        (terms * SCALE).astype(jnp.float16), "z", 0, 0, tiled=True
+    )
+    total = jnp.sum(arrived.astype(jnp.float32), axis=0)
+    hidden = activate(total, gate_matrix.shape[1])
+    gathered = lax.all_gather(hidden, COL, axis=0, tiled=False)
     share = down_product(gathered, down_matrix)
-    r = lax.axis_index("row")
-    mine = lax.dynamic_index_in_dim(share, r, 0, keepdims=False).astype(jnp.float32)
-    return finish(r.reshape(1), mine, lax.all_to_all(share, "row", 0, 0, tiled=True))
+    return finish(lax.all_to_all(share, ROW, 0, 0, tiled=True))
 
 
 def solution(mesh):
-    placed = (P("row", "col"), P("col", "row"), P("col", "row"), P("row", "col"))
+    n_row, n_col = mesh.devices.shape
+    devices = mesh.devices.reshape(n_row // ALONG_X, ALONG_X, n_col // 2, 2)
+    chips = jax.sharding.Mesh(devices, ROW + COL)
+    placed = (P(ROW, COL), P(COL, ROW), P(COL, ROW), P(ROW, COL))
     return jax.shard_map(
-        shards, mesh=mesh, in_specs=placed, out_specs=P("row", "col"), check_vma=False
-    )
+        shards, mesh=chips, in_specs=placed, out_specs=P(ROW, COL), check_vma=False
+    )

time: 123 us -> 119 us (0.967)
  blocking collectives: 18.2 us -> 79.2 us
  waiting for transfers between devices: 58.9 us -> 12.9 us
  starting transfers between devices: 34.2 us -> 19.7 us
  other arithmetic: 3.47 us -> 0.35 us
    all_to_all x0 -> x2, blocking collectives: none -> 59.7 us  [the longest x1 37.5 us: shards(): lax.all_to_all((terms * SCALE).astype(jnp.float16), 'z', 0, 0, tiled=True)]
    all_to_all x3 -> x1, waiting for transfers between devices: 58.7 us -> 12.7 us  [shards(): own = lax.all_to_all(spread(activations, n_row), ROW, 0, 0, tiled=True)]
    all_to_all x3 -> x1, starting transfers between devices: 25.1 us -> 10.5 us  [shards(): own = lax.all_to_all(spread(activations, n_row), ROW, 0, 0, tiled=True)]
    reduce_sum x1, other arithmetic: 1.51 us -> 0.14 us  [shards(): total = jnp.sum(arrived.astype(jnp.float32), axis=0)]
    all_gather x1, blocking collectives: 18.2 us -> 19.5 us  [shards(): gathered = lax.all_gather(hidden, COL, axis=0, tiled=False)]
  transfers between devices with their start and end apart: 6 -> 4, of which waited for: 4 -> 2; matrix products, arithmetic and copies ran while one was open for 1% -> 0% of each run, Pallas kernels for 1% -> 1%
where the time goes in v4:
time: 119 us
  blocking collectives  79.2 us (67%)
  starting transfers between devices  19.7 us (17%)
  waiting for transfers between devices  12.9 us (11%)
  Pallas kernels  5.69 us (5%)
    all_to_all x1, blocking collectives, shards(): lax.all_to_all((terms * SCALE).astype(jnp.float16), 'z', 0, 0, tiled=True)  37.5 us
    all_to_all x1, blocking collectives, shards(): return finish(lax.all_to_all(share, ROW, 0, 0, tiled=True))  22.2 us
    all_gather x1, blocking collectives, shards(): gathered = lax.all_gather(hidden, COL, axis=0, tiled=False)  19.5 us
    all_to_all x1, waiting for transfers between devices, shards(): own = lax.all_to_all(spread(activations, n_row), ROW, 0, 0, tiled=True)  12.7 us
    all_to_all x1, starting transfers between devices, shards(): own = lax.all_to_all(spread(activations, n_row), ROW, 0, 0, tiled=True)  10.5 us
    ppermute x3, starting transfers between devices, other_core(): return lax.ppermute(x, 'core', [(0, 1), (1, 0)])  9.17 us
    pallas_call x2, Pallas kernels, up_product(): pl.pallas_call(kernel, out_shape=pltpu.VMEM((blocks, rows, LANES), jnp.fl...  3.02 us
  transfers between devices with their start and end apart: 4, of which 2 were waited for; matrix products, arithmetic and copies ran while one was open for 0% of the time, Pallas kernels for 1%

profile of v4, /device:TPU:1, one launch (start us, length us, event | category | flops | bytes accessed | tf_op | source)
XLA Modules:
  0.0 118.8 jit_solution(2631937652385819781)
XLA Ops:
  0.0 0.9 copy-done.3
  0.9 0.9 shard_map.46
  1.8 10.5 %all-to-all-start = ((bf16[32,72,128]{2,1,0:T(8,128)(2,1)}), bf16[32,72,128]{2,1,0:T(8,128)(2,1)S(1)}, u32[]{:S(2)}, u32[]{:S(2)}) async-start(bf16[32,72,128]{2,1,0:T(8,128)(2,1)} %shard_map.46), calls=%async_computation | async-start | bytes 1179648 | tf_op jit(solution)/shard_map/all_to_all | solution.py:236
  12.3 2.9 %collective-permute-start.1 = (bf16[512,896]{1,0:T(8,128)(2,1)}, bf16[512,896]{1,0:T(8,128)(2,1)S(1)}, u32[]{:S(2)}, u32[]{:S(2)}) collective-permute-start(bf16[512,896]{1,0:T(8,128)(2,1)} %gate_ref.1), channel_id=1, source_target_pairs={{0,1},{1,0},{2,3},{3,2},{4,5},{5,4},{6,7},{7,6},{8,9},{9,8},{10,11... | collective-permute-start | bytes 2752520 | tf_op jit(solution)/shard_map/ppermute | solution.py:234
  15.2 1.9 %collective-permute-start.2 = (bf16[512,896]{1,0:T(8,128)(2,1)}, bf16[512,896]{1,0:T(8,128)(2,1)}, u32[]{:S(2)}, u32[]{:S(2)}) collective-permute-start(bf16[512,896]{1,0:T(8,128)(2,1)} %up_ref.1), channel_id=1, source_target_pairs={{0,1},{1,0},{2,3},{3,2},{4,5},{5,4},{6,7},{7,6},{8,9},{9,8},{10,11... | collective-permute-start | bytes 2752520 | tf_op jit(solution)/shard_map/ppermute | solution.py:234
  17.1 12.7 %all-to-all-done.own_ref = bf16[32,72,128]{2,1,0:T(8,128)(2,1)S(1)} async-done(((bf16[32,72,128]{2,1,0:T(8,128)(2,1)}), bf16[32,72,128]{2,1,0:T(8,128)(2,1)S(1)}, u32[]{:S(2)}, u32[]{:S(2)}) %all-to-all-start) | async-done | bytes 589856 | tf_op jit(solution)/shard_map/all_to_all | solution.py:236
  29.8 4.4 %collective-permute-start = (bf16[8,2,72,128]{3,2,1,0:T(8,128)(2,1)S(1)}, bf16[8,2,72,128]{3,2,1,0:T(8,128)(2,1)S(1)}, u32[]{:S(2)}, u32[]{:S(2)}) collective-permute-start(bf16[8,2,72,128]{3,2,1,0:T(8,128)(2,1)S(1)} %dynamic-slice_bitcast_fusion), channel_id=1, source_target_pairs={{0,1},{1,0},{2,3},{3,2},{4,5},{5,4},{6,7},{7,6},{8,9},{9,8},{10,11... | collective-permute-start | bytes 884744 | tf_op jit(solution)/shard_map/ppermute | solution.py:234
  34.2 0.0 copy-done
  34.2 0.0 copy-done.1
  34.2 0.9 shard_map.47.base_ref
  35.1 0.0 collective-permute-done.1.gate_ref
  35.2 0.0 collective-permute-done.2.up_ref
  35.2 0.2 collective-permute-done.other_ref
  35.4 2.1 %shard_map.48 = f32[8,504,128]{2,1,0:T(8,128)S(1)} custom-call(bf16[8,2,72,128]{3,2,1,0:T(8,128)(2,1)S(1)} %collective-permute-done.other_ref, bf16[512,896]{1,0:T(8,128)(2,1)S(1)} %collective-permute-done.1.gate_ref, bf16[512,896]{1,0:T(8,128)(2,1)} %collective-permute-done.2.up_ref, f32[8,504,128]{2,1,0:T(8,128)S(1)} %shard_map.47.base_ref), custom_call_target="tpu_custom_call" | custom-call | tf_op jit(solution)/shard_map/pallas_call | solution.py:131
  37.5 0.2 multiply_convert_fusion
  37.7 0.0 copy-start.2
  37.7 37.5 %all_to_all.15 = f16[8,504,128]{2,1,0:T(8,128)(2,1)S(1)} all-to-all(f16[8,504,128]{2,1,0:T(8,128)(2,1)S(1)} %multiply_convert_fusion), channel_id=1, replica_groups=mesh['y'=8,'x'=4,'z'=8,'core'=2] {'z'}, dimensions={0} | all-to-all | bytes 2064384 | tf_op jit(solution)/shard_map/all_to_all | solution.py:252
  75.2 0.1 convert_reduce_fusion.sum_ref
  75.4 0.1 shard_map.49
  75.4 19.5 %all-gather.1.hidden_ref = bf16[16,36,896]{2,1,0:T(8,128)(2,1)S(1)} all-gather(bf16[1,36,896]{2,1,0:T(8,128)(2,1)S(1)} %bitcast.8), channel_id=2, replica_groups=mesh['y'=8,'x'=4,'z'=8,'core'=2] {'z','core'}, dimensions={0}, use_global_device_ids=true | all-gather | bytes 1096704 | tf_op jit(solution)/shard_map/all_gather | solution.py:257
  94.9 0.0 copy-done.2
  94.9 1.0 shard_map.50
  95.9 22.2 %all_to_all.16.shares_ref = bf16[32,72,128]{2,1,0:T(8,128)(2,1)S(1)} all-to-all(bf16[32,72,128]{2,1,0:T(8,128)(2,1)S(1)} %shard_map.50), channel_id=1, replica_groups=mesh['y'=8,'x'=4,'z'=8,'core'=2] {'y','x'}, dimensions={0} | all-to-all | bytes 1179648 | tf_op jit(solution)/shard_map/all_to_all | solution.py:259
  118.1 0.7 shard_map.51
  (4 shorter events, 0.0 us)
Async XLA Ops:
  0.0 34.2 %copy-start = (bf16[512,896]{1,0:T(8,128)(2,1)S(1)}, bf16[512,896]{1,0:T(8,128)(2,1)}, u32[]{:S(2)}) copy-start(bf16[512,896]{1,0:T(8,128)(2,1)} %gate_ref.1) | copy-start | bytes 2752516
  0.0 34.2 %copy-start.1 = (bf16[512,896]{1,0:T(8,128)(2,1)S(1)}, bf16[512,896]{1,0:T(8,128)(2,1)}, u32[]{:S(2)}) copy-start(bf16[512,896]{1,0:T(8,128)(2,1)} %up_ref.1) | copy-start | bytes 2752516
  0.0 0.9 copy-start.3
  1.8 28.0 %all-to-all-start = ((bf16[32,72,128]{2,1,0:T(8,128)(2,1)}), bf16[32,72,128]{2,1,0:T(8,128)(2,1)S(1)}, u32[]{:S(2)}, u32[]{:S(2)}) async-start(bf16[32,72,128]{2,1,0:T(8,128)(2,1)} %shard_map.46), calls=%async_computation | async-start | bytes 1179648 | tf_op jit(solution)/shard_map/all_to_all | solution.py:236
  12.3 22.9 %collective-permute-start.1 = (bf16[512,896]{1,0:T(8,128)(2,1)}, bf16[512,896]{1,0:T(8,128)(2,1)S(1)}, u32[]{:S(2)}, u32[]{:S(2)}) collective-permute-start(bf16[512,896]{1,0:T(8,128)(2,1)} %gate_ref.1), channel_id=1, source_target_pairs={{0,1},{1,0},{2,3},{3,2},{4,5},{5,4},{6,7},{7,6},{8,9},{9,8},{10,11... | collective-permute-start | bytes 2752520 | tf_op jit(solution)/shard_map/ppermute | solution.py:234
  15.2 20.0 %collective-permute-start.2 = (bf16[512,896]{1,0:T(8,128)(2,1)}, bf16[512,896]{1,0:T(8,128)(2,1)}, u32[]{:S(2)}, u32[]{:S(2)}) collective-permute-start(bf16[512,896]{1,0:T(8,128)(2,1)} %up_ref.1), channel_id=1, source_target_pairs={{0,1},{1,0},{2,3},{3,2},{4,5},{5,4},{6,7},{7,6},{8,9},{9,8},{10,11... | collective-permute-start | bytes 2752520 | tf_op jit(solution)/shard_map/ppermute | solution.py:234
  29.8 5.6 %collective-permute-start = (bf16[8,2,72,128]{3,2,1,0:T(8,128)(2,1)S(1)}, bf16[8,2,72,128]{3,2,1,0:T(8,128)(2,1)S(1)}, u32[]{:S(2)}, u32[]{:S(2)}) collective-permute-start(bf16[8,2,72,128]{3,2,1,0:T(8,128)(2,1)S(1)} %dynamic-slice_bitcast_fusion), channel_id=1, source_target_pairs={{0,1},{1,0},{2,3},{3,2},{4,5},{5,4},{6,7},{7,6},{8,9},{9,8},{10,11... | collective-permute-start | bytes 884744 | tf_op jit(solution)/shard_map/ppermute | solution.py:234
  37.7 57.2 %copy-start.2 = (bf16[896,512]{1,0:T(8,128)(2,1)S(1)}, bf16[896,512]{1,0:T(8,128)(2,1)}, u32[]{:S(2)}) copy-start(bf16[896,512]{1,0:T(8,128)(2,1)} %weight_ref.1) | copy-start | bytes 2752516

commit v5 on v4

v5 whole, which is shorter than its diff:
```python
import functools

import jax
import jax.numpy as jnp
from jax import lax
from jax.experimental import pallas as pl
from jax.experimental.pallas import tpu as pltpu
from jax.sharding import PartitionSpec as P

LANES = 128
MAIN = 16
EXTRA = 2
PAIR = 2
LIMIT = pltpu.CompilerParams(vmem_limit_bytes=8 * 1024 * 1024)
SCALAR = pl.BlockSpec(memory_space=pltpu.SMEM)
WHOLE = pl.BlockSpec(memory_space=pltpu.VMEM)
SCALE = 16.0
ROW, COL = ("y", "far", "pair"), ("z", "core")
ALONG_X = 4


def lanes(q):
    return slice(q * LANES, (q + 1) * LANES)


def rows_of(q, count):
    return slice(q * count, (q + 1) * count)


def gather_extra(tiles, shift_of):
    row = lax.broadcasted_iota(jnp.int32, tiles[0].shape, 0) // EXTRA
    out = tiles[0] if shift_of(0) % 8 == 0 else pltpu.roll(tiles[0], shift_of(0) % 8, 0)
    for q in range(1, len(tiles)):
        moved = tiles[q]
        if shift_of(q) % 8:
            moved = pltpu.roll(moved, shift_of(q) % 8, 0)
        out = jnp.where(row == q, moved, out)
    return out


def spread_kernel(x_ref, out_ref):
    x = x_ref[...].astype(jnp.float32)
    tiles = x.shape[1] // LANES
    for q in range(tiles):
        for r in range(out_ref.shape[0]):
            out_ref[r, rows_of(q, MAIN), :] = x_ref[:MAIN, lanes(q)]
    tail = jnp.concatenate(
        [x[MAIN:, lanes(q)] for q in range(tiles)], axis=0
    ).astype(jnp.bfloat16)
    for r in range(out_ref.shape[0]):
        out_ref[r, tiles * MAIN :, :] = tail


def spread(x, copies):
    rows = x.shape[0] * x.shape[1] // LANES
    return pl.pallas_call(
        spread_kernel,
        out_shape=jax.ShapeDtypeStruct((copies, rows, LANES), x.dtype),
        in_specs=[WHOLE],
        out_specs=WHOLE,
        compiler_params=LIMIT,
    )(x)


def add_product(source_at, gate_ref, up_ref, base_ref, out_ref, held):
    sources = out_ref.shape[0]
    tiles = held.shape[1] // LANES
    wide_tiles = gate_ref.shape[1] // LANES
    main = sources * MAIN
    shape = (tiles * sources * 8, sources * 8)
    r = lax.broadcasted_iota(jnp.int32, shape, 0)
    c = lax.broadcasted_iota(jnp.int32, shape, 1)
    place = c == r // 8 % sources * 8 + r // (sources * 8) * EXTRA + r % EXTRA
    tails = []
    for n in range(sources):
        block = source_at(n)
        for q in range(tiles):
            held[rows_of(n, MAIN), lanes(q)] = block[rows_of(q, MAIN)]
        tails.append(block[tiles * MAIN :])
    moved = jnp.dot(
        place.astype(jnp.bfloat16),
        jnp.concatenate(tails, axis=0),
        preferred_element_type=jnp.float32,
    ).astype(jnp.bfloat16)
    for q in range(tiles):
        held[main:, lanes(q)] = moved[rows_of(q, sources * 8)]
    row = lax.broadcasted_iota(jnp.int32, (8, LANES), 0) // EXTRA
    x = held[...]
    for first in range(0, wide_tiles, 2):
        count = min(2, wide_tiles - first)
        columns = slice(first * LANES, (first + count) * LANES)
        gate = jnp.dot(x, gate_ref[:, columns], preferred_element_type=jnp.float32)
        up = jnp.dot(x, up_ref[:, columns], preferred_element_type=jnp.float32)
        for n in range(sources):
            end = slice(main + n * 8, main + n * 8 + 8)
            mixed = jnp.where(row == 0, gate[end, lanes(0)], gate[end, lanes(count - 1)])
            mixed = jnp.where(row == 2, up[end, lanes(0)], mixed)
            mixed = jnp.where(row == 3, up[end, lanes(count - 1)], mixed)
            start = 2 * wide_tiles * MAIN + 4 * first
            parts = [(slice(start, start + 8), mixed)]
            for i in range(count):
                at = rows_of(n, MAIN)
                parts.append((rows_of(first + i, MAIN), gate[at, lanes(i)]))
                parts.append((rows_of(wide_tiles + first + i, MAIN), up[at, lanes(i)]))
            for where, value in parts:
                if base_ref is not None:
                    value += base_ref[n, where, :]
                out_ref[n, where, :] = value


def own_kernel(core_ref, own_ref, gate_ref, up_ref, out_ref, held):
    depth = out_ref.shape[0] // PAIR

    def source_at(n):
        return own_ref[n % depth * 2 * PAIR + core_ref[0] * PAIR + n // depth]

    add_product(source_at, gate_ref, up_ref, None, out_ref, held)


def other_kernel(other_ref, gate_ref, up_ref, base_ref, out_ref, held):
    depth = out_ref.shape[0] // PAIR

    def source_at(n):
        return other_ref[n % depth, n // depth]

    add_product(source_at, gate_ref, up_ref, base_ref, out_ref, held)


def up_product(kernel, specs, sources, operands, gate, up, *base):
    wide_tiles = gate.shape[1] // LANES
    rows = 2 * wide_tiles * MAIN + (wide_tiles + 1) // 2 * 8
    held = pltpu.VMEM((sources * (MAIN + 8), gate.shape[0]), jnp.bfloat16)
    return pl.pallas_call(
        kernel,
        out_shape=pltpu.VMEM((sources, rows, LANES), jnp.float32),
        in_specs=specs + [WHOLE] * (2 + len(base)),
        out_specs=WHOLE,
        scratch_shapes=[held],
        compiler_params=LIMIT,
    )(*operands, gate, up, *base)


def activate_kernel(sum_ref, out_ref):
    wide_tiles = out_ref.shape[1] // LANES

    def total(p, rows):
        return sum_ref[p, rows, :] * (1 / SCALE)

    for p in range(PAIR):
        tail_rows = slice(PAIR * MAIN + p * EXTRA, PAIR * MAIN + (p + 1) * EXTRA)
        for j in range(wide_tiles):
            gate = total(p, rows_of(j, MAIN))
            up = total(p, rows_of(wide_tiles + j, MAIN))
            out_ref[rows_of(p, MAIN), lanes(j)] = (
                gate / (1 + jnp.exp(-gate)) * up
            ).astype(jnp.bfloat16)
        for first in range(0, wide_tiles, 2):
            start = 2 * wide_tiles * MAIN + 4 * first
            mixed = total(p, slice(start, start + 8))
            tail = mixed / (1 + jnp.exp(-mixed)) * pltpu.roll(mixed, 2 * EXTRA, 0)
            tail = tail.astype(jnp.bfloat16)
            for i in range(min(2, wide_tiles - first)):
                out_ref[tail_rows, lanes(first + i)] = tail[rows_of(i, EXTRA)]


def activate(total, hidden_width):
    return pl.pallas_call(
        activate_kernel,
        out_shape=jax.ShapeDtypeStruct(
            (PAIR * (MAIN + EXTRA), hidden_width), jnp.bfloat16
        ),
        in_specs=[WHOLE],
        out_specs=WHOLE,
        compiler_params=LIMIT,
    )(total)


def down_kernel(pair_ref, hidden_ref, own_ref, other_ref, out_ref, own, other):
    sources = hidden_ref.shape[0]
    main = sources * MAIN
    first = pair_ref[0] == 0
    for n in range(sources):
        a, b = hidden_ref[n, :MAIN], hidden_ref[n, MAIN : PAIR * MAIN]
        own[rows_of(n, MAIN), :] = jnp.where(first, a, b)
        other[rows_of(n, MAIN), :] = jnp.where(first, b, a)
        tail = hidden_ref[n, PAIR * MAIN :]
        at = slice(main + n * 8, main + n * 8 + PAIR * EXTRA)
        own[at, :] = tail
        other[at, :] = tail
    tiles = own_ref.shape[1] // LANES
    mine = jnp.dot(own[...], own_ref[...], preferred_element_type=jnp.float32)
    theirs = jnp.dot(other[...], other_ref[...], preferred_element_type=jnp.float32)
    for n in range(sources):
        at, end = rows_of(n, MAIN), slice(main + n * 8, main + n * 8 + 8)
        tails = []
        for q in range(tiles):
            out_ref[n, rows_of(q, MAIN), :] = (
                mine[at, lanes(q)] + theirs[at, lanes(q)]
            ).astype(jnp.bfloat16)
            a, b = mine[end, lanes(q)], theirs[end, lanes(q)]
            later = pltpu.roll(jnp.where(first, b, a), 8 - EXTRA, 0)
            tails.append(jnp.where(first, a, b) + later)
        tail = gather_extra(tails, lambda q: q * EXTRA)
        out_ref[n, tiles * MAIN :, :] = tail.astype(jnp.bfloat16)


def down_product(pair, hidden, weight, other_weight):
    sources, count, width = hidden.shape
    rows = (MAIN + EXTRA) * weight.shape[1] // LANES
    held = pltpu.VMEM((sources * (MAIN + 8), width), jnp.bfloat16)
    return pl.pallas_call(
        down_kernel,
        out_shape=jax.ShapeDtypeStruct((sources, rows, LANES), jnp.bfloat16),
        in_specs=[SCALAR] + [WHOLE] * 3,
        out_specs=WHOLE,
        scratch_shapes=[held, held],
        compiler_params=LIMIT,
    )(pair, hidden, weight, other_weight)


def finish_kernel(shares_ref, out_ref):
    tiles = out_ref.shape[1] // LANES
    total = shares_ref[0].astype(jnp.float32)
    for r in range(1, shares_ref.shape[0]):
        total += shares_ref[r].astype(jnp.float32)
    for q in range(tiles):
        out_ref[:MAIN, lanes(q)] = total[rows_of(q, MAIN)].astype(jnp.bfloat16)
        tail = total[tiles * MAIN + q * EXTRA : tiles * MAIN + (q + 1) * EXTRA]
        out_ref[MAIN:, lanes(q)] = tail.astype(jnp.bfloat16)


def finish(shares):
    width = shares.shape[1] // (MAIN + EXTRA) * LANES
    return pl.pallas_call(
        finish_kernel,
        out_shape=jax.ShapeDtypeStruct((MAIN + EXTRA, width), jnp.bfloat16),
        in_specs=[WHOLE],
        out_specs=WHOLE,
        compiler_params=LIMIT,
    )(shares)


def shards(activations, gate_matrix, up_matrix, down_matrix):
    n_row, depth = lax.axis_size(ROW), lax.axis_size("z")
    core, pair = lax.axis_index("core"), lax.axis_index("pair")

    def swap(x, axis):
        return lax.ppermute(x, axis, [(0, 1), (1, 0)])

    own = lax.all_to_all(spread(activations, n_row), ROW, 0, 0, tiled=True)
    gate_other, up_other = swap(gate_matrix, "core"), swap(up_matrix, "core")
    down_other = swap(down_matrix, "pair")
    by_core = own.reshape(depth, 2, PAIR, *own.shape[1:])
    give = lax.dynamic_index_in_dim(by_core, 1 - core, 1, keepdims=False)
    other = swap(give, "core")
    sources = PAIR * depth
    terms = up_product(
        own_kernel,
        [SCALAR, WHOLE],
        sources,
        (core.reshape(1), own),
        gate_matrix,
        up_matrix,
    )
    terms = up_product(
        other_kernel, [WHOLE], sources, (other,), gate_other, up_other, terms
    )
    arrived = lax.all_to_all(
        (terms * SCALE).astype(jnp.float16), ("pair", "z"), 0, 0, tiled=True
    )
    arrived = arrived.reshape(PAIR, depth, *arrived.shape[1:])
    total = jnp.sum(arrived.astype(jnp.float32), axis=1)
    hidden = activate(total, gate_matrix.shape[1])
    gathered = lax.all_gather(hidden, COL, axis=0, tiled=False)
    share = down_product(pair.reshape(1), gathered, down_matrix, down_other)
    return finish(lax.all_to_all(share, ("y", "far"), 0, 0, tiled=True))


def solution(mesh):
    n_row, n_col = mesh.devices.shape
    far = ALONG_X // PAIR
    devices = mesh.devices.reshape(n_row // ALONG_X, far, PAIR, n_col // 2, 2)
    chips = jax.sharding.Mesh(devices, ROW + COL)
    placed = (P(ROW, COL), P(COL, ROW), P(COL, ROW), P(ROW, COL))
    return jax.shard_map(
        shards, mesh=chips, in_specs=placed, out_specs=P(ROW, COL), check_vma=False
    )
```

time: 119 us -> 115 us (0.966)
  blocking collectives: 79.2 us -> 37.9 us
  waiting for transfers between devices: 12.9 us -> 35 us
  starting transfers between devices: 19.7 us -> 33.5 us
    all_to_all x2 -> x1, blocking collectives: 59.7 us -> 17.1 us  [shards(): return finish(lax.all_to_all(share, ('y', 'far'), 0, 0, tiled=True))]
    all_to_all x0 -> x1, waiting for transfers between devices: none -> 22.2 us  [shards(): lax.all_to_all((terms * SCALE).astype(jnp.float16), ('pair', 'z'), 0, 0,...]
    all_to_all x0 -> x1, starting transfers between devices: none -> 10.6 us  [shards(): lax.all_to_all((terms * SCALE).astype(jnp.float16), ('pair', 'z'), 0, 0,...]
    ppermute x3 -> x4, starting transfers between devices: 9.17 us -> 12.4 us  [swap(): return lax.ppermute(x, axis, [(0, 1), (1, 0)])]
    all_gather x1, blocking collectives: 19.5 us -> 20.8 us  [shards(): gathered = lax.all_gather(hidden, COL, axis=0, tiled=False)]
  transfers between devices with their start and end apart: 4 -> 6, of which waited for: 2 -> 3; matrix products, arithmetic and copies ran while one was open for 0% -> 0% of each run, Pallas kernels for 1% -> 1%
where the time goes in v5:
time: 115 us
  blocking collectives  37.9 us (33%)
  waiting for transfers between devices  35 us (30%)
  starting transfers between devices  33.5 us (29%)
  Pallas kernels  5.92 us (5%)
  other arithmetic  1.44 us (1%)
    all_to_all x1, waiting for transfers between devices, shards(): lax.all_to_all((terms * SCALE).astype(jnp.float16), ('pair', 'z'), 0, 0,...  22.2 us
    all_gather x1, blocking collectives, shards(): gathered = lax.all_gather(hidden, COL, axis=0, tiled=False)  20.8 us
    all_to_all x1, blocking collectives, shards(): return finish(lax.all_to_all(share, ('y', 'far'), 0, 0, tiled=True))  17.1 us
    all_to_all x1, waiting for transfers between devices, shards(): own = lax.all_to_all(spread(activations, n_row), ROW, 0, 0, tiled=True)  12.7 us
    ppermute x4, starting transfers between devices, swap(): return lax.ppermute(x, axis, [(0, 1), (1, 0)])  12.4 us
    all_to_all x1, starting transfers between devices, shards(): lax.all_to_all((terms * SCALE).astype(jnp.float16), ('pair', 'z'), 0, 0,...  10.6 us
    all_to_all x1, starting transfers between devices, shards(): own = lax.all_to_all(spread(activations, n_row), ROW, 0, 0, tiled=True)  10.5 us
    pallas_call x2, Pallas kernels, up_product(): pl.pallas_call(kernel, out_shape=pltpu.VMEM((sources, rows, LANES), jnp.f...  3.27 us
  transfers between devices with their start and end apart: 6, of which 3 were waited for; matrix products, arithmetic and copies ran while one was open for 0% of the time, Pallas kernels for 1%

profile of v5, /device:TPU:1, one launch (start us, length us, event | category | flops | bytes accessed | tf_op | source)
XLA Modules:
  0.0 114.9 jit_solution(8748220729188475059)
XLA Ops:
  0.0 0.9 copy-done.3
  0.9 0.9 shard_map.46
  1.8 10.5 %all-to-all-start = ((bf16[32,72,128]{2,1,0:T(8,128)(2,1)}), bf16[32,72,128]{2,1,0:T(8,128)(2,1)S(1)}, u32[]{:S(2)}, u32[]{:S(2)}) async-start(bf16[32,72,128]{2,1,0:T(8,128)(2,1)} %shard_map.46), calls=%async_computation | async-start | bytes 1179648 | tf_op jit(solution)/shard_map/all_to_all | solution.py:250
  12.3 2.9 %collective-permute-start.1 = (bf16[512,896]{1,0:T(8,128)(2,1)}, bf16[512,896]{1,0:T(8,128)(2,1)S(1)}, u32[]{:S(2)}, u32[]{:S(2)}) collective-permute-start(bf16[512,896]{1,0:T(8,128)(2,1)} %gate_ref.1), channel_id=1, source_target_pairs={{0,1},{1,0},{2,3},{3,2},{4,5},{5,4},{6,7},{7,6},{8,9},{9,8},{10,11... | collective-permute-start | bytes 2752520 | tf_op jit(solution)/shard_map/ppermute | solution.py:248
  15.2 1.9 %collective-permute-start.2 = (bf16[512,896]{1,0:T(8,128)(2,1)}, bf16[512,896]{1,0:T(8,128)(2,1)}, u32[]{:S(2)}, u32[]{:S(2)}) collective-permute-start(bf16[512,896]{1,0:T(8,128)(2,1)} %up_ref.1), channel_id=1, source_target_pairs={{0,1},{1,0},{2,3},{3,2},{4,5},{5,4},{6,7},{7,6},{8,9},{9,8},{10,11... | collective-permute-start | bytes 2752520 | tf_op jit(solution)/shard_map/ppermute | solution.py:248
  17.1 12.7 %all-to-all-done.own_ref = bf16[32,72,128]{2,1,0:T(8,128)(2,1)S(1)} async-done(((bf16[32,72,128]{2,1,0:T(8,128)(2,1)}), bf16[32,72,128]{2,1,0:T(8,128)(2,1)S(1)}, u32[]{:S(2)}, u32[]{:S(2)}) %all-to-all-start) | async-done | bytes 589856 | tf_op jit(solution)/shard_map/all_to_all | solution.py:250
  29.8 4.4 %collective-permute-start = (bf16[8,2,72,128]{3,2,1,0:T(8,128)(2,1)S(1)}, bf16[8,2,72,128]{3,2,1,0:T(8,128)(2,1)S(1)}, u32[]{:S(2)}, u32[]{:S(2)}) collective-permute-start(bf16[8,2,72,128]{3,2,1,0:T(8,128)(2,1)S(1)} %dynamic-slice_bitcast_fusion), channel_id=1, source_target_pairs={{0,1},{1,0},{2,3},{3,2},{4,5},{5,4},{6,7},{7,6},{8,9},{9,8},{10,11... | collective-permute-start | bytes 884744 | tf_op jit(solution)/shard_map/ppermute | solution.py:248
  34.2 1.0 shard_map.47.base_ref
  35.3 0.0 collective-permute-done.1.gate_ref
  35.3 0.0 collective-permute-done.2.up_ref
  35.3 0.1 collective-permute-done.other_ref
  35.4 2.2 %shard_map.48 = f32[16,256,128]{2,1,0:T(8,128)S(1)} custom-call(bf16[8,2,72,128]{3,2,1,0:T(8,128)(2,1)S(1)} %collective-permute-done.other_ref, bf16[512,896]{1,0:T(8,128)(2,1)S(1)} %collective-permute-done.1.gate_ref, bf16[512,896]{1,0:T(8,128)(2,1)} %collective-permute-done.2.up_ref, f32[16,256,128]{2,1,0:T(8,128)S(1)} %shard_map.47.base_ref), custom_call_target="tpu_custom_call" | custom-call | tf_op jit(solution)/shard_map/pallas_call | solution.py:133
  37.6 0.0 copy-start.2
  37.6 1.3 %multiply_convert_fusion = f16[16,256,128]{2,1,0:T(8,128)(2,1)} fusion(f32[16,256,128]{2,1,0:T(8,128)S(1)} %shard_map.48), kind=kLoop, calls=%fused_computation.1 | loop fusion | flops 1048576 | bytes 3145728 | tf_op jit(solution)/shard_map/convert_element_type | solution.py:269
  38.9 10.6 %all-to-all-start.1 = ((f16[16,256,128]{2,1,0:T(8,128)(2,1)}), f16[16,256,128]{2,1,0:T(8,128)(2,1)S(1)}, u32[]{:S(2)}, u32[]{:S(2)}) async-start(f16[16,256,128]{2,1,0:T(8,128)(2,1)} %multiply_convert_fusion), calls=%async_computation.1 | async-start | bytes 2097152 | tf_op jit(solution)/shard_map/all_to_all | solution.py:268
  49.5 3.3 %collective-permute-start.3 = (bf16[896,512]{1,0:T(8,128)(2,1)S(1)}, bf16[896,512]{1,0:T(8,128)(2,1)S(1)}, u32[]{:S(2)}, u32[]{:S(2)}) collective-permute-start(bf16[896,512]{1,0:T(8,128)(2,1)S(1)} %copy-done.2), channel_id=1, source_target_pairs={{0,16},{16,0},{1,17},{17,1},{2,18},{18,2},{3,19},{19,3},{4,20},{20... | collective-permute-start | bytes 2752520 | tf_op jit(solution)/shard_map/ppermute | solution.py:248
  52.8 22.2 %all-to-all-done.1 = f16[16,256,128]{2,1,0:T(8,128)(2,1)S(1)} async-done(((f16[16,256,128]{2,1,0:T(8,128)(2,1)}), f16[16,256,128]{2,1,0:T(8,128)(2,1)S(1)}, u32[]{:S(2)}, u32[]{:S(2)}) %all-to-all-start.1) | async-done | bytes 1048608 | tf_op jit(solution)/shard_map/all_to_all | solution.py:268
  75.0 0.1 convert_reduce_fusion.sum_ref
  75.2 0.1 shard_map.49
  75.3 20.8 %all-gather.1.hidden_ref = bf16[16,36,896]{2,1,0:T(8,128)(2,1)S(1)} all-gather(bf16[1,36,896]{2,1,0:T(8,128)(2,1)S(1)} %bitcast.12), channel_id=2, replica_groups=mesh['y'=8,'far'=2,'pair'=2,'z'=8,'core'=2] {'z','core'}, dimensions={0}, use_global_device_ids=true | all-gather | bytes 1096704 | tf_op jit(solution)/shard_map/all_gather | solution.py:274
  96.1 0.0 collective-permute-done.3.other_ref
  96.1 1.0 shard_map.50
  97.1 17.1 %all_to_all.15.shares_ref = bf16[16,72,128]{2,1,0:T(8,128)(2,1)S(1)} all-to-all(bf16[16,72,128]{2,1,0:T(8,128)(2,1)S(1)} %shard_map.50), channel_id=1, replica_groups=mesh['y'=8,'far'=2,'pair'=2,'z'=8,'core'=2] {'y','far'}, dimensions={0} | all-to-all | bytes 589824 | tf_op jit(solution)/shard_map/all_to_all | solution.py:276
  114.3 0.7 shard_map.51
  (7 shorter events, 0.0 us)
Async XLA Ops:
  0.0 34.2 %copy-start = (bf16[512,896]{1,0:T(8,128)(2,1)S(1)}, bf16[512,896]{1,0:T(8,128)(2,1)}, u32[]{:S(2)}) copy-start(bf16[512,896]{1,0:T(8,128)(2,1)} %gate_ref.1) | copy-start | bytes 2752516
  0.0 34.2 %copy-start.1 = (bf16[512,896]{1,0:T(8,128)(2,1)S(1)}, bf16[512,896]{1,0:T(8,128)(2,1)}, u32[]{:S(2)}) copy-start(bf16[512,896]{1,0:T(8,128)(2,1)} %up_ref.1) | copy-start | bytes 2752516
  0.0 0.9 copy-start.3
  1.8 28.0 %all-to-all-start = ((bf16[32,72,128]{2,1,0:T(8,128)(2,1)}), bf16[32,72,128]{2,1,0:T(8,128)(2,1)S(1)}, u32[]{:S(2)}, u32[]{:S(2)}) async-start(bf16[32,72,128]{2,1,0:T(8,128)(2,1)} %shard_map.46), calls=%async_computation | async-start | bytes 1179648 | tf_op jit(solution)/shard_map/all_to_all | solution.py:250
  12.3 23.0 %collective-permute-start.1 = (bf16[512,896]{1,0:T(8,128)(2,1)}, bf16[512,896]{1,0:T(8,128)(2,1)S(1)}, u32[]{:S(2)}, u32[]{:S(2)}) collective-permute-start(bf16[512,896]{1,0:T(8,128)(2,1)} %gate_ref.1), channel_id=1, source_target_pairs={{0,1},{1,0},{2,3},{3,2},{4,5},{5,4},{6,7},{7,6},{8,9},{9,8},{10,11... | collective-permute-start | bytes 2752520 | tf_op jit(solution)/shard_map/ppermute | solution.py:248
  15.2 20.1 %collective-permute-start.2 = (bf16[512,896]{1,0:T(8,128)(2,1)}, bf16[512,896]{1,0:T(8,128)(2,1)}, u32[]{:S(2)}, u32[]{:S(2)}) collective-permute-start(bf16[512,896]{1,0:T(8,128)(2,1)} %up_ref.1), channel_id=1, source_target_pairs={{0,1},{1,0},{2,3},{3,2},{4,5},{5,4},{6,7},{7,6},{8,9},{9,8},{10,11... | collective-permute-start | bytes 2752520 | tf_op jit(solution)/shard_map/ppermute | solution.py:248
  29.8 5.6 %collective-permute-start = (bf16[8,2,72,128]{3,2,1,0:T(8,128)(2,1)S(1)}, bf16[8,2,72,128]{3,2,1,0:T(8,128)(2,1)S(1)}, u32[]{:S(2)}, u32[]{:S(2)}) collective-permute-start(bf16[8,2,72,128]{3,2,1,0:T(8,128)(2,1)S(1)} %dynamic-slice_bitcast_fusion), channel_id=1, source_target_pairs={{0,1},{1,0},{2,3},{3,2},{4,5},{5,4},{6,7},{7,6},{8,9},{9,8},{10,11... | collective-permute-start | bytes 884744 | tf_op jit(solution)/shard_map/ppermute | solution.py:248
  37.6 11.9 %copy-start.2 = (bf16[896,512]{1,0:T(8,128)(2,1)S(1)}, bf16[896,512]{1,0:T(8,128)(2,1)}, u32[]{:S(2)}) copy-start(bf16[896,512]{1,0:T(8,128)(2,1)} %own_ref.1) | copy-start | bytes 2752516
  38.9 36.1 %all-to-all-start.1 = ((f16[16,256,128]{2,1,0:T(8,128)(2,1)}), f16[16,256,128]{2,1,0:T(8,128)(2,1)S(1)}, u32[]{:S(2)}, u32[]{:S(2)}) async-start(f16[16,256,128]{2,1,0:T(8,128)(2,1)} %multiply_convert_fusion), calls=%async_computation.1 | async-start | bytes 2097152 | tf_op jit(solution)/shard_map/all_to_all | solution.py:268
  49.5 46.6 %collective-permute-start.3 = (bf16[896,512]{1,0:T(8,128)(2,1)S(1)}, bf16[896,512]{1,0:T(8,128)(2,1)S(1)}, u32[]{:S(2)}, u32[]{:S(2)}) collective-permute-start(bf16[896,512]{1,0:T(8,128)(2,1)S(1)} %copy-done.2), channel_id=1, source_target_pairs={{0,16},{16,0},{1,17},{17,1},{2,18},{18,2},{3,19},{19,3},{4,20},{20... | collective-permute-start | bytes 2752520 | tf_op jit(solution)/shard_map/ppermute | solution.py:248

commit v6 on v5

--- a/solution.py
+++ b/solution.py
@@ -15,8 +15,10 @@
 SCALAR = pl.BlockSpec(memory_space=pltpu.SMEM)
 WHOLE = pl.BlockSpec(memory_space=pltpu.VMEM)
 SCALE = 16.0
+COST = 8
 ROW, COL = ("y", "far", "pair"), ("z", "core")
 ALONG_X = 4
+FAR = ALONG_X // PAIR
 
 
 def lanes(q):
@@ -108,36 +110,34 @@
                 out_ref[n, where, :] = value
 
 
-def own_kernel(core_ref, own_ref, gate_ref, up_ref, out_ref, held):
+def up_kernel(flip, core_ref, got_ref, gate_ref, up_ref, *refs):
+    *base, out_ref, held = refs
     depth = out_ref.shape[0] // PAIR
+    side = flip + (1 - 2 * flip) * core_ref[0]
 
     def source_at(n):
-        return own_ref[n % depth * 2 * PAIR + core_ref[0] * PAIR + n // depth]
-
-    add_product(source_at, gate_ref, up_ref, None, out_ref, held)
-
-
-def other_kernel(other_ref, gate_ref, up_ref, base_ref, out_ref, held):
-    depth = out_ref.shape[0] // PAIR
-
-    def source_at(n):
-        return other_ref[n % depth, n // depth]
-
-    add_product(source_at, gate_ref, up_ref, base_ref, out_ref, held)
-
-
-def up_product(kernel, specs, sources, operands, gate, up, *base):
+        b = n % depth
+        return got_ref[(b % FAR * PAIR + n // depth) * 2 + side, b // FAR]
+
+    add_product(source_at, gate_ref, up_ref, base[0] if base else None, out_ref, held)
+
+
+def up_product(flip, core, got, sources, gate, up, *base):
     wide_tiles = gate.shape[1] // LANES
     rows = 2 * wide_tiles * MAIN + (wide_tiles + 1) // 2 * 8
     held = pltpu.VMEM((sources * (MAIN + 8), gate.shape[0]), jnp.bfloat16)
-    return pl.pallas_call(
-        kernel,
+    work = COST * sources * (MAIN + 8) * gate.size
+    return pl.pallas_call(
+        functools.partial(up_kernel, flip),
+        cost_estimate=pl.CostEstimate(
+            flops=4 * work, bytes_accessed=4 * gate.size, transcendentals=0
+        ),
         out_shape=pltpu.VMEM((sources, rows, LANES), jnp.float32),
-        in_specs=specs + [WHOLE] * (2 + len(base)),
+        in_specs=[SCALAR] + [WHOLE] * (3 + len(base)),
         out_specs=WHOLE,
         scratch_shapes=[held],
         compiler_params=LIMIT,
-    )(*operands, gate, up, *base)
+    )(core, got, gate, up, *base)
 
 
 def activate_kernel(sum_ref, out_ref):
@@ -192,16 +192,17 @@
     theirs = jnp.dot(other[...], other_ref[...], preferred_element_type=jnp.float32)
     for n in range(sources):
         at, end = rows_of(n, MAIN), slice(main + n * 8, main + n * 8 + 8)
+        to = n % 2 * (sources // 2) + n // 2
         tails = []
         for q in range(tiles):
-            out_ref[n, rows_of(q, MAIN), :] = (
+            out_ref[to, rows_of(q, MAIN), :] = (
                 mine[at, lanes(q)] + theirs[at, lanes(q)]
             ).astype(jnp.bfloat16)
             a, b = mine[end, lanes(q)], theirs[end, lanes(q)]
             later = pltpu.roll(jnp.where(first, b, a), 8 - EXTRA, 0)
             tails.append(jnp.where(first, a, b) + later)
         tail = gather_extra(tails, lambda q: q * EXTRA)
-        out_ref[n, tiles * MAIN :, :] = tail.astype(jnp.bfloat16)
+        out_ref[to, tiles * MAIN :, :] = tail.astype(jnp.bfloat16)
 
 
 def down_product(pair, hidden, weight, other_weight):
@@ -247,24 +248,25 @@
     def swap(x, axis):
         return lax.ppermute(x, axis, [(0, 1), (1, 0)])
 
-    own = lax.all_to_all(spread(activations, n_row), ROW, 0, 0, tiled=True)
-    gate_other, up_other = swap(gate_matrix, "core"), swap(up_matrix, "core")
+    near = lax.all_to_all(
+        spread(activations, n_row // ALONG_X), "y", 0, 0, tiled=True
+    )
+    halves = near.reshape(1, 2, near.shape[0] // 2, *near.shape[1:])
+    halves = jnp.broadcast_to(halves, (ALONG_X, *halves.shape[1:]))
+    halves = halves.reshape(2 * ALONG_X, *halves.shape[2:])
+    halves, gate, up = lax.optimization_barrier((halves, gate_matrix, up_matrix))
+    gate_other, up_other = swap(gate, "core"), swap(up, "core")
     down_other = swap(down_matrix, "pair")
-    by_core = own.reshape(depth, 2, PAIR, *own.shape[1:])
-    give = lax.dynamic_index_in_dim(by_core, 1 - core, 1, keepdims=False)
-    other = swap(give, "core")
-    sources = PAIR * depth
-    terms = up_product(
-        own_kernel,
-        [SCALAR, WHOLE],
-        sources,
-        (core.reshape(1), own),
-        gate_matrix,
-        up_matrix,
-    )
-    terms = up_product(
-        other_kernel, [WHOLE], sources, (other,), gate_other, up_other, terms
-    )
+    got = lax.all_to_all(
+        halves,
+        ("far", "pair", "core"),
+        0,
+        0,
+        tiled=True,
+    )
+    me, sources = core.reshape(1), PAIR * depth
+    terms = up_product(0, me, got, sources, gate, up)
+    terms = up_product(1, me, got, sources, gate_other, up_other, terms)
     arrived = lax.all_to_all(
         (terms * SCALE).astype(jnp.float16), ("pair", "z"), 0, 0, tiled=True
     )
@@ -278,8 +280,7 @@
 
 def solution(mesh):
     n_row, n_col = mesh.devices.shape
-    far = ALONG_X // PAIR
-    devices = mesh.devices.reshape(n_row // ALONG_X, far, PAIR, n_col // 2, 2)
+    devices = mesh.devices.reshape(n_row // ALONG_X, FAR, PAIR, n_col // 2, 2)
     chips = jax.sharding.Mesh(devices, ROW + COL)
     placed = (P(ROW, COL), P(COL, ROW), P(COL, ROW), P(ROW, COL))
     return jax.shard_map(

time: 115 us -> 114 us (level)
  blocking collectives: 37.9 us -> 53 us
  starting transfers between devices: 33.5 us -> 24.3 us
  waiting for transfers between devices: 35 us -> 28 us
    all_to_all x0 -> x1, blocking collectives: none -> 15.7 us  [shards(): lax.all_to_all(spread(activations, n_row // ALONG_X), 'y', 0, 0, tiled=True)]
    all_to_all x1, waiting for transfers between devices: 12.7 us -> 5.83 us  [shards(): got = lax.all_to_all(halves, ('far', 'pair', 'core'), 0, 0, tiled=True)]
    ppermute x4 -> x3, starting transfers between devices: 12.4 us -> 7.59 us  [swap(): return lax.ppermute(x, axis, [(0, 1), (1, 0)])]
    all_to_all x1, starting transfers between devices: 10.5 us -> 6.55 us  [shards(): got = lax.all_to_all(halves, ('far', 'pair', 'core'), 0, 0, tiled=True)]
  transfers between devices with their start and end apart: 6 -> 5, of which waited for: 3 -> 2; matrix products, arithmetic and copies ran while one was open for 0% -> 0% of each run, Pallas kernels for 1% -> 1%
where the time goes in v6:
time: 114 us
  blocking collectives  53 us (46%)
  waiting for transfers between devices  28 us (25%)
  starting transfers between devices  24.3 us (21%)
  Pallas kernels  5.07 us (4%)
  local copies, waits for them, and re-layouts  1.66 us (1%)
  other arithmetic  1.44 us (1%)
    all_to_all x1, waiting for transfers between devices, shards(): lax.all_to_all((terms * SCALE).astype(jnp.float16), ('pair', 'z'), 0, 0,...  22.1 us
    all_gather x1, blocking collectives, shards(): gathered = lax.all_gather(hidden, COL, axis=0, tiled=False)  20.9 us
    all_to_all x1, blocking collectives, shards(): return finish(lax.all_to_all(share, ('y', 'far'), 0, 0, tiled=True))  16.4 us
    all_to_all x1, blocking collectives, shards(): lax.all_to_all(spread(activations, n_row // ALONG_X), 'y', 0, 0, tiled=True)  15.7 us
    all_to_all x1, starting transfers between devices, shards(): lax.all_to_all((terms * SCALE).astype(jnp.float16), ('pair', 'z'), 0, 0,...  10.1 us
    ppermute x3, starting transfers between devices, swap(): return lax.ppermute(x, axis, [(0, 1), (1, 0)])  7.59 us
    all_to_all x1, starting transfers between devices, shards(): got = lax.all_to_all(halves, ('far', 'pair', 'core'), 0, 0, tiled=True)  6.55 us
    all_to_all x1, waiting for transfers between devices, shards(): got = lax.all_to_all(halves, ('far', 'pair', 'core'), 0, 0, tiled=True)  5.83 us
  transfers between devices with their start and end apart: 5, of which 2 were waited for; matrix products, arithmetic and copies ran while one was open for 0% of the time, Pallas kernels for 1%

profile of v6, /device:TPU:1, one launch (start us, length us, event | category | flops | bytes accessed | tf_op | source)
XLA Modules:
  0.0 113.6 jit_solution(13603903763834136889)
XLA Ops:
  0.0 0.7 copy-done.1
  0.8 15.7 %all_to_all.20 = bf16[8,72,128]{2,1,0:T(8,128)(2,1)S(1)} all-to-all(bf16[8,72,128]{2,1,0:T(8,128)(2,1)S(1)} %shard_map.46), channel_id=1, replica_groups=mesh['y'=8,'far'=2,'pair'=2,'z'=8,'core'=2] {'y'}, dimensions={0} | all-to-all | bytes 294912 | tf_op jit(solution)/shard_map/all_to_all | solution.py:251
  16.5 0.9 broadcast_in_dim.8
  17.4 6.5 %all-to-all-start.1 = ((bf16[8,4,72,128]{3,2,1,0:T(8,128)(2,1)}), bf16[8,4,72,128]{3,2,1,0:T(8,128)(2,1)S(1)}, u32[]{:S(2)}, u32[]{:S(2)}) async-start(bf16[8,4,72,128]{3,2,1,0:T(8,128)(2,1)} %bitcast.3), calls=%async_computation.1 | async-start | bytes 1179648 | tf_op jit(solution)/shard_map/all_to_all | solution.py:260
  23.9 1.9 %collective-permute-start = (bf16[512,896]{1,0:T(8,128)(2,1)S(1)}, bf16[512,896]{1,0:T(8,128)(2,1)S(1)}, u32[]{:S(2)}, u32[]{:S(2)}) collective-permute-start(bf16[512,896]{1,0:T(8,128)(2,1)S(1)} %copy-done.2), channel_id=1, source_target_pairs={{0,1},{1,0},{2,3},{3,2},{4,5},{5,4},{6,7},{7,6},{8,9},{9,8},{10,11... | collective-permute-start | bytes 2752520 | tf_op jit(solution)/shard_map/ppermute | solution.py:249
  25.9 0.0 copy-done.3
  25.9 2.4 %collective-permute-start.1 = (bf16[512,896]{1,0:T(8,128)(2,1)S(1)}, bf16[512,896]{1,0:T(8,128)(2,1)}, u32[]{:S(2)}, u32[]{:S(2)}) collective-permute-start(bf16[512,896]{1,0:T(8,128)(2,1)S(1)} %copy-done.3), channel_id=1, source_target_pairs={{0,1},{1,0},{2,3},{3,2},{4,5},{5,4},{6,7},{7,6},{8,9},{9,8},{10,11... | collective-permute-start | bytes 2752520 | tf_op jit(solution)/shard_map/ppermute | solution.py:249
  28.3 5.8 %all-to-all-done.1.got_ref = bf16[8,4,72,128]{3,2,1,0:T(8,128)(2,1)S(1)} async-done(((bf16[8,4,72,128]{3,2,1,0:T(8,128)(2,1)}), bf16[8,4,72,128]{3,2,1,0:T(8,128)(2,1)S(1)}, u32[]{:S(2)}, u32[]{:S(2)}) %all-to-all-start.1) | async-done | bytes 589856 | tf_op jit(solution)/shard_map/all_to_all | solution.py:260
  34.1 1.0 shard_map.47.refs_0_
  35.2 0.0 collective-permute-done.gate_ref
  35.2 0.0 collective-permute-done.1.up_ref
  35.2 2.3 %shard_map.48 = f32[16,256,128]{2,1,0:T(8,128)S(1)} custom-call(s32[1]{0:T(128)} %bitcast.1.core_ref, bf16[8,4,72,128]{3,2,1,0:T(8,128)(2,1)S(1)} %all-to-all-done.1.got_ref, bf16[512,896]{1,0:T(8,128)(2,1)S(1)} %collective-permute-done.gate_ref, bf16[512,896]{1,0:T(8,128)(2,1)} %collective-permute-done.1.up_ref, f32[16,256,128]{2,1,0:T(8,128)S(1)} %shard_map.47.refs_0_), custom_call_target="tpu_custom_call" | custom-call | flops 5637144576 | bytes 1835008 | tf_op jit(solution)/shard_map/pallas_call | solution.py:130
  37.5 0.0 copy-start
  37.5 1.3 %multiply_convert_fusion = f16[16,256,128]{2,1,0:T(8,128)(2,1)} fusion(f32[16,256,128]{2,1,0:T(8,128)S(1)} %shard_map.48), kind=kLoop, calls=%fused_computation.1 | loop fusion | flops 1048576 | bytes 3145728 | tf_op jit(solution)/shard_map/convert_element_type | solution.py:271
  38.8 10.1 %all-to-all-start.2 = ((f16[16,256,128]{2,1,0:T(8,128)(2,1)}), f16[16,256,128]{2,1,0:T(8,128)(2,1)S(1)}, u32[]{:S(2)}, u32[]{:S(2)}) async-start(f16[16,256,128]{2,1,0:T(8,128)(2,1)} %multiply_convert_fusion), calls=%async_computation.2 | async-start | bytes 2097152 | tf_op jit(solution)/shard_map/all_to_all | solution.py:270
  48.9 3.3 %collective-permute-start.2 = (bf16[896,512]{1,0:T(8,128)(2,1)S(1)}, bf16[896,512]{1,0:T(8,128)(2,1)S(1)}, u32[]{:S(2)}, u32[]{:S(2)}) collective-permute-start(bf16[896,512]{1,0:T(8,128)(2,1)S(1)} %copy-done), channel_id=1, source_target_pairs={{0,16},{16,0},{1,17},{17,1},{2,18},{18,2},{3,19},{19,3},{4,20},{20... | collective-permute-start | bytes 2752520 | tf_op jit(solution)/shard_map/ppermute | solution.py:249
  52.2 22.1 %all-to-all-done.2 = f16[16,256,128]{2,1,0:T(8,128)(2,1)S(1)} async-done(((f16[16,256,128]{2,1,0:T(8,128)(2,1)}), f16[16,256,128]{2,1,0:T(8,128)(2,1)S(1)}, u32[]{:S(2)}, u32[]{:S(2)}) %all-to-all-start.2) | async-done | bytes 1048608 | tf_op jit(solution)/shard_map/all_to_all | solution.py:270
  74.4 0.1 convert_reduce_fusion.sum_ref
  74.5 0.1 shard_map.49
  74.6 20.9 %all-gather.1.hidden_ref = bf16[16,36,896]{2,1,0:T(8,128)(2,1)S(1)} all-gather(bf16[1,36,896]{2,1,0:T(8,128)(2,1)S(1)} %bitcast.8), channel_id=2, replica_groups=mesh['y'=8,'far'=2,'pair'=2,'z'=8,'core'=2] {'z','core'}, dimensions={0}, use_global_device_ids=true | all-gather | bytes 1096704 | tf_op jit(solution)/shard_map/all_gather | solution.py:276
  95.5 0.0 collective-permute-done.2.other_ref
  95.5 1.0 shard_map.50
  96.6 16.4 %all_to_all.21.shares_ref = bf16[16,72,128]{2,1,0:T(8,128)(2,1)S(1)} all-to-all(bf16[16,72,128]{2,1,0:T(8,128)(2,1)S(1)} %shard_map.50), channel_id=1, replica_groups=mesh['y'=8,'far'=2,'pair'=2,'z'=8,'core'=2] {'y','far'}, dimensions={0} | all-to-all | bytes 589824 | tf_op jit(solution)/shard_map/all_to_all | solution.py:278
  112.9 0.7 shard_map.51
  (6 shorter events, 0.0 us)
Async XLA Ops:
  0.0 0.7 copy-start.1
  0.7 23.2 %copy-start.2 = (bf16[512,896]{1,0:T(8,128)(2,1)S(1)}, bf16[512,896]{1,0:T(8,128)(2,1)}, u32[]{:S(2)}) copy-start(bf16[512,896]{1,0:T(8,128)(2,1)} %gate_ref) | copy-start | bytes 2752516
  0.7 25.1 %copy-start.3 = (bf16[512,896]{1,0:T(8,128)(2,1)S(1)}, bf16[512,896]{1,0:T(8,128)(2,1)}, u32[]{:S(2)}) copy-start(bf16[512,896]{1,0:T(8,128)(2,1)} %up_ref) | copy-start | bytes 2752516
  17.4 16.7 %all-to-all-start.1 = ((bf16[8,4,72,128]{3,2,1,0:T(8,128)(2,1)}), bf16[8,4,72,128]{3,2,1,0:T(8,128)(2,1)S(1)}, u32[]{:S(2)}, u32[]{:S(2)}) async-start(bf16[8,4,72,128]{3,2,1,0:T(8,128)(2,1)} %bitcast.3), calls=%async_computation.1 | async-start | bytes 1179648 | tf_op jit(solution)/shard_map/all_to_all | solution.py:260
  23.9 11.2 %collective-permute-start = (bf16[512,896]{1,0:T(8,128)(2,1)S(1)}, bf16[512,896]{1,0:T(8,128)(2,1)S(1)}, u32[]{:S(2)}, u32[]{:S(2)}) collective-permute-start(bf16[512,896]{1,0:T(8,128)(2,1)S(1)} %copy-done.2), channel_id=1, source_target_pairs={{0,1},{1,0},{2,3},{3,2},{4,5},{5,4},{6,7},{7,6},{8,9},{9,8},{10,11... | collective-permute-start | bytes 2752520 | tf_op jit(solution)/shard_map/ppermute | solution.py:249
  25.9 9.3 %collective-permute-start.1 = (bf16[512,896]{1,0:T(8,128)(2,1)S(1)}, bf16[512,896]{1,0:T(8,128)(2,1)}, u32[]{:S(2)}, u32[]{:S(2)}) collective-permute-start(bf16[512,896]{1,0:T(8,128)(2,1)S(1)} %copy-done.3), channel_id=1, source_target_pairs={{0,1},{1,0},{2,3},{3,2},{4,5},{5,4},{6,7},{7,6},{8,9},{9,8},{10,11... | collective-permute-start | bytes 2752520 | tf_op jit(solution)/shard_map/ppermute | solution.py:249
  37.5 11.5 %copy-start = (bf16[896,512]{1,0:T(8,128)(2,1)S(1)}, bf16[896,512]{1,0:T(8,128)(2,1)}, u32[]{:S(2)}) copy-start(bf16[896,512]{1,0:T(8,128)(2,1)} %own_ref.1) | copy-start | bytes 2752516
  38.8 35.6 %all-to-all-start.2 = ((f16[16,256,128]{2,1,0:T(8,128)(2,1)}), f16[16,256,128]{2,1,0:T(8,128)(2,1)S(1)}, u32[]{:S(2)}, u32[]{:S(2)}) async-start(f16[16,256,128]{2,1,0:T(8,128)(2,1)} %multiply_convert_fusion), calls=%async_computation.2 | async-start | bytes 2097152 | tf_op jit(solution)/shard_map/all_to_all | solution.py:270
  48.9 46.6 %collective-permute-start.2 = (bf16[896,512]{1,0:T(8,128)(2,1)S(1)}, bf16[896,512]{1,0:T(8,128)(2,1)S(1)}, u32[]{:S(2)}, u32[]{:S(2)}) collective-permute-start(bf16[896,512]{1,0:T(8,128)(2,1)S(1)} %copy-done), channel_id=1, source_target_pairs={{0,16},{16,0},{1,17},{17,1},{2,18},{18,2},{3,19},{19,3},{4,20},{20... | collective-permute-start | bytes 2752520 | tf_op jit(solution)/shard_map/ppermute | solution.py:249

commit v7 on v6

--- a/solution.py
+++ b/solution.py
@@ -64,7 +64,7 @@
     )(x)
 
 
-def add_product(source_at, gate_ref, up_ref, base_ref, out_ref, held):
+def add_product(source_at, ready, gate_ref, up_ref, base_ref, out_ref, held):
     sources = out_ref.shape[0]
     tiles = held.shape[1] // LANES
     wide_tiles = gate_ref.shape[1] // LANES
@@ -88,30 +88,42 @@
         held[main:, lanes(q)] = moved[rows_of(q, sources * 8)]
     row = lax.broadcasted_iota(jnp.int32, (8, LANES), 0) // EXTRA
     x = held[...]
-    for first in range(0, wide_tiles, 2):
-        count = min(2, wide_tiles - first)
-        columns = slice(first * LANES, (first + count) * LANES)
-        gate = jnp.dot(x, gate_ref[:, columns], preferred_element_type=jnp.float32)
-        up = jnp.dot(x, up_ref[:, columns], preferred_element_type=jnp.float32)
-        for n in range(sources):
-            end = slice(main + n * 8, main + n * 8 + 8)
-            mixed = jnp.where(row == 0, gate[end, lanes(0)], gate[end, lanes(count - 1)])
-            mixed = jnp.where(row == 2, up[end, lanes(0)], mixed)
-            mixed = jnp.where(row == 3, up[end, lanes(count - 1)], mixed)
-            start = 2 * wide_tiles * MAIN + 4 * first
-            parts = [(slice(start, start + 8), mixed)]
-            for i in range(count):
-                at = rows_of(n, MAIN)
-                parts.append((rows_of(first + i, MAIN), gate[at, lanes(i)]))
-                parts.append((rows_of(wide_tiles + first + i, MAIN), up[at, lanes(i)]))
-            for where, value in parts:
+    for kind, weight_ref in enumerate((gate_ref, up_ref)):
+        if kind:
+            ready()
+        for first in range(0, wide_tiles, 2):
+            count = min(2, wide_tiles - first)
+            columns = slice(first * LANES, (first + count) * LANES)
+            term = jnp.dot(x, weight_ref[:, columns], preferred_element_type=jnp.float32)
+            for n in range(sources):
+                end = slice(main + n * 8, main + n * 8 + 8)
+                start = 2 * wide_tiles * MAIN + 4 * first
+                where = slice(start, start + 8)
+                mixed = jnp.where(
+                    row % 2 == 0, term[end, lanes(0)], term[end, lanes(count - 1)]
+                )
                 if base_ref is not None:
-                    value += base_ref[n, where, :]
-                out_ref[n, where, :] = value
+                    mixed += base_ref[n, where, :]
+                if kind:
+                    mixed = jnp.where(row < 2, out_ref[n, where, :], mixed)
+                out_ref[n, where, :] = mixed
+                for i in range(count):
+                    where = rows_of(kind * wide_tiles + first + i, MAIN)
+                    value = term[rows_of(n, MAIN), lanes(i)]
+                    if base_ref is not None:
+                        value += base_ref[n, where, :]
+                    out_ref[n, where, :] = value
 
 
 def up_kernel(flip, core_ref, got_ref, gate_ref, up_ref, *refs):
-    *base, out_ref, held = refs
+    base_ref, ready = None, lambda: None
+    if flip:
+        base_ref, out_ref, held, up_held, done = refs
+        fetch = pltpu.make_async_copy(up_ref, up_held, done)
+        fetch.start()
+        up_ref, ready = up_held, fetch.wait
+    else:
+        out_ref, held = refs
     depth = out_ref.shape[0] // PAIR
     side = flip + (1 - 2 * flip) * core_ref[0]
 
@@ -119,23 +131,27 @@
         b = n % depth
         return got_ref[(b % FAR * PAIR + n // depth) * 2 + side, b // FAR]
 
-    add_product(source_at, gate_ref, up_ref, base[0] if base else None, out_ref, held)
+    add_product(source_at, ready, gate_ref, up_ref, base_ref, out_ref, held)
 
 
 def up_product(flip, core, got, sources, gate, up, *base):
     wide_tiles = gate.shape[1] // LANES
     rows = 2 * wide_tiles * MAIN + (wide_tiles + 1) // 2 * 8
-    held = pltpu.VMEM((sources * (MAIN + 8), gate.shape[0]), jnp.bfloat16)
     work = COST * sources * (MAIN + 8) * gate.size
+    held = [pltpu.VMEM((sources * (MAIN + 8), gate.shape[0]), jnp.bfloat16)]
+    up_spec = WHOLE
+    if flip:
+        held += [pltpu.VMEM(up.shape, up.dtype), pltpu.SemaphoreType.DMA]
+        up_spec = pl.BlockSpec(memory_space=pl.ANY)
     return pl.pallas_call(
         functools.partial(up_kernel, flip),
         cost_estimate=pl.CostEstimate(
             flops=4 * work, bytes_accessed=4 * gate.size, transcendentals=0
         ),
         out_shape=pltpu.VMEM((sources, rows, LANES), jnp.float32),
-        in_specs=[SCALAR] + [WHOLE] * (3 + len(base)),
-        out_specs=WHOLE,
-        scratch_shapes=[held],
+        in_specs=[SCALAR, WHOLE, WHOLE, up_spec] + [WHOLE] * len(base),
+        out_specs=WHOLE,
+        scratch_shapes=held,
         compiler_params=LIMIT,
     )(core, got, gate, up, *base)
 

time: 114 us -> 114 us (level)
  no operation moved by 1% of the time
where the time goes in v7:
time: 114 us; the launch traced here: 113 us
  blocking collectives  53 us (46%)
  waiting for transfers between devices  28 us (25%)
  starting transfers between devices  24.3 us (21%)
  Pallas kernels  4.59 us (4%)
  local copies, waits for them, and re-layouts  1.66 us (1%)
  other arithmetic  1.44 us (1%)
    all_to_all x1, waiting for transfers between devices, shards(): lax.all_to_all((terms * SCALE).astype(jnp.float16), ('pair', 'z'), 0, 0,...  22.1 us
    all_gather x1, blocking collectives, shards(): gathered = lax.all_gather(hidden, COL, axis=0, tiled=False)  20.9 us
    all_to_all x1, blocking collectives, shards(): return finish(lax.all_to_all(share, ('y', 'far'), 0, 0, tiled=True))  16.4 us
    all_to_all x1, blocking collectives, shards(): lax.all_to_all(spread(activations, n_row // ALONG_X), 'y', 0, 0, tiled=True)  15.7 us
    all_to_all x1, starting transfers between devices, shards(): lax.all_to_all((terms * SCALE).astype(jnp.float16), ('pair', 'z'), 0, 0,...  10.1 us
    ppermute x3, starting transfers between devices, swap(): return lax.ppermute(x, axis, [(0, 1), (1, 0)])  7.59 us
    all_to_all x1, starting transfers between devices, shards(): got = lax.all_to_all(halves, ('far', 'pair', 'core'), 0, 0, tiled=True)  6.55 us
    all_to_all x1, waiting for transfers between devices, shards(): got = lax.all_to_all(halves, ('far', 'pair', 'core'), 0, 0, tiled=True)  5.83 us
  transfers between devices with their start and end apart: 5, of which 2 were waited for; matrix products, arithmetic and copies ran while one was open for 0% of the time, Pallas kernels for 1%

profile of v7, /device:TPU:1, one launch (start us, length us, event | category | flops | bytes accessed | tf_op | source)
XLA Modules:
  0.0 113.1 jit_solution(2411935364202489105)
XLA Ops:
  0.0 0.7 copy-done.1
  0.8 15.7 %all_to_all.20 = bf16[8,72,128]{2,1,0:T(8,128)(2,1)S(1)} all-to-all(bf16[8,72,128]{2,1,0:T(8,128)(2,1)S(1)} %shard_map.46), channel_id=1, replica_groups=mesh['y'=8,'far'=2,'pair'=2,'z'=8,'core'=2] {'y'}, dimensions={0} | all-to-all | bytes 294912 | tf_op jit(solution)/shard_map/all_to_all | solution.py:267
  16.5 0.9 broadcast_in_dim.8
  17.4 6.5 %all-to-all-start.1 = ((bf16[8,4,72,128]{3,2,1,0:T(8,128)(2,1)}), bf16[8,4,72,128]{3,2,1,0:T(8,128)(2,1)S(1)}, u32[]{:S(2)}, u32[]{:S(2)}) async-start(bf16[8,4,72,128]{3,2,1,0:T(8,128)(2,1)} %bitcast.3), calls=%async_computation.1 | async-start | bytes 1179648 | tf_op jit(solution)/shard_map/all_to_all | solution.py:276
  23.9 1.9 %collective-permute-start = (bf16[512,896]{1,0:T(8,128)(2,1)S(1)}, bf16[512,896]{1,0:T(8,128)(2,1)S(1)}, u32[]{:S(2)}, u32[]{:S(2)}) collective-permute-start(bf16[512,896]{1,0:T(8,128)(2,1)S(1)} %copy-done.2), channel_id=1, source_target_pairs={{0,1},{1,0},{2,3},{3,2},{4,5},{5,4},{6,7},{7,6},{8,9},{9,8},{10,11... | collective-permute-start | bytes 2752520 | tf_op jit(solution)/shard_map/ppermute | solution.py:265
  25.9 0.0 copy-done.3
  25.9 2.4 %collective-permute-start.1 = (bf16[512,896]{1,0:T(8,128)(2,1)S(1)}, bf16[512,896]{1,0:T(8,128)(2,1)}, u32[]{:S(2)}, u32[]{:S(2)}) collective-permute-start(bf16[512,896]{1,0:T(8,128)(2,1)S(1)} %copy-done.3), channel_id=1, source_target_pairs={{0,1},{1,0},{2,3},{3,2},{4,5},{5,4},{6,7},{7,6},{8,9},{9,8},{10,11... | collective-permute-start | bytes 2752520 | tf_op jit(solution)/shard_map/ppermute | solution.py:265
  28.3 5.8 %all-to-all-done.1.got_ref = bf16[8,4,72,128]{3,2,1,0:T(8,128)(2,1)S(1)} async-done(((bf16[8,4,72,128]{3,2,1,0:T(8,128)(2,1)}), bf16[8,4,72,128]{3,2,1,0:T(8,128)(2,1)S(1)}, u32[]{:S(2)}, u32[]{:S(2)}) %all-to-all-start.1) | async-done | bytes 589856 | tf_op jit(solution)/shard_map/all_to_all | solution.py:276
  34.1 1.0 shard_map.47.refs_0_
  35.2 0.0 collective-permute-done.gate_ref
  35.2 0.0 collective-permute-done.1.up_ref
  35.2 1.8 %shard_map.48 = f32[16,256,128]{2,1,0:T(8,128)S(1)} custom-call(s32[1]{0:T(128)} %bitcast.1.core_ref, bf16[8,4,72,128]{3,2,1,0:T(8,128)(2,1)S(1)} %all-to-all-done.1.got_ref, bf16[512,896]{1,0:T(8,128)(2,1)S(1)} %collective-permute-done.gate_ref, bf16[512,896]{1,0:T(8,128)(2,1)} %collective-permute-done.1.up_ref, f32[16,256,128]{2,1,0:T(8,128)S(1)} %shard_map.47.refs_0_), custom_call_target="tpu_custom_call" | custom-call | flops 5637144576 | bytes 1835008 | tf_op jit(solution)/shard_map/pallas_call | solution.py:146
  37.0 0.0 copy-start
  37.0 1.3 %multiply_convert_fusion = f16[16,256,128]{2,1,0:T(8,128)(2,1)} fusion(f32[16,256,128]{2,1,0:T(8,128)S(1)} %shard_map.48), kind=kLoop, calls=%fused_computation.1 | loop fusion | flops 1048576 | bytes 3145728 | tf_op jit(solution)/shard_map/convert_element_type | solution.py:287
  38.3 10.1 %all-to-all-start.2 = ((f16[16,256,128]{2,1,0:T(8,128)(2,1)}), f16[16,256,128]{2,1,0:T(8,128)(2,1)S(1)}, u32[]{:S(2)}, u32[]{:S(2)}) async-start(f16[16,256,128]{2,1,0:T(8,128)(2,1)} %multiply_convert_fusion), calls=%async_computation.2 | async-start | bytes 2097152 | tf_op jit(solution)/shard_map/all_to_all | solution.py:286
  48.4 3.3 %collective-permute-start.2 = (bf16[896,512]{1,0:T(8,128)(2,1)S(1)}, bf16[896,512]{1,0:T(8,128)(2,1)S(1)}, u32[]{:S(2)}, u32[]{:S(2)}) collective-permute-start(bf16[896,512]{1,0:T(8,128)(2,1)S(1)} %copy-done), channel_id=1, source_target_pairs={{0,16},{16,0},{1,17},{17,1},{2,18},{18,2},{3,19},{19,3},{4,20},{20... | collective-permute-start | bytes 2752520 | tf_op jit(solution)/shard_map/ppermute | solution.py:265
  51.7 22.1 %all-to-all-done.2 = f16[16,256,128]{2,1,0:T(8,128)(2,1)S(1)} async-done(((f16[16,256,128]{2,1,0:T(8,128)(2,1)}), f16[16,256,128]{2,1,0:T(8,128)(2,1)S(1)}, u32[]{:S(2)}, u32[]{:S(2)}) %all-to-all-start.2) | async-done | bytes 1048608 | tf_op jit(solution)/shard_map/all_to_all | solution.py:286
  73.9 0.1 convert_reduce_fusion.sum_ref
  74.0 0.1 shard_map.49
  74.1 20.9 %all-gather.1.hidden_ref = bf16[16,36,896]{2,1,0:T(8,128)(2,1)S(1)} all-gather(bf16[1,36,896]{2,1,0:T(8,128)(2,1)S(1)} %bitcast.8), channel_id=2, replica_groups=mesh['y'=8,'far'=2,'pair'=2,'z'=8,'core'=2] {'z','core'}, dimensions={0}, use_global_device_ids=true | all-gather | bytes 1096704 | tf_op jit(solution)/shard_map/all_gather | solution.py:292
  95.0 0.0 collective-permute-done.2.other_ref
  95.0 1.0 shard_map.50
  96.1 16.4 %all_to_all.21.shares_ref = bf16[16,72,128]{2,1,0:T(8,128)(2,1)S(1)} all-to-all(bf16[16,72,128]{2,1,0:T(8,128)(2,1)S(1)} %shard_map.50), channel_id=1, replica_groups=mesh['y'=8,'far'=2,'pair'=2,'z'=8,'core'=2] {'y','far'}, dimensions={0} | all-to-all | bytes 589824 | tf_op jit(solution)/shard_map/all_to_all | solution.py:294
  112.5 0.7 shard_map.51
  (6 shorter events, 0.0 us)
Async XLA Ops:
  0.0 0.7 copy-start.1
  0.7 23.2 %copy-start.2 = (bf16[512,896]{1,0:T(8,128)(2,1)S(1)}, bf16[512,896]{1,0:T(8,128)(2,1)}, u32[]{:S(2)}) copy-start(bf16[512,896]{1,0:T(8,128)(2,1)} %gate_ref) | copy-start | bytes 2752516
  0.7 25.1 %copy-start.3 = (bf16[512,896]{1,0:T(8,128)(2,1)S(1)}, bf16[512,896]{1,0:T(8,128)(2,1)}, u32[]{:S(2)}) copy-start(bf16[512,896]{1,0:T(8,128)(2,1)} %up_ref) | copy-start | bytes 2752516
  17.4 16.7 %all-to-all-start.1 = ((bf16[8,4,72,128]{3,2,1,0:T(8,128)(2,1)}), bf16[8,4,72,128]{3,2,1,0:T(8,128)(2,1)S(1)}, u32[]{:S(2)}, u32[]{:S(2)}) async-start(bf16[8,4,72,128]{3,2,1,0:T(8,128)(2,1)} %bitcast.3), calls=%async_computation.1 | async-start | bytes 1179648 | tf_op jit(solution)/shard_map/all_to_all | solution.py:276
  23.9 11.2 %collective-permute-start = (bf16[512,896]{1,0:T(8,128)(2,1)S(1)}, bf16[512,896]{1,0:T(8,128)(2,1)S(1)}, u32[]{:S(2)}, u32[]{:S(2)}) collective-permute-start(bf16[512,896]{1,0:T(8,128)(2,1)S(1)} %copy-done.2), channel_id=1, source_target_pairs={{0,1},{1,0},{2,3},{3,2},{4,5},{5,4},{6,7},{7,6},{8,9},{9,8},{10,11... | collective-permute-start | bytes 2752520 | tf_op jit(solution)/shard_map/ppermute | solution.py:265
  25.9 9.3 %collective-permute-start.1 = (bf16[512,896]{1,0:T(8,128)(2,1)S(1)}, bf16[512,896]{1,0:T(8,128)(2,1)}, u32[]{:S(2)}, u32[]{:S(2)}) collective-permute-start(bf16[512,896]{1,0:T(8,128)(2,1)S(1)} %copy-done.3), channel_id=1, source_target_pairs={{0,1},{1,0},{2,3},{3,2},{4,5},{5,4},{6,7},{7,6},{8,9},{9,8},{10,11... | collective-permute-start | bytes 2752520 | tf_op jit(solution)/shard_map/ppermute | solution.py:265
  37.0 11.5 %copy-start = (bf16[896,512]{1,0:T(8,128)(2,1)S(1)}, bf16[896,512]{1,0:T(8,128)(2,1)}, u32[]{:S(2)}) copy-start(bf16[896,512]{1,0:T(8,128)(2,1)} %own_ref.1) | copy-start | bytes 2752516
  38.3 35.6 %all-to-all-start.2 = ((f16[16,256,128]{2,1,0:T(8,128)(2,1)}), f16[16,256,128]{2,1,0:T(8,128)(2,1)S(1)}, u32[]{:S(2)}, u32[]{:S(2)}) async-start(f16[16,256,128]{2,1,0:T(8,128)(2,1)} %multiply_convert_fusion), calls=%async_computation.2 | async-start | bytes 2097152 | tf_op jit(solution)/shard_map/all_to_all | solution.py:286
  48.4 46.6 %collective-permute-start.2 = (bf16[896,512]{1,0:T(8,128)(2,1)S(1)}, bf16[896,512]{1,0:T(8,128)(2,1)S(1)}, u32[]{:S(2)}, u32[]{:S(2)}) collective-permute-start(bf16[896,512]{1,0:T(8,128)(2,1)S(1)} %copy-done), channel_id=1, source_target_pairs={{0,16},{16,0},{1,17},{17,1},{2,18},{18,2},{3,19},{19,3},{4,20},{20... | collective-permute-start | bytes 2752520 | tf_op jit(solution)/shard_map/ppermute | solution.py:265

commit v8 on v7

--- a/solution.py
+++ b/solution.py
@@ -157,33 +157,39 @@
 
 
 def activate_kernel(sum_ref, out_ref):
-    wide_tiles = out_ref.shape[1] // LANES
+    wide_tiles = out_ref.shape[0] // (PAIR * (MAIN + EXTRA))
+    row = lax.broadcasted_iota(jnp.int32, (8, LANES), 0) // EXTRA
 
     def total(p, rows):
         return sum_ref[p, rows, :] * (1 / SCALE)
 
     for p in range(PAIR):
-        tail_rows = slice(PAIR * MAIN + p * EXTRA, PAIR * MAIN + (p + 1) * EXTRA)
         for j in range(wide_tiles):
             gate = total(p, rows_of(j, MAIN))
             up = total(p, rows_of(wide_tiles + j, MAIN))
-            out_ref[rows_of(p, MAIN), lanes(j)] = (
+            out_ref[rows_of(j * PAIR + p, MAIN), :] = (
                 gate / (1 + jnp.exp(-gate)) * up
             ).astype(jnp.bfloat16)
-        for first in range(0, wide_tiles, 2):
-            start = 2 * wide_tiles * MAIN + 4 * first
+    for first in range(0, wide_tiles, 2):
+        start = 2 * wide_tiles * MAIN + 4 * first
+        tails = []
+        for p in range(PAIR):
             mixed = total(p, slice(start, start + 8))
-            tail = mixed / (1 + jnp.exp(-mixed)) * pltpu.roll(mixed, 2 * EXTRA, 0)
-            tail = tail.astype(jnp.bfloat16)
-            for i in range(min(2, wide_tiles - first)):
-                out_ref[tail_rows, lanes(first + i)] = tail[rows_of(i, EXTRA)]
+            tails.append(mixed / (1 + jnp.exp(-mixed)) * pltpu.roll(mixed, 4, 0))
+        low, high = tails
+        tail = jnp.where(row == 1, pltpu.roll(high, 2, 0), low)
+        tail = jnp.where(row == 2, pltpu.roll(low, 2, 0), tail)
+        tail = jnp.where(row == 3, pltpu.roll(high, 4, 0), tail)
+        count = min(2, wide_tiles - first) * 4
+        start = wide_tiles * PAIR * MAIN + 4 * first
+        out_ref[start : start + count, :] = tail[:count].astype(jnp.bfloat16)
 
 
 def activate(total, hidden_width):
     return pl.pallas_call(
         activate_kernel,
         out_shape=jax.ShapeDtypeStruct(
-            (PAIR * (MAIN + EXTRA), hidden_width), jnp.bfloat16
+            (PAIR * (MAIN + EXTRA) * hidden_width // LANES, LANES), jnp.bfloat16
         ),
         in_specs=[WHOLE],
         out_specs=WHOLE,
@@ -195,14 +201,24 @@
     sources = hidden_ref.shape[0]
     main = sources * MAIN
     first = pair_ref[0] == 0
+    wide_tiles = own.shape[1] // LANES
     for n in range(sources):
-        a, b = hidden_ref[n, :MAIN], hidden_ref[n, MAIN : PAIR * MAIN]
-        own[rows_of(n, MAIN), :] = jnp.where(first, a, b)
-        other[rows_of(n, MAIN), :] = jnp.where(first, b, a)
-        tail = hidden_ref[n, PAIR * MAIN :]
-        at = slice(main + n * 8, main + n * 8 + PAIR * EXTRA)
-        own[at, :] = tail
-        other[at, :] = tail
+        for j in range(wide_tiles):
+            a = hidden_ref[n, rows_of(j * PAIR, MAIN), :]
+            b = hidden_ref[n, rows_of(j * PAIR + 1, MAIN), :]
+            own[rows_of(n, MAIN), lanes(j)] = jnp.where(first, a, b)
+            other[rows_of(n, MAIN), lanes(j)] = jnp.where(first, b, a)
+        for j in range(0, wide_tiles, 2):
+            count = min(2, wide_tiles - j)
+            start = wide_tiles * PAIR * MAIN + 4 * j
+            tail = hidden_ref[n, start : start + 4 * count, :]
+            at = slice(main + n * 8, main + n * 8 + 4 * count)
+            own[at, lanes(j)] = tail
+            other[at, lanes(j)] = tail
+            if count == 2:
+                tail = pltpu.roll(tail.astype(jnp.float32), 4, 0).astype(jnp.bfloat16)
+                own[at, lanes(j + 1)] = tail
+                other[at, lanes(j + 1)] = tail
     tiles = own_ref.shape[1] // LANES
     mine = jnp.dot(own[...], own_ref[...], preferred_element_type=jnp.float32)
     theirs = jnp.dot(other[...], other_ref[...], preferred_element_type=jnp.float32)
@@ -222,7 +238,7 @@
 
 
 def down_product(pair, hidden, weight, other_weight):
-    sources, count, width = hidden.shape
+    sources, width = hidden.shape[0], weight.shape[0]
     rows = (MAIN + EXTRA) * weight.shape[1] // LANES
     held = pltpu.VMEM((sources * (MAIN + 8), width), jnp.bfloat16)
     return pl.pallas_call(

time: 114 us -> 114 us (level)
  no operation moved by 1% of the time
where the time goes in v8:
time: 114 us; the launch traced here: 113 us
  blocking collectives  52.8 us (46%)
  waiting for transfers between devices  28 us (25%)
  starting transfers between devices  24.3 us (21%)
  Pallas kernels  4.6 us (4%)
  local copies, waits for them, and re-layouts  1.66 us (1%)
  other arithmetic  1.44 us (1%)
    all_to_all x1, waiting for transfers between devices, shards(): lax.all_to_all((terms * SCALE).astype(jnp.float16), ('pair', 'z'), 0, 0,...  22.1 us
    all_gather x1, blocking collectives, shards(): gathered = lax.all_gather(hidden, COL, axis=0, tiled=False)  20.7 us
    all_to_all x1, blocking collectives, shards(): return finish(lax.all_to_all(share, ('y', 'far'), 0, 0, tiled=True))  16.4 us
    all_to_all x1, blocking collectives, shards(): lax.all_to_all(spread(activations, n_row // ALONG_X), 'y', 0, 0, tiled=True)  15.7 us
    all_to_all x1, starting transfers between devices, shards(): lax.all_to_all((terms * SCALE).astype(jnp.float16), ('pair', 'z'), 0, 0,...  10.1 us
    ppermute x3, starting transfers between devices, swap(): return lax.ppermute(x, axis, [(0, 1), (1, 0)])  7.59 us
    all_to_all x1, starting transfers between devices, shards(): got = lax.all_to_all(halves, ('far', 'pair', 'core'), 0, 0, tiled=True)  6.55 us
    all_to_all x1, waiting for transfers between devices, shards(): got = lax.all_to_all(halves, ('far', 'pair', 'core'), 0, 0, tiled=True)  5.83 us
  transfers between devices with their start and end apart: 5, of which 2 were waited for; matrix products, arithmetic and copies ran while one was open for 0% of the time, Pallas kernels for 1%

profile of v8, /device:TPU:1, one launch (start us, length us, event | category | flops | bytes accessed | tf_op | source)
XLA Modules:
  0.0 112.9 jit_solution(2770361935322880945)
XLA Ops:
  0.0 0.7 copy-done.1
  0.8 15.7 %all_to_all.20 = bf16[8,72,128]{2,1,0:T(8,128)(2,1)S(1)} all-to-all(bf16[8,72,128]{2,1,0:T(8,128)(2,1)S(1)} %shard_map.46), channel_id=1, replica_groups=mesh['y'=8,'far'=2,'pair'=2,'z'=8,'core'=2] {'y'}, dimensions={0} | all-to-all | bytes 294912 | tf_op jit(solution)/shard_map/all_to_all | solution.py:283
  16.5 0.9 broadcast_in_dim.8
  17.4 6.5 %all-to-all-start.1 = ((bf16[8,4,72,128]{3,2,1,0:T(8,128)(2,1)}), bf16[8,4,72,128]{3,2,1,0:T(8,128)(2,1)S(1)}, u32[]{:S(2)}, u32[]{:S(2)}) async-start(bf16[8,4,72,128]{3,2,1,0:T(8,128)(2,1)} %bitcast.3), calls=%async_computation.1 | async-start | bytes 1179648 | tf_op jit(solution)/shard_map/all_to_all | solution.py:292
  23.9 1.9 %collective-permute-start = (bf16[512,896]{1,0:T(8,128)(2,1)S(1)}, bf16[512,896]{1,0:T(8,128)(2,1)S(1)}, u32[]{:S(2)}, u32[]{:S(2)}) collective-permute-start(bf16[512,896]{1,0:T(8,128)(2,1)S(1)} %copy-done.2), channel_id=1, source_target_pairs={{0,1},{1,0},{2,3},{3,2},{4,5},{5,4},{6,7},{7,6},{8,9},{9,8},{10,11... | collective-permute-start | bytes 2752520 | tf_op jit(solution)/shard_map/ppermute | solution.py:281
  25.9 2.4 %collective-permute-start.1 = (bf16[512,896]{1,0:T(8,128)(2,1)S(1)}, bf16[512,896]{1,0:T(8,128)(2,1)}, u32[]{:S(2)}, u32[]{:S(2)}) collective-permute-start(bf16[512,896]{1,0:T(8,128)(2,1)S(1)} %copy-done.3), channel_id=1, source_target_pairs={{0,1},{1,0},{2,3},{3,2},{4,5},{5,4},{6,7},{7,6},{8,9},{9,8},{10,11... | collective-permute-start | bytes 2752520 | tf_op jit(solution)/shard_map/ppermute | solution.py:281
  28.3 5.8 %all-to-all-done.1.got_ref = bf16[8,4,72,128]{3,2,1,0:T(8,128)(2,1)S(1)} async-done(((bf16[8,4,72,128]{3,2,1,0:T(8,128)(2,1)}), bf16[8,4,72,128]{3,2,1,0:T(8,128)(2,1)S(1)}, u32[]{:S(2)}, u32[]{:S(2)}) %all-to-all-start.1) | async-done | bytes 589856 | tf_op jit(solution)/shard_map/all_to_all | solution.py:292
  34.1 1.0 shard_map.47.refs_0_
  35.2 0.0 collective-permute-done.gate_ref
  35.2 0.0 collective-permute-done.1.up_ref
  35.2 1.8 %shard_map.48 = f32[16,256,128]{2,1,0:T(8,128)S(1)} custom-call(s32[1]{0:T(128)} %bitcast.1.core_ref, bf16[8,4,72,128]{3,2,1,0:T(8,128)(2,1)S(1)} %all-to-all-done.1.got_ref, bf16[512,896]{1,0:T(8,128)(2,1)S(1)} %collective-permute-done.gate_ref, bf16[512,896]{1,0:T(8,128)(2,1)} %collective-permute-done.1.up_ref, f32[16,256,128]{2,1,0:T(8,128)S(1)} %shard_map.47.refs_0_), custom_call_target="tpu_custom_call" | custom-call | flops 5637144576 | bytes 1835008 | tf_op jit(solution)/shard_map/pallas_call | solution.py:146
  37.0 0.0 copy-start
  37.0 1.3 %multiply_convert_fusion = f16[16,256,128]{2,1,0:T(8,128)(2,1)} fusion(f32[16,256,128]{2,1,0:T(8,128)S(1)} %shard_map.48), kind=kLoop, calls=%fused_computation.1 | loop fusion | flops 1048576 | bytes 3145728 | tf_op jit(solution)/shard_map/convert_element_type | solution.py:303
  38.3 10.1 %all-to-all-start.2 = ((f16[16,256,128]{2,1,0:T(8,128)(2,1)}), f16[16,256,128]{2,1,0:T(8,128)(2,1)S(1)}, u32[]{:S(2)}, u32[]{:S(2)}) async-start(f16[16,256,128]{2,1,0:T(8,128)(2,1)} %multiply_convert_fusion), calls=%async_computation.2 | async-start | bytes 2097152 | tf_op jit(solution)/shard_map/all_to_all | solution.py:302
  48.4 0.0 copy-done
  48.4 3.3 %collective-permute-start.2 = (bf16[896,512]{1,0:T(8,128)(2,1)S(1)}, bf16[896,512]{1,0:T(8,128)(2,1)S(1)}, u32[]{:S(2)}, u32[]{:S(2)}) collective-permute-start(bf16[896,512]{1,0:T(8,128)(2,1)S(1)} %copy-done), channel_id=1, source_target_pairs={{0,16},{16,0},{1,17},{17,1},{2,18},{18,2},{3,19},{19,3},{4,20},{20... | collective-permute-start | bytes 2752520 | tf_op jit(solution)/shard_map/ppermute | solution.py:281
  51.7 22.1 %all-to-all-done.2 = f16[16,256,128]{2,1,0:T(8,128)(2,1)S(1)} async-done(((f16[16,256,128]{2,1,0:T(8,128)(2,1)}), f16[16,256,128]{2,1,0:T(8,128)(2,1)S(1)}, u32[]{:S(2)}, u32[]{:S(2)}) %all-to-all-start.2) | async-done | bytes 1048608 | tf_op jit(solution)/shard_map/all_to_all | solution.py:302
  73.9 0.1 convert_reduce_fusion.sum_ref
  74.0 0.1 shard_map.49
  74.1 20.7 %all-gather.1.hidden_ref = bf16[16,252,128]{2,1,0:T(8,128)(2,1)S(1)} all-gather(bf16[1,252,128]{2,1,0:T(8,128)(2,1)S(1)} %bitcast.8), channel_id=2, replica_groups=mesh['y'=8,'far'=2,'pair'=2,'z'=8,'core'=2] {'z','core'}, dimensions={0}, use_global_device_ids=true | all-gather | bytes 1096704 | tf_op jit(solution)/shard_map/all_gather | solution.py:308
  94.8 0.0 collective-permute-done.2.other_ref
  94.8 1.0 shard_map.50
  95.8 16.4 %all_to_all.21.shares_ref = bf16[16,72,128]{2,1,0:T(8,128)(2,1)S(1)} all-to-all(bf16[16,72,128]{2,1,0:T(8,128)(2,1)S(1)} %shard_map.50), channel_id=1, replica_groups=mesh['y'=8,'far'=2,'pair'=2,'z'=8,'core'=2] {'y','far'}, dimensions={0} | all-to-all | bytes 589824 | tf_op jit(solution)/shard_map/all_to_all | solution.py:310
  112.2 0.7 shard_map.51
  (6 shorter events, 0.0 us)
Async XLA Ops:
  0.0 0.7 copy-start.1
  0.7 23.2 %copy-start.2 = (bf16[512,896]{1,0:T(8,128)(2,1)S(1)}, bf16[512,896]{1,0:T(8,128)(2,1)}, u32[]{:S(2)}) copy-start(bf16[512,896]{1,0:T(8,128)(2,1)} %gate_ref) | copy-start | bytes 2752516
  0.7 25.1 %copy-start.3 = (bf16[512,896]{1,0:T(8,128)(2,1)S(1)}, bf16[512,896]{1,0:T(8,128)(2,1)}, u32[]{:S(2)}) copy-start(bf16[512,896]{1,0:T(8,128)(2,1)} %up_ref) | copy-start | bytes 2752516
  17.4 16.7 %all-to-all-start.1 = ((bf16[8,4,72,128]{3,2,1,0:T(8,128)(2,1)}), bf16[8,4,72,128]{3,2,1,0:T(8,128)(2,1)S(1)}, u32[]{:S(2)}, u32[]{:S(2)}) async-start(bf16[8,4,72,128]{3,2,1,0:T(8,128)(2,1)} %bitcast.3), calls=%async_computation.1 | async-start | bytes 1179648 | tf_op jit(solution)/shard_map/all_to_all | solution.py:292
  23.9 11.2 %collective-permute-start = (bf16[512,896]{1,0:T(8,128)(2,1)S(1)}, bf16[512,896]{1,0:T(8,128)(2,1)S(1)}, u32[]{:S(2)}, u32[]{:S(2)}) collective-permute-start(bf16[512,896]{1,0:T(8,128)(2,1)S(1)} %copy-done.2), channel_id=1, source_target_pairs={{0,1},{1,0},{2,3},{3,2},{4,5},{5,4},{6,7},{7,6},{8,9},{9,8},{10,11... | collective-permute-start | bytes 2752520 | tf_op jit(solution)/shard_map/ppermute | solution.py:281
  25.9 9.3 %collective-permute-start.1 = (bf16[512,896]{1,0:T(8,128)(2,1)S(1)}, bf16[512,896]{1,0:T(8,128)(2,1)}, u32[]{:S(2)}, u32[]{:S(2)}) collective-permute-start(bf16[512,896]{1,0:T(8,128)(2,1)S(1)} %copy-done.3), channel_id=1, source_target_pairs={{0,1},{1,0},{2,3},{3,2},{4,5},{5,4},{6,7},{7,6},{8,9},{9,8},{10,11... | collective-permute-start | bytes 2752520 | tf_op jit(solution)/shard_map/ppermute | solution.py:281
  37.0 11.5 %copy-start = (bf16[896,512]{1,0:T(8,128)(2,1)S(1)}, bf16[896,512]{1,0:T(8,128)(2,1)}, u32[]{:S(2)}) copy-start(bf16[896,512]{1,0:T(8,128)(2,1)} %own_ref.1) | copy-start | bytes 2752516
  38.3 35.6 %all-to-all-start.2 = ((f16[16,256,128]{2,1,0:T(8,128)(2,1)}), f16[16,256,128]{2,1,0:T(8,128)(2,1)S(1)}, u32[]{:S(2)}, u32[]{:S(2)}) async-start(f16[16,256,128]{2,1,0:T(8,128)(2,1)} %multiply_convert_fusion), calls=%async_computation.2 | async-start | bytes 2097152 | tf_op jit(solution)/shard_map/all_to_all | solution.py:302
  48.4 46.3 %collective-permute-start.2 = (bf16[896,512]{1,0:T(8,128)(2,1)S(1)}, bf16[896,512]{1,0:T(8,128)(2,1)S(1)}, u32[]{:S(2)}, u32[]{:S(2)}) collective-permute-start(bf16[896,512]{1,0:T(8,128)(2,1)S(1)} %copy-done), channel_id=1, source_target_pairs={{0,16},{16,0},{1,17},{17,1},{2,18},{18,2},{3,19},{19,3},{4,20},{20... | collective-permute-start | bytes 2752520 | tf_op jit(solution)/shard_map/ppermute | solution.py:281

commit v9 on v8

--- a/solution.py
+++ b/solution.py
@@ -124,12 +124,11 @@
         up_ref, ready = up_held, fetch.wait
     else:
         out_ref, held = refs
-    depth = out_ref.shape[0] // PAIR
     side = flip + (1 - 2 * flip) * core_ref[0]
 
     def source_at(n):
-        b = n % depth
-        return got_ref[(b % FAR * PAIR + n // depth) * 2 + side, b // FAR]
+        b = n // PAIR
+        return got_ref[(b % FAR * PAIR + n % PAIR) * 2 + side, b // FAR]
 
     add_product(source_at, ready, gate_ref, up_ref, base_ref, out_ref, held)
 
@@ -300,10 +299,10 @@
     terms = up_product(0, me, got, sources, gate, up)
     terms = up_product(1, me, got, sources, gate_other, up_other, terms)
     arrived = lax.all_to_all(
-        (terms * SCALE).astype(jnp.float16), ("pair", "z"), 0, 0, tiled=True
+        (terms * SCALE).astype(jnp.float16), ("z", "pair"), 0, 0, tiled=True
     )
-    arrived = arrived.reshape(PAIR, depth, *arrived.shape[1:])
-    total = jnp.sum(arrived.astype(jnp.float32), axis=1)
+    arrived = arrived.reshape(depth, PAIR, *arrived.shape[1:])
+    total = jnp.sum(arrived.astype(jnp.float32), axis=0)
     hidden = activate(total, gate_matrix.shape[1])
     gathered = lax.all_gather(hidden, COL, axis=0, tiled=False)
     share = down_product(pair.reshape(1), gathered, down_matrix, down_other)

time: 114 us -> 114 us (level)
  no operation moved by 1% of the time
where the time goes in v9:
time: 114 us
  blocking collectives  53.7 us (47%)
  waiting for transfers between devices  27.7 us (24%)
  starting transfers between devices  24.3 us (21%)
  Pallas kernels  4.62 us (4%)
  local copies, waits for them, and re-layouts  1.66 us (1%)
  other arithmetic  1.46 us (1%)
    all_to_all x1, waiting for transfers between devices, shards(): lax.all_to_all((terms * SCALE).astype(jnp.float16), ('z', 'pair'), 0, 0,...  21.8 us
    all_gather x1, blocking collectives, shards(): gathered = lax.all_gather(hidden, COL, axis=0, tiled=False)  21.7 us
    all_to_all x1, blocking collectives, shards(): return finish(lax.all_to_all(share, ('y', 'far'), 0, 0, tiled=True))  16.4 us
    all_to_all x1, blocking collectives, shards(): lax.all_to_all(spread(activations, n_row // ALONG_X), 'y', 0, 0, tiled=True)  15.7 us
    all_to_all x1, starting transfers between devices, shards(): lax.all_to_all((terms * SCALE).astype(jnp.float16), ('z', 'pair'), 0, 0,...  10.1 us
    ppermute x3, starting transfers between devices, swap(): return lax.ppermute(x, axis, [(0, 1), (1, 0)])  7.59 us
    all_to_all x1, starting transfers between devices, shards(): got = lax.all_to_all(halves, ('far', 'pair', 'core'), 0, 0, tiled=True)  6.55 us
    all_to_all x1, waiting for transfers between devices, shards(): got = lax.all_to_all(halves, ('far', 'pair', 'core'), 0, 0, tiled=True)  5.83 us
  transfers between devices with their start and end apart: 5, of which 2 were waited for; matrix products, arithmetic and copies ran while one was open for 0% of the time, Pallas kernels for 1%

profile of v9, /device:TPU:1, one launch (start us, length us, event | category | flops | bytes accessed | tf_op | source)
XLA Modules:
  0.0 113.5 jit_solution(16366696109257302829)
XLA Ops:
  0.0 0.7 copy-done.1
  0.8 15.7 %all_to_all.20 = bf16[8,72,128]{2,1,0:T(8,128)(2,1)S(1)} all-to-all(bf16[8,72,128]{2,1,0:T(8,128)(2,1)S(1)} %shard_map.46), channel_id=1, replica_groups=mesh['y'=8,'far'=2,'pair'=2,'z'=8,'core'=2] {'y'}, dimensions={0} | all-to-all | bytes 294912 | tf_op jit(solution)/shard_map/all_to_all | solution.py:282
  16.5 0.9 broadcast_in_dim.8
  17.4 6.5 %all-to-all-start.1 = ((bf16[8,4,72,128]{3,2,1,0:T(8,128)(2,1)}), bf16[8,4,72,128]{3,2,1,0:T(8,128)(2,1)S(1)}, u32[]{:S(2)}, u32[]{:S(2)}) async-start(bf16[8,4,72,128]{3,2,1,0:T(8,128)(2,1)} %bitcast.3), calls=%async_computation.1 | async-start | bytes 1179648 | tf_op jit(solution)/shard_map/all_to_all | solution.py:291
  23.9 0.0 copy-done.2
  23.9 1.9 %collective-permute-start = (bf16[512,896]{1,0:T(8,128)(2,1)S(1)}, bf16[512,896]{1,0:T(8,128)(2,1)S(1)}, u32[]{:S(2)}, u32[]{:S(2)}) collective-permute-start(bf16[512,896]{1,0:T(8,128)(2,1)S(1)} %copy-done.2), channel_id=1, source_target_pairs={{0,1},{1,0},{2,3},{3,2},{4,5},{5,4},{6,7},{7,6},{8,9},{9,8},{10,11... | collective-permute-start | bytes 2752520 | tf_op jit(solution)/shard_map/ppermute | solution.py:280
  25.9 2.4 %collective-permute-start.1 = (bf16[512,896]{1,0:T(8,128)(2,1)S(1)}, bf16[512,896]{1,0:T(8,128)(2,1)}, u32[]{:S(2)}, u32[]{:S(2)}) collective-permute-start(bf16[512,896]{1,0:T(8,128)(2,1)S(1)} %copy-done.3), channel_id=1, source_target_pairs={{0,1},{1,0},{2,3},{3,2},{4,5},{5,4},{6,7},{7,6},{8,9},{9,8},{10,11... | collective-permute-start | bytes 2752520 | tf_op jit(solution)/shard_map/ppermute | solution.py:280
  28.3 5.8 %all-to-all-done.1.got_ref = bf16[8,4,72,128]{3,2,1,0:T(8,128)(2,1)S(1)} async-done(((bf16[8,4,72,128]{3,2,1,0:T(8,128)(2,1)}), bf16[8,4,72,128]{3,2,1,0:T(8,128)(2,1)S(1)}, u32[]{:S(2)}, u32[]{:S(2)}) %all-to-all-start.1) | async-done | bytes 589856 | tf_op jit(solution)/shard_map/all_to_all | solution.py:291
  34.1 1.0 shard_map.47.refs_0_
  35.2 0.0 collective-permute-done.gate_ref
  35.2 0.0 collective-permute-done.1.up_ref
  35.2 1.8 %shard_map.48 = f32[16,256,128]{2,1,0:T(8,128)S(1)} custom-call(s32[1]{0:T(128)} %bitcast.1.core_ref, bf16[8,4,72,128]{3,2,1,0:T(8,128)(2,1)S(1)} %all-to-all-done.1.got_ref, bf16[512,896]{1,0:T(8,128)(2,1)S(1)} %collective-permute-done.gate_ref, bf16[512,896]{1,0:T(8,128)(2,1)} %collective-permute-done.1.up_ref, f32[16,256,128]{2,1,0:T(8,128)S(1)} %shard_map.47.refs_0_), custom_call_target="tpu_custom_call" | custom-call | flops 5637144576 | bytes 1835008 | tf_op jit(solution)/shard_map/pallas_call | solution.py:145
  37.0 0.0 copy-start
  37.0 1.3 %multiply_convert_fusion = f16[16,256,128]{2,1,0:T(8,128)(2,1)} fusion(f32[16,256,128]{2,1,0:T(8,128)S(1)} %shard_map.48), kind=kLoop, calls=%fused_computation.1 | loop fusion | flops 1048576 | bytes 3145728 | tf_op jit(solution)/shard_map/convert_element_type | solution.py:302
  38.3 10.1 %all-to-all-start.2 = ((f16[16,256,128]{2,1,0:T(8,128)(2,1)}), f16[16,256,128]{2,1,0:T(8,128)(2,1)S(1)}, u32[]{:S(2)}, u32[]{:S(2)}) async-start(f16[16,256,128]{2,1,0:T(8,128)(2,1)} %multiply_convert_fusion), calls=%async_computation.2 | async-start | bytes 2097152 | tf_op jit(solution)/shard_map/all_to_all | solution.py:301
  48.4 3.3 %collective-permute-start.2 = (bf16[896,512]{1,0:T(8,128)(2,1)S(1)}, bf16[896,512]{1,0:T(8,128)(2,1)S(1)}, u32[]{:S(2)}, u32[]{:S(2)}) collective-permute-start(bf16[896,512]{1,0:T(8,128)(2,1)S(1)} %copy-done), channel_id=1, source_target_pairs={{0,16},{16,0},{1,17},{17,1},{2,18},{18,2},{3,19},{19,3},{4,20},{20... | collective-permute-start | bytes 2752520 | tf_op jit(solution)/shard_map/ppermute | solution.py:280
  51.7 21.8 %all-to-all-done.2 = f16[16,256,128]{2,1,0:T(8,128)(2,1)S(1)} async-done(((f16[16,256,128]{2,1,0:T(8,128)(2,1)}), f16[16,256,128]{2,1,0:T(8,128)(2,1)S(1)}, u32[]{:S(2)}, u32[]{:S(2)}) %all-to-all-start.2) | async-done | bytes 1048608 | tf_op jit(solution)/shard_map/all_to_all | solution.py:301
  73.5 0.2 convert_reduce_fusion.sum_ref
  73.7 0.1 shard_map.49
  73.8 21.7 %all-gather.1.hidden_ref = bf16[16,252,128]{2,1,0:T(8,128)(2,1)S(1)} all-gather(bf16[1,252,128]{2,1,0:T(8,128)(2,1)S(1)} %bitcast.7), channel_id=2, replica_groups=mesh['y'=8,'far'=2,'pair'=2,'z'=8,'core'=2] {'z','core'}, dimensions={0}, use_global_device_ids=true | all-gather | bytes 1096704 | tf_op jit(solution)/shard_map/all_gather | solution.py:307
  95.4 0.0 collective-permute-done.2.other_ref
  95.4 1.1 shard_map.50
  96.5 16.4 %all_to_all.21.shares_ref = bf16[16,72,128]{2,1,0:T(8,128)(2,1)S(1)} all-to-all(bf16[16,72,128]{2,1,0:T(8,128)(2,1)S(1)} %shard_map.50), channel_id=1, replica_groups=mesh['y'=8,'far'=2,'pair'=2,'z'=8,'core'=2] {'y','far'}, dimensions={0} | all-to-all | bytes 589824 | tf_op jit(solution)/shard_map/all_to_all | solution.py:309
  112.9 0.7 shard_map.51
  (6 shorter events, 0.0 us)
Async XLA Ops:
  0.0 0.7 copy-start.1
  0.7 23.2 %copy-start.2 = (bf16[512,896]{1,0:T(8,128)(2,1)S(1)}, bf16[512,896]{1,0:T(8,128)(2,1)}, u32[]{:S(2)}) copy-start(bf16[512,896]{1,0:T(8,128)(2,1)} %gate_ref) | copy-start | bytes 2752516
  0.7 25.1 %copy-start.3 = (bf16[512,896]{1,0:T(8,128)(2,1)S(1)}, bf16[512,896]{1,0:T(8,128)(2,1)}, u32[]{:S(2)}) copy-start(bf16[512,896]{1,0:T(8,128)(2,1)} %up_ref) | copy-start | bytes 2752516
  17.4 16.7 %all-to-all-start.1 = ((bf16[8,4,72,128]{3,2,1,0:T(8,128)(2,1)}), bf16[8,4,72,128]{3,2,1,0:T(8,128)(2,1)S(1)}, u32[]{:S(2)}, u32[]{:S(2)}) async-start(bf16[8,4,72,128]{3,2,1,0:T(8,128)(2,1)} %bitcast.3), calls=%async_computation.1 | async-start | bytes 1179648 | tf_op jit(solution)/shard_map/all_to_all | solution.py:291
  23.9 11.2 %collective-permute-start = (bf16[512,896]{1,0:T(8,128)(2,1)S(1)}, bf16[512,896]{1,0:T(8,128)(2,1)S(1)}, u32[]{:S(2)}, u32[]{:S(2)}) collective-permute-start(bf16[512,896]{1,0:T(8,128)(2,1)S(1)} %copy-done.2), channel_id=1, source_target_pairs={{0,1},{1,0},{2,3},{3,2},{4,5},{5,4},{6,7},{7,6},{8,9},{9,8},{10,11... | collective-permute-start | bytes 2752520 | tf_op jit(solution)/shard_map/ppermute | solution.py:280
  25.9 9.3 %collective-permute-start.1 = (bf16[512,896]{1,0:T(8,128)(2,1)S(1)}, bf16[512,896]{1,0:T(8,128)(2,1)}, u32[]{:S(2)}, u32[]{:S(2)}) collective-permute-start(bf16[512,896]{1,0:T(8,128)(2,1)S(1)} %copy-done.3), channel_id=1, source_target_pairs={{0,1},{1,0},{2,3},{3,2},{4,5},{5,4},{6,7},{7,6},{8,9},{9,8},{10,11... | collective-permute-start | bytes 2752520 | tf_op jit(solution)/shard_map/ppermute | solution.py:280
  37.0 11.5 %copy-start = (bf16[896,512]{1,0:T(8,128)(2,1)S(1)}, bf16[896,512]{1,0:T(8,128)(2,1)}, u32[]{:S(2)}) copy-start(bf16[896,512]{1,0:T(8,128)(2,1)} %own_ref.1) | copy-start | bytes 2752516
  38.3 35.3 %all-to-all-start.2 = ((f16[16,256,128]{2,1,0:T(8,128)(2,1)}), f16[16,256,128]{2,1,0:T(8,128)(2,1)S(1)}, u32[]{:S(2)}, u32[]{:S(2)}) async-start(f16[16,256,128]{2,1,0:T(8,128)(2,1)} %multiply_convert_fusion), calls=%async_computation.2 | async-start | bytes 2097152 | tf_op jit(solution)/shard_map/all_to_all | solution.py:301
  48.4 47.0 %collective-permute-start.2 = (bf16[896,512]{1,0:T(8,128)(2,1)S(1)}, bf16[896,512]{1,0:T(8,128)(2,1)S(1)}, u32[]{:S(2)}, u32[]{:S(2)}) collective-permute-start(bf16[896,512]{1,0:T(8,128)(2,1)S(1)} %copy-done), channel_id=1, source_target_pairs={{0,16},{16,0},{1,17},{17,1},{2,18},{18,2},{3,19},{19,3},{4,20},{20... | collective-permute-start | bytes 2752520 | tf_op jit(solution)/shard_map/ppermute | solution.py:280
